TPU v7x, 32 devices: a whole 2x2x4 slice. The times are simulated.
32 devices in a mesh: wide: 8 (over z, y), narrow: 4 (over x, core).
Axes of the slice: x: 2, y: 2, z: 4, core: 2. Of those that a mesh axis runs over, the one named last changes fastest.
Arguments:
- tiles: float32 [8, 24, 256, 256], P('wide', 'narrow'), may hold values from -12 to 12, as said below
- tile_rows: int32 [8, 24], P('wide', 'narrow'), may hold values from 0 to 31, as said below
- tile_cols: int32 [8, 24], P('wide', 'narrow'), may hold values from 0 to 31, as said below
- tile_counts: int32 [8, 4], P('wide', 'narrow'), may hold values from 0 to 6, as said below
Outputs:
- scaled_tiles: float32 [8, 24, 256, 256], P('wide', 'narrow')
- scaling: float32 [32, 256], P('wide')
Inputs may be any that keep to these rules, and one draw needn't show every extreme that they name: `tile_rows`: A live slot of device (w, n) names a block row in w * 4 to (w + 1) * 4 - 1, and every block row has exactly one live diagonal tile, on the device whose block columns hold it. Unused slots name block row w * 4. `tile_cols`: A live slot of device (w, n) names a block column in n * 8 to (n + 1) * 8 - 1, not below its block row; no tile is stored twice. Unused slots name block column n * 8. `tile_counts`: the device that holds a block row's diagonal tile uses all slots. Diagonal tiles are symmetric with diagonal entries in 0.3 to 1.5.
All inputs are finite; a program needn't handle non-finite values.
Results may differ from a plain program's by a relative error of at most 0.00002.
Values sent between devices are 32-bit elements; how exact they have to be, the bound alone decides.
No kernel may reach another device: no remote copies, remote signals or barrier semaphores. Data moves between devices by JAX's collectives and lax.ppermute only.
A program may use at most 64 MiB of HBM per device.

v0:
```python
import jax
import jax.numpy as jnp
from jax import lax
from jax.sharding import PartitionSpec as P

TILE = 256
ROWB = 4
ITERS = 2


def from_root(block, axis, owner):
    block = jnp.where(lax.axis_index(axis) == owner, block, jnp.zeros_like(block))
    return lax.psum(block, axis)


def on_device(tiles, tile_rows, tile_cols, tile_counts):
    wide_size = lax.axis_size("wide")
    narrow_size = lax.axis_size("narrow")
    column_blocks = ROWB * wide_size // narrow_size
    slot_count = tiles.shape[1]
    wide_index = lax.axis_index("wide")
    narrow_index = lax.axis_index("narrow")
    blocks = tiles[0]
    magnitude = jnp.abs(blocks)
    row_local = tile_rows[0] - wide_index * ROWB
    col_local = tile_cols[0] - narrow_index * column_blocks
    live_slots = jnp.arange(slot_count) < tile_counts[0, 0]
    col_target = jnp.where(live_slots, col_local, 0)
    offset = wide_index * ROWB - narrow_index * column_blocks
    inside = (offset >= 0) & (offset < column_blocks)
    start_block = jnp.clip(offset, 0, column_blocks - ROWB)
    home_index = wide_index * ROWB // column_blocks
    row_scale = jnp.ones((ROWB, TILE), jnp.float32)
    col_scale = jnp.ones((column_blocks, TILE), jnp.float32)
    for iteration in range(ITERS):
        left_scale = row_scale[row_local]
        right_scale = col_scale[col_local]
        scaled = magnitude * left_scale[:, :, None] * right_scale[:, None, :]
        scaled = jnp.where(live_slots[:, None, None], scaled, jnp.float32(0.0))
        row_peak = jnp.max(scaled, axis=2)
        col_peak = jnp.max(scaled, axis=1)
        row_part = jnp.zeros((ROWB, TILE), jnp.float32).at[row_local].max(row_peak)
        row_full = lax.pmax(row_part, "narrow")
        own_rows = jnp.where(inside, row_full, jnp.float32(0.0))
        empty_columns = jnp.zeros((column_blocks, TILE), jnp.float32)
        col_part = empty_columns.at[col_target].max(col_peak)
        window = lax.dynamic_slice_in_dim(col_part, start_block, ROWB, 0)
        col_part = lax.dynamic_update_slice_in_dim(
            col_part, jnp.maximum(window, own_rows), start_block, 0
        )
        col_full = lax.pmax(col_part, "wide")
        row_window = lax.dynamic_slice_in_dim(col_full, start_block, ROWB, 0)
        row_total = from_root(row_window, "narrow", home_index)
        row_scale = row_scale / jnp.sqrt(row_total)
        col_scale = col_scale / jnp.sqrt(col_full)
    left_scale = row_scale[row_local]
    right_scale = col_scale[col_local]
    result = blocks * left_scale[:, :, None] * right_scale[:, None, :]
    result = jnp.where(live_slots[:, None, None], result, jnp.float32(0.0))
    return (result[None], row_scale)


def solution(mesh):
    placed = (
        P("wide", "narrow", None, None),
        P("wide", "narrow"),
        P("wide", "narrow"),
        P("wide", "narrow"),
    )
    return jax.shard_map(
        on_device,
        mesh=mesh,
        in_specs=placed,
        out_specs=(P("wide", "narrow", None, None), P("wide", None)),
        check_vma=False,
    )
```

profile of v0, /device:TPU:0, one launch (start us, length us, event | category | flops | bytes accessed | tf_op | source)
XLA Modules:
  0.0 77.6 jit_solution(8317869756076923600)
XLA Ops:
  0.6 0.0 copy-start
  1.4 0.7 fusion.17
  2.2 0.6 gather_fusion
  2.7 0.6 gather_fusion.1
  3.3 2.0 %fusion.6 = (f32[6,256]{1,0:T(8,128)S(1)}, f32[6,256]{1,0:T(8,128)S(1)}) fusion(f32[1,6,256,256]{3,2,1,0:T(8,128)} %param.4, f32[6,256]{1,0:T(8,128)S(1)} %gather_fusion.1, f32[6,256]{1,0:T(8,128)S(1)} %gather_fusion, pred[6]{0:T(512)(128)(4,1)S(1)} %iota_compare_fusion), kind=kLoop, calls=%fused_computation.19 | loop fusion | flops 2356224 | bytes 1597446 | tf_op jit(solution)/shard_map/reduce_max | solution.py:40
  5.3 0.6 scatter_custom_fusion.1
  5.9 0.6 scatter_custom_fusion
  6.6 8.3 %pmax.28 = f32[4,256]{1,0:T(4,128)S(1)} all-reduce(f32[4,256]{1,0:T(4,128)S(1)} %scatter_custom_fusion.1), channel_id=1, replica_groups=mesh['wide'=8,'narrow'=4] {'narrow'}, use_global_device_ids=true, to_apply=%region_4.5 | all-reduce | flops 1024 | bytes 8192 | tf_op jit(solution)/shard_map/pmax | solution.py:43
  14.9 0.1 dynamic_update_slice.6
  15.1 21.9 %pmax.29 = f32[8,256]{1,0:T(8,128)S(1)} all-reduce(f32[8,256]{1,0:T(8,128)S(1)} %dynamic_update_slice.6), channel_id=1, replica_groups=mesh['wide'=8,'narrow'=4] {'wide'}, use_global_device_ids=true, to_apply=%region_5.6 | all-reduce | flops 2048 | bytes 16384 | tf_op jit(solution)/shard_map/pmax | solution.py:51
  37.0 5.9 %psum.14 = f32[4,256]{1,0:T(4,128)S(1)} all-reduce(f32[4,256]{1,0:T(4,128)S(1)} %dynamic-slice_select_fusion.1), channel_id=1, replica_groups=mesh['wide'=8,'narrow'=4] {'narrow'}, use_global_device_ids=true, to_apply=%region_6.7 | all-reduce | flops 1024 | bytes 8192 | tf_op jit(solution)/shard_map/psum | solution.py:13
  42.9 0.6 gather_fusion.2
  43.5 0.6 gather_fusion.3
  44.1 0.0 copy-done
  44.1 0.7 fusion.4
  44.8 0.6 scatter_custom_fusion.3
  45.4 0.6 scatter_custom_fusion.2
  46.0 5.8 %pmax.30 = f32[4,256]{1,0:T(4,128)S(1)} all-reduce(f32[4,256]{1,0:T(4,128)S(1)} %scatter_custom_fusion.3), channel_id=1, replica_groups=mesh['wide'=8,'narrow'=4] {'narrow'}, use_global_device_ids=true, to_apply=%region_11.12 | all-reduce | flops 1024 | bytes 8192 | tf_op jit(solution)/shard_map/pmax | solution.py:43
  51.8 0.1 dynamic_update_slice.7
  52.0 17.4 %pmax.31 = f32[8,256]{1,0:T(8,128)S(1)} all-reduce(f32[8,256]{1,0:T(8,128)S(1)} %dynamic_update_slice.7), channel_id=1, replica_groups=mesh['wide'=8,'narrow'=4] {'wide'}, use_global_device_ids=true, to_apply=%region_12.13 | all-reduce | flops 2048 | bytes 16384 | tf_op jit(solution)/shard_map/pmax | solution.py:51
  69.4 0.6 gather_fusion.5
  69.9 5.7 %psum.15 = f32[4,256]{1,0:T(4,128)S(1)} all-reduce(f32[4,256]{1,0:T(4,128)S(1)} %dynamic-slice_select_fusion), channel_id=1, replica_groups=mesh['wide'=8,'narrow'=4] {'narrow'}, use_global_device_ids=true, to_apply=%region_13.14 | all-reduce | flops 1024 | bytes 8192 | tf_op jit(solution)/shard_map/psum | solution.py:13
  75.6 0.0 copy-start.1
  75.6 0.6 gather_fusion.4
  76.2 1.4 %multiply_select_fusion = f32[1,6,256,256]{3,2,1,0:T(8,128)} fusion(f32[1,6,256,256]{3,2,1,0:T(8,128)S(1)} %copy-done, f32[6,256]{1,0:T(8,128)S(1)} %gather_fusion.5, f32[6,256]{1,0:T(8,128)S(1)} %gather_fusion.4, pred[6]{0:T(512)(128)(4,1)S(1)} %iota_compare_fusion), kind=kLoop, calls=%fused_computation.16 | loop fusion | flops 1179648 | bytes 3158022 | tf_op jit(solution)/shard_map/jit(_where)/select_n | solution.py:59
  77.6 0.0 copy-done.1
  (13 shorter events, 0.1 us)
Async XLA Ops:
  0.6 43.5 %copy-start = (f32[1,6,256,256]{3,2,1,0:T(8,128)S(1)}, f32[1,6,256,256]{3,2,1,0:T(8,128)}, u32[]{:S(2)}) copy-start(f32[1,6,256,256]{3,2,1,0:T(8,128)} %param.4) | copy-start | bytes 4718596
  75.6 2.0 %copy-start.1 = (f32[4,256]{1,0:T(4,128)}, f32[4,256]{1,0:T(4,128)S(1)}, u32[]{:S(2)}) copy-start(f32[4,256]{1,0:T(4,128)S(1)} %rsqrt_multiply_fusion.1) | copy-start | bytes 12292
where the time goes:
time: 77.9 us; the launch traced here: 77.6 us
  blocking collectives  65 us (83%)
  other arithmetic  7.37 us (9%)
  local copies, waits for them, and re-layouts  3.64 us (5%)
  between operations  1.59 us (2%)
    pmax x2, blocking collectives, on_device(): col_full = lax.pmax(col_part, 'wide')  39.3 us
    pmax x2, blocking collectives, on_device(): row_full = lax.pmax(row_part, 'narrow')  14.1 us
    psum x2, blocking collectives, from_root(): return lax.psum(block, axis)  11.6 us
    reduce_max x2, other arithmetic, on_device(): row_peak = jnp.max(scaled, axis=2)  2.71 us
    gather x3, local copies, waits for them, and re-layouts, on_device(): left_scale = row_scale[row_local]  1.68 us
    gather x3, local copies, waits for them, and re-layouts, on_device(): right_scale = col_scale[col_local]  1.68 us

commit v1 on v0

v1 whole, which is shorter than its diff:
```python
import functools

import jax
import jax.numpy as jnp
from jax import lax
from jax.experimental import pallas as pl
from jax.experimental.pallas import tpu as pltpu
from jax.sharding import PartitionSpec as P

ROWB = 4
ITERS = 2
BOTH = ("wide", "narrow")
SMEM = pl.BlockSpec(memory_space=pltpu.SMEM)
VMEM = pl.BlockSpec(memory_space=pltpu.VMEM)
HBM = pl.BlockSpec(memory_space=pltpu.HBM)


def raise_row(peak_ref, index, row):
    peak_ref[pl.ds(index, 1), :] = jnp.maximum(peak_ref[pl.ds(index, 1), :], row)


def lane_max(block):
    half = block.shape[1] // 2
    folded = jnp.maximum(block[:, :half], block[:, half:])
    return jnp.max(folded.T, axis=0, keepdims=True)


def as_column(row, half):
    return jnp.broadcast_to(row, (half, row.shape[1])).T


def first_kernel(rows_ref, cols_ref, count_ref, tiles_ref, held_ref, peak_ref, sems):
    slots = tiles_ref.shape[1]
    copies = [
        pltpu.make_async_copy(tiles_ref.at[0, s], held_ref.at[s], sems.at[s])
        for s in range(slots)
    ]
    for copy in copies:
        copy.start()
    peak_ref[...] = jnp.zeros_like(peak_ref)
    for s in range(slots):
        copies[s].wait()

        @pl.when(s < count_ref[0, 0])
        def _():
            size = jnp.abs(held_ref[s])
            raise_row(peak_ref, cols_ref[0, s], jnp.max(size, axis=0, keepdims=True))
            raise_row(peak_ref, rows_ref[0, s], lane_max(size))


def next_kernel(rows_ref, cols_ref, count_ref, held_ref, *refs):
    *old_refs, peak_ref, scale_ref = refs
    slots, _, tile = held_ref.shape
    half = tile // 2
    scale = lax.rsqrt(old_refs[0][...])
    for old_ref in old_refs[1:]:
        scale = scale * lax.rsqrt(old_ref[...])
    scale_ref[...] = scale
    peak_ref[...] = jnp.zeros_like(peak_ref)
    for s in range(slots):

        @pl.when(s < count_ref[0, 0])
        def _():
            size = jnp.abs(held_ref[s])
            row, col = rows_ref[0, s], cols_ref[0, s]
            left = scale_ref[pl.ds(row, 1), :]
            right = scale_ref[pl.ds(col, 1), :]
            raise_row(peak_ref, row, lane_max(size * right) * left)
            column = as_column(left, half)
            below = jnp.concatenate(
                [
                    jnp.max(size[:, :half] * column, axis=0, keepdims=True),
                    jnp.max(size[:, half:] * column, axis=0, keepdims=True),
                ],
                axis=1,
            )
            raise_row(peak_ref, col, below * right)


def last_kernel(row_blocks, rows_ref, cols_ref, count_ref, held_ref, *refs):
    *old_refs, out_ref, own_ref, scale_ref, done_ref, sems = refs
    slots, _, tile = held_ref.shape
    half = tile // 2
    scale = lax.rsqrt(old_refs[0][...])
    for old_ref in old_refs[1:]:
        scale = scale * lax.rsqrt(old_ref[...])
    scale_ref[...] = scale
    start = lax.axis_index("wide") * row_blocks
    for k in range(row_blocks):
        own_ref[pl.ds(k, 1), :] = scale_ref[pl.ds(start + k, 1), :]
    copies = []
    for s in range(slots):
        live = s < count_ref[0, 0]

        @pl.when(live)
        def _():
            left = scale_ref[pl.ds(rows_ref[0, s], 1), :]
            right = scale_ref[pl.ds(cols_ref[0, s], 1), :]
            column = as_column(left, half)
            done_ref[s, :, :half] = held_ref[s, :, :half] * column * right[:, :half]
            done_ref[s, :, half:] = held_ref[s, :, half:] * column * right[:, half:]

        @pl.when(jnp.logical_not(live))
        def _():
            done_ref[s] = jnp.zeros((tile, tile), jnp.float32)

        copy = pltpu.make_async_copy(done_ref.at[s], out_ref.at[0, s], sems.at[s])
        copy.start()
        copies.append(copy)
    for copy in copies:
        copy.wait()


def swap(values, wide_size, narrow_size, wide_bit, narrow_bit, odd_only):
    pairs = []
    for w in range(wide_size):
        for n in range(narrow_size):
            here = w * narrow_size + n
            there = (w ^ wide_bit) * narrow_size + (n ^ narrow_bit)
            pairs.append((here, here if odd_only and n % 2 == 0 else there))
    return jnp.maximum(values, lax.ppermute(values, BOTH, pairs))


def max_over_devices(values, wide_size, narrow_size):
    step = functools.partial(swap, wide_size=wide_size, narrow_size=narrow_size)
    values = step(values, wide_bit=0, narrow_bit=1, odd_only=False)
    steps = []
    bit = 1
    while bit < wide_size:
        steps.append((bit, 0))
        bit *= 2
    bit = 2
    while bit < narrow_size:
        steps.insert(len(steps) - 1, (0, bit))
        bit *= 2
    for wide_bit, narrow_bit in steps:
        values = step(values, wide_bit=wide_bit, narrow_bit=narrow_bit, odd_only=True)
    return step(values, wide_bit=0, narrow_bit=1, odd_only=False)


def on_device(wide_size, narrow_size, row_blocks, tiles, tile_rows, tile_cols, tile_counts):
    slots, tile = tiles.shape[1], tiles.shape[2]
    blocks = row_blocks * wide_size
    places = (tile_rows, tile_cols, tile_counts)
    held_shape = jax.ShapeDtypeStruct((slots, tile, tile), jnp.float32)
    peak_shape = jax.ShapeDtypeStruct((blocks, tile), jnp.float32)
    held, part = pl.pallas_call(
        first_kernel,
        out_shape=(held_shape, peak_shape),
        in_specs=[SMEM] * 3 + [HBM],
        out_specs=(VMEM, VMEM),
        scratch_shapes=[pltpu.SemaphoreType.DMA((slots,))],
        name="first_peaks",
    )(*places, tiles)
    peaks = []
    for iteration in range(ITERS):
        if iteration:
            part = pl.pallas_call(
                next_kernel,
                out_shape=peak_shape,
                in_specs=[SMEM] * 3 + [VMEM] * (1 + len(peaks)),
                out_specs=VMEM,
                scratch_shapes=[pltpu.VMEM((blocks, tile), jnp.float32)],
                name="next_peaks",
            )(*places, held, *peaks)
        peaks.append(max_over_devices(part, wide_size, narrow_size))
    return pl.pallas_call(
        functools.partial(last_kernel, row_blocks),
        out_shape=(
            jax.ShapeDtypeStruct(tiles.shape, jnp.float32),
            jax.ShapeDtypeStruct((row_blocks, tile), jnp.float32),
        ),
        in_specs=[SMEM] * 3 + [VMEM] * (1 + len(peaks)),
        out_specs=(HBM, VMEM),
        scratch_shapes=[
            pltpu.VMEM((blocks, tile), jnp.float32),
            pltpu.VMEM((slots, tile, tile), jnp.float32),
            pltpu.SemaphoreType.DMA((slots,)),
        ],
        name="scaled_tiles",
    )(*places, held, *peaks)


def solution(mesh):
    wide_size, narrow_size = mesh.shape["wide"], mesh.shape["narrow"]
    placed = (
        P("wide", "narrow", None, None),
        P("wide", "narrow"),
        P("wide", "narrow"),
        P("wide", "narrow"),
    )
    row_blocks = ROWB
    return jax.shard_map(
        functools.partial(on_device, wide_size, narrow_size, row_blocks),
        mesh=mesh,
        in_specs=placed,
        out_specs=(P("wide", "narrow", None, None), P("wide", None)),
        check_vma=False,
    )
```

time: 77.9 us -> 60 us (0.77)
  blocking collectives: 65 us -> 0 us
  starting transfers between devices: 0 us -> 40.7 us
  Pallas kernels: 0 us -> 10.1 us
  other arithmetic: 7.37 us -> 2.82 us
  waiting for transfers between devices: 0 us -> 4.44 us
  local copies, waits for them, and re-layouts: 3.64 us -> 0 us
    pmax x4 -> x0, blocking collectives: 53.4 us -> none  [the longest x2 39.3 us: on_device(): col_full = lax.pmax(col_part, 'wide')]
    ppermute x0 -> x12, starting transfers between devices: none -> 40.7 us  [swap(): return jnp.maximum(values, lax.ppermute(values, BOTH, pairs))]
    psum x2 -> x0, blocking collectives: 11.6 us -> none  [from_root(): return lax.psum(block, axis)]
    pallas_call x0 -> x3, Pallas kernels: none -> 10.1 us  [the longest x1 3.56 us: on_device(): pl.pallas_call(first_kernel, out_shape=(held_shape, peak_shape), in_specs...]
    ppermute x0 -> x12, waiting for transfers between devices: none -> 4.44 us  [swap(): return jnp.maximum(values, lax.ppermute(values, BOTH, pairs))]
    gather x6 -> x0, local copies, waits for them, and re-layouts: 3.36 us -> none  [the longest x3 1.68 us: on_device(): left_scale = row_scale[row_local]]
    max x2 -> x12, other arithmetic: 0.02 us -> 2.82 us  [swap(): return jnp.maximum(values, lax.ppermute(values, BOTH, pairs))]
    reduce_max x2 -> x0, other arithmetic: 2.71 us -> none  [on_device(): row_peak = jnp.max(scaled, axis=2)]
  transfers between devices with their start and end apart: 0 -> 12, of which waited for: 0 -> 4; matrix products, arithmetic and copies ran while one was open for 0% -> 0% of each run, Pallas kernels for 0% -> 0%
where the time goes in v1:
time: 60 us; the launch traced here: 59.5 us
  starting transfers between devices  40.7 us (68%)
  Pallas kernels  10.1 us (17%)
  waiting for transfers between devices  4.44 us (7%)
  other arithmetic  2.82 us (5%)
  between operations  1.48 us (2%)
    ppermute x12, starting transfers between devices, swap(): return jnp.maximum(values, lax.ppermute(values, BOTH, pairs))  40.7 us
    ppermute x12, waiting for transfers between devices, swap(): return jnp.maximum(values, lax.ppermute(values, BOTH, pairs))  4.44 us
    pallas_call x1, Pallas kernels, on_device(): pl.pallas_call(first_kernel, out_shape=(held_shape, peak_shape), in_specs...  3.56 us
    pallas_call x1, Pallas kernels, on_device(): pl.pallas_call(functools.partial(last_kernel, row_blocks), out_shape=(jax...  3.47 us
    pallas_call x1, Pallas kernels, on_device(): pl.pallas_call(next_kernel, out_shape=peak_shape, in_specs=[SMEM] * 3 + [...  3.02 us
    max x12, other arithmetic, swap(): return jnp.maximum(values, lax.ppermute(values, BOTH, pairs))  2.82 us
  transfers between devices with their start and end apart: 12, of which 4 were waited for; matrix products, arithmetic and copies ran while one was open for 0% of the time, Pallas kernels for 0%

profile of v1, /device:TPU:0, one launch (start us, length us, event | category | flops | bytes accessed | tf_op | source)
XLA Modules:
  0.0 59.5 jit_solution(16757168081691154525)
XLA Ops:
  1.3 3.6 %first_peaks.1 = (f32[6,256,256]{2,1,0:T(8,128)}, f32[32,256]{1,0:T(8,128)}) custom-call(s32[1,6]{1,0:T(1,128)} %rows_ref.5, s32[1,6]{1,0:T(1,128)} %cols_ref.5, s32[1,1]{1,0:T(1,128)S(6)} %copy.6.count_ref, f32[1,6,256,256]{3,2,1,0:T(8,128)} %tiles_ref.1), custom_call_target="tpu_custom_call" | custom-call | tf_op jit(solution)/shard_map/first_peaks/pallas_call | solution.py:147
  4.8 0.2 collective-permute-start
  5.0 1.3 %collective-permute-done = f32[32,256]{1,0:T(8,128)S(1)} collective-permute-done((f32[32,256]{1,0:T(8,128)}, f32[32,256]{1,0:T(8,128)S(1)}, u32[]{:S(2)}, u32[]{:S(2)}) %collective-permute-start) | collective-permute-done | bytes 32800 | tf_op jit(solution)/shard_map/ppermute | solution.py:121
  6.3 0.8 %max.36 = f32[32,256]{1,0:T(8,128)S(1)} maximum(f32[32,256]{1,0:T(8,128)} %get-tuple-element.5, f32[32,256]{1,0:T(8,128)S(1)} %collective-permute-done) | non-fusion elementwise | flops 8192 | bytes 98304 | tf_op jit(solution)/shard_map/max | solution.py:121
  7.1 0.7 %collective-permute-start.1 = (f32[32,256]{1,0:T(8,128)S(1)}, f32[32,256]{1,0:T(8,128)S(1)}, u32[]{:S(2)}, u32[]{:S(2)}) collective-permute-start(f32[32,256]{1,0:T(8,128)S(1)} %max.36), channel_id=1, source_target_pairs={{0,0},{1,5},{2,2},{3,7},{4,4},{5,1},{6,6},{7,3},{8,8},{9,13},{10,1... | collective-permute-start | bytes 98312 | tf_op jit(solution)/shard_map/ppermute | solution.py:121
  7.7 0.0 collective-permute-done.1
  7.8 0.7 %collective-permute-start.2 = (f32[32,256]{1,0:T(8,128)S(1)}, f32[32,256]{1,0:T(8,128)S(1)}, u32[]{:S(2)}, u32[]{:S(2)}) collective-permute-start(f32[32,256]{1,0:T(8,128)S(1)} %max.37), channel_id=1, source_target_pairs={{0,0},{1,9},{2,2},{3,11},{4,4},{5,13},{6,6},{7,15},{8,8},{9,1},{10... | collective-permute-start | bytes 98312 | tf_op jit(solution)/shard_map/ppermute | solution.py:121
  8.4 0.0 collective-permute-done.2
  8.5 0.7 %collective-permute-start.3 = (f32[32,256]{1,0:T(8,128)S(1)}, f32[32,256]{1,0:T(8,128)S(1)}, u32[]{:S(2)}, u32[]{:S(2)}) collective-permute-start(f32[32,256]{1,0:T(8,128)S(1)} %max.38), channel_id=1, source_target_pairs={{0,0},{1,3},{2,2},{3,1},{4,4},{5,7},{6,6},{7,5},{8,8},{9,11},{10,1... | collective-permute-start | bytes 98312 | tf_op jit(solution)/shard_map/ppermute | solution.py:121
  9.1 0.0 collective-permute-done.3
  9.2 0.7 %collective-permute-start.4 = (f32[32,256]{1,0:T(8,128)S(1)}, f32[32,256]{1,0:T(8,128)S(1)}, u32[]{:S(2)}, u32[]{:S(2)}) collective-permute-start(f32[32,256]{1,0:T(8,128)S(1)} %max.39), channel_id=1, source_target_pairs={{0,0},{1,17},{2,2},{3,19},{4,4},{5,21},{6,6},{7,23},{8,8},{9,25},{... | collective-permute-start | bytes 98312 | tf_op jit(solution)/shard_map/ppermute | solution.py:121
  9.8 0.0 collective-permute-done.4
  9.9 18.1 %collective-permute-start.5 = (f32[32,256]{1,0:T(8,128)S(1)}, f32[32,256]{1,0:T(8,128)S(1)}, u32[]{:S(2)}, u32[]{:S(2)}) collective-permute-start(f32[32,256]{1,0:T(8,128)S(1)} %max.40), channel_id=1, source_target_pairs={{0,1},{1,0},{2,3},{3,2},{4,5},{5,4},{6,7},{7,6},{8,9},{9,8},{10,11... | collective-permute-start | bytes 98312 | tf_op jit(solution)/shard_map/ppermute | solution.py:121
  28.0 0.9 %collective-permute-done.5 = f32[32,256]{1,0:T(8,128)S(1)} collective-permute-done((f32[32,256]{1,0:T(8,128)S(1)}, f32[32,256]{1,0:T(8,128)S(1)}, u32[]{:S(2)}, u32[]{:S(2)}) %collective-permute-start.5) | collective-permute-done | bytes 32800 | tf_op jit(solution)/shard_map/ppermute | solution.py:121
  28.9 0.6 %max.41.refs_0_ = f32[32,256]{1,0:T(8,128)} maximum(f32[32,256]{1,0:T(8,128)S(1)} %max.40, f32[32,256]{1,0:T(8,128)S(1)} %collective-permute-done.5) | non-fusion elementwise | flops 8192 | bytes 98304 | tf_op jit(solution)/shard_map/max | solution.py:121
  29.5 3.0 %next_peaks.1 = f32[32,256]{1,0:T(8,128)} custom-call(s32[1,6]{1,0:T(1,128)} %rows_ref.5, s32[1,6]{1,0:T(1,128)} %cols_ref.5, s32[1,1]{1,0:T(1,128)S(6)} %copy.6.count_ref, f32[6,256,256]{2,1,0:T(8,128)} %get-tuple-element.4.held_ref, f32[32,256]{1,0:T(8,128)} %max.41.refs_0_), custom_call_target="tpu_custom_call" | custom-call | tf_op jit(solution)/shard_map/next_peaks/pallas_call | solution.py:158
  32.5 0.0 collective-permute-start.6
  32.5 1.4 %collective-permute-done.6 = f32[32,256]{1,0:T(8,128)S(1)} collective-permute-done((f32[32,256]{1,0:T(8,128)}, f32[32,256]{1,0:T(8,128)S(1)}, u32[]{:S(2)}, u32[]{:S(2)}) %collective-permute-start.6) | collective-permute-done | bytes 32800 | tf_op jit(solution)/shard_map/ppermute | solution.py:121
  33.9 0.8 %max.42 = f32[32,256]{1,0:T(8,128)S(1)} maximum(f32[32,256]{1,0:T(8,128)} %next_peaks.1, f32[32,256]{1,0:T(8,128)S(1)} %collective-permute-done.6) | non-fusion elementwise | flops 8192 | bytes 98304 | tf_op jit(solution)/shard_map/max | solution.py:121
  34.7 0.7 %collective-permute-start.7 = (f32[32,256]{1,0:T(8,128)S(1)}, f32[32,256]{1,0:T(8,128)S(1)}, u32[]{:S(2)}, u32[]{:S(2)}) collective-permute-start(f32[32,256]{1,0:T(8,128)S(1)} %max.42), channel_id=1, source_target_pairs={{0,0},{1,5},{2,2},{3,7},{4,4},{5,1},{6,6},{7,3},{8,8},{9,13},{10,1... | collective-permute-start | bytes 98312 | tf_op jit(solution)/shard_map/ppermute | solution.py:121
  35.3 0.0 collective-permute-done.7
  35.4 0.7 %collective-permute-start.8 = (f32[32,256]{1,0:T(8,128)S(1)}, f32[32,256]{1,0:T(8,128)S(1)}, u32[]{:S(2)}, u32[]{:S(2)}) collective-permute-start(f32[32,256]{1,0:T(8,128)S(1)} %max.43), channel_id=1, source_target_pairs={{0,0},{1,9},{2,2},{3,11},{4,4},{5,13},{6,6},{7,15},{8,8},{9,1},{10... | collective-permute-start | bytes 98312 | tf_op jit(solution)/shard_map/ppermute | solution.py:121
  36.0 0.0 collective-permute-done.8
  36.1 0.7 %collective-permute-start.9 = (f32[32,256]{1,0:T(8,128)S(1)}, f32[32,256]{1,0:T(8,128)S(1)}, u32[]{:S(2)}, u32[]{:S(2)}) collective-permute-start(f32[32,256]{1,0:T(8,128)S(1)} %max.44), channel_id=1, source_target_pairs={{0,0},{1,3},{2,2},{3,1},{4,4},{5,7},{6,6},{7,5},{8,8},{9,11},{10,1... | collective-permute-start | bytes 98312 | tf_op jit(solution)/shard_map/ppermute | solution.py:121
  36.7 0.0 collective-permute-done.9
  36.8 0.7 %collective-permute-start.10 = (f32[32,256]{1,0:T(8,128)S(1)}, f32[32,256]{1,0:T(8,128)S(1)}, u32[]{:S(2)}, u32[]{:S(2)}) collective-permute-start(f32[32,256]{1,0:T(8,128)S(1)} %max.45), channel_id=1, source_target_pairs={{0,0},{1,17},{2,2},{3,19},{4,4},{5,21},{6,6},{7,23},{8,8},{9,25},{... | collective-permute-start | bytes 98312 | tf_op jit(solution)/shard_map/ppermute | solution.py:121
  37.4 0.0 collective-permute-done.10
  37.5 17.1 %collective-permute-start.11 = (f32[32,256]{1,0:T(8,128)S(1)}, f32[32,256]{1,0:T(8,128)S(1)}, u32[]{:S(2)}, u32[]{:S(2)}) collective-permute-start(f32[32,256]{1,0:T(8,128)S(1)} %max.46), channel_id=1, source_target_pairs={{0,1},{1,0},{2,3},{3,2},{4,5},{5,4},{6,7},{7,6},{8,9},{9,8},{10,11... | collective-permute-start | bytes 98312 | tf_op jit(solution)/shard_map/ppermute | solution.py:121
  54.6 0.9 %collective-permute-done.11 = f32[32,256]{1,0:T(8,128)S(1)} collective-permute-done((f32[32,256]{1,0:T(8,128)S(1)}, f32[32,256]{1,0:T(8,128)S(1)}, u32[]{:S(2)}, u32[]{:S(2)}) %collective-permute-start.11) | collective-permute-done | bytes 32800 | tf_op jit(solution)/shard_map/ppermute | solution.py:121
  55.4 0.6 %max.47.refs_1_ = f32[32,256]{1,0:T(8,128)} maximum(f32[32,256]{1,0:T(8,128)S(1)} %max.46, f32[32,256]{1,0:T(8,128)S(1)} %collective-permute-done.11) | non-fusion elementwise | flops 8192 | bytes 98304 | tf_op jit(solution)/shard_map/max | solution.py:121
  56.1 3.5 %scaled_tiles.1 = (f32[1,6,256,256]{3,2,1,0:T(8,128)}, f32[4,256]{1,0:T(4,128)}) custom-call(s32[1,6]{1,0:T(1,128)} %rows_ref.5, s32[1,6]{1,0:T(1,128)} %cols_ref.5, s32[1,1]{1,0:T(1,128)S(6)} %copy.6.count_ref, f32[6,256,256]{2,1,0:T(8,128)} %get-tuple-element.4.held_ref, f32[32,256]{1,0:T(8,128)} %max.41.refs_0_, f32[32,256]{1,0:T(8,128)} %max.47.refs_1_), custom_call_target="tpu_custom_call" | custom-call | tf_op jit(solution)/shard_map/scaled_tiles/pallas_call | solution.py:167
  (8 shorter events, 0.1 us)
Async XLA Ops:
  4.8 1.5 %collective-permute-start = (f32[32,256]{1,0:T(8,128)}, f32[32,256]{1,0:T(8,128)S(1)}, u32[]{:S(2)}, u32[]{:S(2)}) collective-permute-start(f32[32,256]{1,0:T(8,128)} %get-tuple-element.5), channel_id=1, source_target_pairs={{0,1},{1,0},{2,3},{3,2},{4,5},{5,4},{6,7},{7,6},{8,9},{9,8},{10,11... | collective-permute-start | bytes 98312 | tf_op jit(solution)/shard_map/ppermute | solution.py:121
  7.1 0.7 %collective-permute-start.1 = (f32[32,256]{1,0:T(8,128)S(1)}, f32[32,256]{1,0:T(8,128)S(1)}, u32[]{:S(2)}, u32[]{:S(2)}) collective-permute-start(f32[32,256]{1,0:T(8,128)S(1)} %max.36), channel_id=1, source_target_pairs={{0,0},{1,5},{2,2},{3,7},{4,4},{5,1},{6,6},{7,3},{8,8},{9,13},{10,1... | collective-permute-start | bytes 98312 | tf_op jit(solution)/shard_map/ppermute | solution.py:121
  7.8 0.7 %collective-permute-start.2 = (f32[32,256]{1,0:T(8,128)S(1)}, f32[32,256]{1,0:T(8,128)S(1)}, u32[]{:S(2)}, u32[]{:S(2)}) collective-permute-start(f32[32,256]{1,0:T(8,128)S(1)} %max.37), channel_id=1, source_target_pairs={{0,0},{1,9},{2,2},{3,11},{4,4},{5,13},{6,6},{7,15},{8,8},{9,1},{10... | collective-permute-start | bytes 98312 | tf_op jit(solution)/shard_map/ppermute | solution.py:121
  8.5 0.7 %collective-permute-start.3 = (f32[32,256]{1,0:T(8,128)S(1)}, f32[32,256]{1,0:T(8,128)S(1)}, u32[]{:S(2)}, u32[]{:S(2)}) collective-permute-start(f32[32,256]{1,0:T(8,128)S(1)} %max.38), channel_id=1, source_target_pairs={{0,0},{1,3},{2,2},{3,1},{4,4},{5,7},{6,6},{7,5},{8,8},{9,11},{10,1... | collective-permute-start | bytes 98312 | tf_op jit(solution)/shard_map/ppermute | solution.py:121
  9.2 0.7 %collective-permute-start.4 = (f32[32,256]{1,0:T(8,128)S(1)}, f32[32,256]{1,0:T(8,128)S(1)}, u32[]{:S(2)}, u32[]{:S(2)}) collective-permute-start(f32[32,256]{1,0:T(8,128)S(1)} %max.39), channel_id=1, source_target_pairs={{0,0},{1,17},{2,2},{3,19},{4,4},{5,21},{6,6},{7,23},{8,8},{9,25},{... | collective-permute-start | bytes 98312 | tf_op jit(solution)/shard_map/ppermute | solution.py:121
  9.9 19.0 %collective-permute-start.5 = (f32[32,256]{1,0:T(8,128)S(1)}, f32[32,256]{1,0:T(8,128)S(1)}, u32[]{:S(2)}, u32[]{:S(2)}) collective-permute-start(f32[32,256]{1,0:T(8,128)S(1)} %max.40), channel_id=1, source_target_pairs={{0,1},{1,0},{2,3},{3,2},{4,5},{5,4},{6,7},{7,6},{8,9},{9,8},{10,11... | collective-permute-start | bytes 98312 | tf_op jit(solution)/shard_map/ppermute | solution.py:121
  32.5 1.4 %collective-permute-start.6 = (f32[32,256]{1,0:T(8,128)}, f32[32,256]{1,0:T(8,128)S(1)}, u32[]{:S(2)}, u32[]{:S(2)}) collective-permute-start(f32[32,256]{1,0:T(8,128)} %next_peaks.1), channel_id=1, source_target_pairs={{0,1},{1,0},{2,3},{3,2},{4,5},{5,4},{6,7},{7,6},{8,9},{9,8},{10,11... | collective-permute-start | bytes 98312 | tf_op jit(solution)/shard_map/ppermute | solution.py:121
  34.7 0.7 %collective-permute-start.7 = (f32[32,256]{1,0:T(8,128)S(1)}, f32[32,256]{1,0:T(8,128)S(1)}, u32[]{:S(2)}, u32[]{:S(2)}) collective-permute-start(f32[32,256]{1,0:T(8,128)S(1)} %max.42), channel_id=1, source_target_pairs={{0,0},{1,5},{2,2},{3,7},{4,4},{5,1},{6,6},{7,3},{8,8},{9,13},{10,1... | collective-permute-start | bytes 98312 | tf_op jit(solution)/shard_map/ppermute | solution.py:121
  35.4 0.7 %collective-permute-start.8 = (f32[32,256]{1,0:T(8,128)S(1)}, f32[32,256]{1,0:T(8,128)S(1)}, u32[]{:S(2)}, u32[]{:S(2)}) collective-permute-start(f32[32,256]{1,0:T(8,128)S(1)} %max.43), channel_id=1, source_target_pairs={{0,0},{1,9},{2,2},{3,11},{4,4},{5,13},{6,6},{7,15},{8,8},{9,1},{10... | collective-permute-start | bytes 98312 | tf_op jit(solution)/shard_map/ppermute | solution.py:121
  36.1 0.7 %collective-permute-start.9 = (f32[32,256]{1,0:T(8,128)S(1)}, f32[32,256]{1,0:T(8,128)S(1)}, u32[]{:S(2)}, u32[]{:S(2)}) collective-permute-start(f32[32,256]{1,0:T(8,128)S(1)} %max.44), channel_id=1, source_target_pairs={{0,0},{1,3},{2,2},{3,1},{4,4},{5,7},{6,6},{7,5},{8,8},{9,11},{10,1... | collective-permute-start | bytes 98312 | tf_op jit(solution)/shard_map/ppermute | solution.py:121
  36.8 0.7 %collective-permute-start.10 = (f32[32,256]{1,0:T(8,128)S(1)}, f32[32,256]{1,0:T(8,128)S(1)}, u32[]{:S(2)}, u32[]{:S(2)}) collective-permute-start(f32[32,256]{1,0:T(8,128)S(1)} %max.45), channel_id=1, source_target_pairs={{0,0},{1,17},{2,2},{3,19},{4,4},{5,21},{6,6},{7,23},{8,8},{9,25},{... | collective-permute-start | bytes 98312 | tf_op jit(solution)/shard_map/ppermute | solution.py:121
  37.5 18.0 %collective-permute-start.11 = (f32[32,256]{1,0:T(8,128)S(1)}, f32[32,256]{1,0:T(8,128)S(1)}, u32[]{:S(2)}, u32[]{:S(2)}) collective-permute-start(f32[32,256]{1,0:T(8,128)S(1)} %max.46), channel_id=1, source_target_pairs={{0,1},{1,0},{2,3},{3,2},{4,5},{5,4},{6,7},{7,6},{8,9},{9,8},{10,11... | collective-permute-start | bytes 98312 | tf_op jit(solution)/shard_map/ppermute | solution.py:121

commit v2 on v1

--- a/solution.py
+++ b/solution.py
@@ -9,6 +9,7 @@
 
 ROWB = 4
 ITERS = 2
+PARAMS = pltpu.CompilerParams(vmem_limit_bytes=16 << 20)
 BOTH = ("wide", "narrow")
 SMEM = pl.BlockSpec(memory_space=pltpu.SMEM)
 VMEM = pl.BlockSpec(memory_space=pltpu.VMEM)
@@ -111,31 +112,29 @@
         copy.wait()
 
 
-def swap(values, wide_size, narrow_size, wide_bit, narrow_bit, odd_only):
+def swap(values, wide_size, narrow_size, wide_bit, narrow_bit):
     pairs = []
     for w in range(wide_size):
         for n in range(narrow_size):
-            here = w * narrow_size + n
             there = (w ^ wide_bit) * narrow_size + (n ^ narrow_bit)
-            pairs.append((here, here if odd_only and n % 2 == 0 else there))
+            pairs.append((w * narrow_size + n, there))
     return jnp.maximum(values, lax.ppermute(values, BOTH, pairs))
 
 
 def max_over_devices(values, wide_size, narrow_size):
-    step = functools.partial(swap, wide_size=wide_size, narrow_size=narrow_size)
-    values = step(values, wide_bit=0, narrow_bit=1, odd_only=False)
+    values = swap(values, wide_size, narrow_size, 0, 1)
     steps = []
     bit = 1
     while bit < wide_size:
-        steps.append((bit, 0))
+        steps.append((bit, 1))
         bit *= 2
     bit = 2
     while bit < narrow_size:
-        steps.insert(len(steps) - 1, (0, bit))
+        steps.insert(len(steps) - 1, (0, bit + 1))
         bit *= 2
     for wide_bit, narrow_bit in steps:
-        values = step(values, wide_bit=wide_bit, narrow_bit=narrow_bit, odd_only=True)
-    return step(values, wide_bit=0, narrow_bit=1, odd_only=False)
+        values = swap(values, wide_size, narrow_size, wide_bit, narrow_bit)
+    return values
 
 
 def on_device(wide_size, narrow_size, row_blocks, tiles, tile_rows, tile_cols, tile_counts):
@@ -150,6 +149,7 @@
         in_specs=[SMEM] * 3 + [HBM],
         out_specs=(VMEM, VMEM),
         scratch_shapes=[pltpu.SemaphoreType.DMA((slots,))],
+        compiler_params=PARAMS,
         name="first_peaks",
     )(*places, tiles)
     peaks = []
@@ -161,6 +161,7 @@
                 in_specs=[SMEM] * 3 + [VMEM] * (1 + len(peaks)),
                 out_specs=VMEM,
                 scratch_shapes=[pltpu.VMEM((blocks, tile), jnp.float32)],
+                compiler_params=PARAMS,
                 name="next_peaks",
             )(*places, held, *peaks)
         peaks.append(max_over_devices(part, wide_size, narrow_size))
@@ -177,6 +178,7 @@
             pltpu.VMEM((slots, tile, tile), jnp.float32),
             pltpu.SemaphoreType.DMA((slots,)),
         ],
+        compiler_params=PARAMS,
         name="scaled_tiles",
     )(*places, held, *peaks)
 

time: 60 us -> 42.4 us (0.71)
  starting transfers between devices: 40.7 us -> 14.5 us
  waiting for transfers between devices: 4.44 us -> 18.1 us
  Pallas kernels: 10.1 us -> 5.53 us
  other arithmetic: 2.82 us -> 0.05 us
  local copies, waits for them, and re-layouts: 0 us -> 2.71 us
    ppermute x12 -> x10, starting transfers between devices: 40.7 us -> 14.5 us  [swap(): return jnp.maximum(values, lax.ppermute(values, BOTH, pairs))]
    ppermute x12 -> x10, waiting for transfers between devices: 4.44 us -> 18.1 us  [swap(): return jnp.maximum(values, lax.ppermute(values, BOTH, pairs))]
    max x12 -> x10, other arithmetic: 2.82 us -> 0.05 us  [swap(): return jnp.maximum(values, lax.ppermute(values, BOTH, pairs))]
    unnamed x0 -> x6, local copies, waits for them, and re-layouts: none -> 2.71 us
    pallas_call x1, Pallas kernels: 3.56 us -> 1.42 us  [on_device(): pl.pallas_call(first_kernel, out_shape=(held_shape, peak_shape), in_specs...]
    pallas_call x1, Pallas kernels: 3.02 us -> 1.52 us  [on_device(): pl.pallas_call(next_kernel, out_shape=peak_shape, in_specs=[SMEM] * 3 + [...]
    pallas_call x1, Pallas kernels: 3.47 us -> 2.58 us  [on_device(): pl.pallas_call(functools.partial(last_kernel, row_blocks), out_shape=(jax...]
  transfers between devices with their start and end apart: 12 -> 10, of which waited for: 4 -> 10; matrix products, arithmetic and copies ran while one was open for 0% -> 0% of each run, Pallas kernels for 0% -> 0%
where the time goes in v2:
time: 42.4 us; the launch traced here: 42.2 us
  waiting for transfers between devices  18.1 us (43%)
  starting transfers between devices  14.5 us (34%)
  Pallas kernels  5.53 us (13%)
  local copies, waits for them, and re-layouts  2.71 us (6%)
  between operations  1.33 us (3%)
    ppermute x10, waiting for transfers between devices, swap(): return jnp.maximum(values, lax.ppermute(values, BOTH, pairs))  18.1 us
    ppermute x10, starting transfers between devices, swap(): return jnp.maximum(values, lax.ppermute(values, BOTH, pairs))  14.5 us
    unnamed x6, local copies, waits for them, and re-layouts  2.71 us
    pallas_call x1, Pallas kernels, on_device(): pl.pallas_call(functools.partial(last_kernel, row_blocks), out_shape=(jax...  2.58 us
    pallas_call x1, Pallas kernels, on_device(): pl.pallas_call(next_kernel, out_shape=peak_shape, in_specs=[SMEM] * 3 + [...  1.52 us
    pallas_call x1, Pallas kernels, on_device(): pl.pallas_call(first_kernel, out_shape=(held_shape, peak_shape), in_specs...  1.42 us
  transfers between devices with their start and end apart: 10, of which 10 were waited for; matrix products, arithmetic and copies ran while one was open for 0% of the time, Pallas kernels for 0%

profile of v2, /device:TPU:0, one launch (start us, length us, event | category | flops | bytes accessed | tf_op | source)
XLA Modules:
  0.0 42.2 jit_solution(4260253090849311824)
XLA Ops:
  1.3 0.0 copy-start
  1.3 1.4 %copy-done = f32[1,6,256,256]{3,2,1,0:T(8,128)S(1)} copy-done((f32[1,6,256,256]{3,2,1,0:T(8,128)S(1)}, f32[1,6,256,256]{3,2,1,0:T(8,128)}, u32[]{:S(2)}) %copy-start) | copy-done | bytes 1572888
  2.7 0.0 copy-start.1
  2.7 0.7 %copy-done.1 = s32[1,6]{1,0:T(1,128)S(1)} copy-done((s32[1,6]{1,0:T(1,128)S(1)}, s32[1,6]{1,0:T(1,128)}, u32[]{:S(2)}) %copy-start.1) | copy-done | bytes 48
  3.3 0.0 copy-start.2
  3.3 0.7 %copy-done.2 = s32[1,6]{1,0:T(1,128)S(1)} copy-done((s32[1,6]{1,0:T(1,128)S(1)}, s32[1,6]{1,0:T(1,128)}, u32[]{:S(2)}) %copy-start.2) | copy-done | bytes 48
  4.0 1.4 %first_peaks.1 = (f32[6,256,256]{2,1,0:T(8,128)S(1)}, f32[32,256]{1,0:T(8,128)S(1)}) custom-call(s32[1,6]{1,0:T(1,128)S(1)} %copy-done.1, s32[1,6]{1,0:T(1,128)S(1)} %copy-done.2, s32[1,1]{1,0:T(1,128)S(6)} %copy.6.count_ref, f32[1,6,256,256]{3,2,1,0:T(8,128)S(1)} %copy-done), custom_call_target="tpu_custom_call" | custom-call | tf_op jit(solution)/shard_map/first_peaks/pallas_call | solution.py:146
  5.4 0.1 collective-permute-start
  5.5 1.2 %collective-permute-done = f32[32,256]{1,0:T(8,128)S(1)} collective-permute-done((f32[32,256]{1,0:T(8,128)S(1)}, f32[32,256]{1,0:T(8,128)S(1)}, u32[]{:S(2)}, u32[]{:S(2)}) %collective-permute-start) | collective-permute-done | bytes 32800 | tf_op jit(solution)/shard_map/ppermute | solution.py:121
  6.7 2.7 %collective-permute-start.1 = (f32[32,256]{1,0:T(8,128)S(1)}, f32[32,256]{1,0:T(8,128)S(1)}, u32[]{:S(2)}, u32[]{:S(2)}) collective-permute-start(f32[32,256]{1,0:T(8,128)S(1)} %max.30), channel_id=1, source_target_pairs={{0,5},{1,4},{2,7},{3,6},{4,1},{5,0},{6,3},{7,2},{8,13},{9,12},{10,... | collective-permute-start | bytes 98312 | tf_op jit(solution)/shard_map/ppermute | solution.py:121
  9.4 1.6 %collective-permute-done.1 = f32[32,256]{1,0:T(8,128)S(1)} collective-permute-done((f32[32,256]{1,0:T(8,128)S(1)}, f32[32,256]{1,0:T(8,128)S(1)}, u32[]{:S(2)}, u32[]{:S(2)}) %collective-permute-start.1) | collective-permute-done | bytes 32800 | tf_op jit(solution)/shard_map/ppermute | solution.py:121
  11.0 1.5 %collective-permute-start.2 = (f32[32,256]{1,0:T(8,128)S(1)}, f32[32,256]{1,0:T(8,128)S(1)}, u32[]{:S(2)}, u32[]{:S(2)}) collective-permute-start(f32[32,256]{1,0:T(8,128)S(1)} %max.31), channel_id=1, source_target_pairs={{0,9},{1,8},{2,11},{3,10},{4,13},{5,12},{6,15},{7,14},{8,1},{9,0},... | collective-permute-start | bytes 98312 | tf_op jit(solution)/shard_map/ppermute | solution.py:121
  12.5 1.9 %collective-permute-done.2 = f32[32,256]{1,0:T(8,128)S(1)} collective-permute-done((f32[32,256]{1,0:T(8,128)S(1)}, f32[32,256]{1,0:T(8,128)S(1)}, u32[]{:S(2)}, u32[]{:S(2)}) %collective-permute-start.2) | collective-permute-done | bytes 32800 | tf_op jit(solution)/shard_map/ppermute | solution.py:121
  14.4 1.4 %collective-permute-start.3 = (f32[32,256]{1,0:T(8,128)S(1)}, f32[32,256]{1,0:T(8,128)S(1)}, u32[]{:S(2)}, u32[]{:S(2)}) collective-permute-start(f32[32,256]{1,0:T(8,128)S(1)} %max.32), channel_id=1, source_target_pairs={{0,3},{1,2},{2,1},{3,0},{4,7},{5,6},{6,5},{7,4},{8,11},{9,10},{10,... | collective-permute-start | bytes 98312 | tf_op jit(solution)/shard_map/ppermute | solution.py:121
  15.8 2.0 %collective-permute-done.3 = f32[32,256]{1,0:T(8,128)S(1)} collective-permute-done((f32[32,256]{1,0:T(8,128)S(1)}, f32[32,256]{1,0:T(8,128)S(1)}, u32[]{:S(2)}, u32[]{:S(2)}) %collective-permute-start.3) | collective-permute-done | bytes 32800 | tf_op jit(solution)/shard_map/ppermute | solution.py:121
  17.7 2.5 %collective-permute-start.4 = (f32[32,256]{1,0:T(8,128)S(1)}, f32[32,256]{1,0:T(8,128)S(1)}, u32[]{:S(2)}, u32[]{:S(2)}) collective-permute-start(f32[32,256]{1,0:T(8,128)S(1)} %max.33), channel_id=1, source_target_pairs={{0,17},{1,16},{2,19},{3,18},{4,21},{5,20},{6,23},{7,22},{8,25},{9,... | collective-permute-start | bytes 98312 | tf_op jit(solution)/shard_map/ppermute | solution.py:121
  20.3 1.7 %collective-permute-done.4 = f32[32,256]{1,0:T(8,128)S(1)} collective-permute-done((f32[32,256]{1,0:T(8,128)S(1)}, f32[32,256]{1,0:T(8,128)S(1)}, u32[]{:S(2)}, u32[]{:S(2)}) %collective-permute-start.4) | collective-permute-done | bytes 32800 | tf_op jit(solution)/shard_map/ppermute | solution.py:121
  22.0 1.5 %next_peaks.1 = f32[32,256]{1,0:T(8,128)S(1)} custom-call(s32[1,6]{1,0:T(1,128)S(1)} %copy-done.1, s32[1,6]{1,0:T(1,128)S(1)} %copy-done.2, s32[1,1]{1,0:T(1,128)S(6)} %copy.6.count_ref, f32[6,256,256]{2,1,0:T(8,128)S(1)} %get-tuple-element.4.held_ref, f32[32,256]{1,0:T(8,128)S(1)} %max.34.refs_0_), custom_call_target="tpu_custom_call" | custom-call | tf_op jit(solution)/shard_map/next_peaks/pallas_call | solution.py:158
  23.5 0.1 collective-permute-start.5
  23.6 1.2 %collective-permute-done.5 = f32[32,256]{1,0:T(8,128)S(1)} collective-permute-done((f32[32,256]{1,0:T(8,128)S(1)}, f32[32,256]{1,0:T(8,128)S(1)}, u32[]{:S(2)}, u32[]{:S(2)}) %collective-permute-start.5) | collective-permute-done | bytes 32800 | tf_op jit(solution)/shard_map/ppermute | solution.py:121
  24.8 2.3 %collective-permute-start.6 = (f32[32,256]{1,0:T(8,128)S(1)}, f32[32,256]{1,0:T(8,128)S(1)}, u32[]{:S(2)}, u32[]{:S(2)}) collective-permute-start(f32[32,256]{1,0:T(8,128)S(1)} %max.35), channel_id=1, source_target_pairs={{0,5},{1,4},{2,7},{3,6},{4,1},{5,0},{6,3},{7,2},{8,13},{9,12},{10,... | collective-permute-start | bytes 98312 | tf_op jit(solution)/shard_map/ppermute | solution.py:121
  27.1 1.6 %collective-permute-done.6 = f32[32,256]{1,0:T(8,128)S(1)} collective-permute-done((f32[32,256]{1,0:T(8,128)S(1)}, f32[32,256]{1,0:T(8,128)S(1)}, u32[]{:S(2)}, u32[]{:S(2)}) %collective-permute-start.6) | collective-permute-done | bytes 32800 | tf_op jit(solution)/shard_map/ppermute | solution.py:121
  28.7 0.9 %collective-permute-start.7 = (f32[32,256]{1,0:T(8,128)S(1)}, f32[32,256]{1,0:T(8,128)S(1)}, u32[]{:S(2)}, u32[]{:S(2)}) collective-permute-start(f32[32,256]{1,0:T(8,128)S(1)} %max.36), channel_id=1, source_target_pairs={{0,9},{1,8},{2,11},{3,10},{4,13},{5,12},{6,15},{7,14},{8,1},{9,0},... | collective-permute-start | bytes 98312 | tf_op jit(solution)/shard_map/ppermute | solution.py:121
  29.6 2.4 %collective-permute-done.7 = f32[32,256]{1,0:T(8,128)S(1)} collective-permute-done((f32[32,256]{1,0:T(8,128)S(1)}, f32[32,256]{1,0:T(8,128)S(1)}, u32[]{:S(2)}, u32[]{:S(2)}) %collective-permute-start.7) | collective-permute-done | bytes 32800 | tf_op jit(solution)/shard_map/ppermute | solution.py:121
  32.1 1.1 %collective-permute-start.8 = (f32[32,256]{1,0:T(8,128)S(1)}, f32[32,256]{1,0:T(8,128)S(1)}, u32[]{:S(2)}, u32[]{:S(2)}) collective-permute-start(f32[32,256]{1,0:T(8,128)S(1)} %max.37), channel_id=1, source_target_pairs={{0,3},{1,2},{2,1},{3,0},{4,7},{5,6},{6,5},{7,4},{8,11},{9,10},{10,... | collective-permute-start | bytes 98312 | tf_op jit(solution)/shard_map/ppermute | solution.py:121
  33.1 2.3 %collective-permute-done.8 = f32[32,256]{1,0:T(8,128)S(1)} collective-permute-done((f32[32,256]{1,0:T(8,128)S(1)}, f32[32,256]{1,0:T(8,128)S(1)}, u32[]{:S(2)}, u32[]{:S(2)}) %collective-permute-start.8) | collective-permute-done | bytes 32800 | tf_op jit(solution)/shard_map/ppermute | solution.py:121
  35.4 2.0 %collective-permute-start.9 = (f32[32,256]{1,0:T(8,128)S(1)}, f32[32,256]{1,0:T(8,128)S(1)}, u32[]{:S(2)}, u32[]{:S(2)}) collective-permute-start(f32[32,256]{1,0:T(8,128)S(1)} %max.38), channel_id=1, source_target_pairs={{0,17},{1,16},{2,19},{3,18},{4,21},{5,20},{6,23},{7,22},{8,25},{9,... | collective-permute-start | bytes 98312 | tf_op jit(solution)/shard_map/ppermute | solution.py:121
  37.4 2.3 %collective-permute-done.9 = f32[32,256]{1,0:T(8,128)S(1)} collective-permute-done((f32[32,256]{1,0:T(8,128)S(1)}, f32[32,256]{1,0:T(8,128)S(1)}, u32[]{:S(2)}, u32[]{:S(2)}) %collective-permute-start.9) | collective-permute-done | bytes 32800 | tf_op jit(solution)/shard_map/ppermute | solution.py:121
  39.6 2.6 %scaled_tiles.1 = (f32[1,6,256,256]{3,2,1,0:T(8,128)}, f32[4,256]{1,0:T(4,128)}) custom-call(s32[1,6]{1,0:T(1,128)S(1)} %copy-done.1, s32[1,6]{1,0:T(1,128)S(1)} %copy-done.2, s32[1,1]{1,0:T(1,128)S(6)} %copy.6.count_ref, f32[6,256,256]{2,1,0:T(8,128)S(1)} %get-tuple-element.4.held_ref, f32[32,256]{1,0:T(8,128)S(1)} %max.34.refs_0_, f32[32,256]{1,0:T(8,128)S(1)} %max.39.refs_1_), custom_call_target="tpu_custom_call" | custom-call | tf_op jit(solution)/shard_map/scaled_tiles/pallas_call | solution.py:168
  (10 shorter events, 0.1 us)
Async XLA Ops:
  1.3 1.4 %copy-start = (f32[1,6,256,256]{3,2,1,0:T(8,128)S(1)}, f32[1,6,256,256]{3,2,1,0:T(8,128)}, u32[]{:S(2)}) copy-start(f32[1,6,256,256]{3,2,1,0:T(8,128)} %tiles_ref.1) | copy-start | bytes 4718596
  2.7 0.7 %copy-start.1 = (s32[1,6]{1,0:T(1,128)S(1)}, s32[1,6]{1,0:T(1,128)}, u32[]{:S(2)}) copy-start(s32[1,6]{1,0:T(1,128)} %rows_ref.5) | copy-start | bytes 76
  3.3 0.7 %copy-start.2 = (s32[1,6]{1,0:T(1,128)S(1)}, s32[1,6]{1,0:T(1,128)}, u32[]{:S(2)}) copy-start(s32[1,6]{1,0:T(1,128)} %cols_ref.5) | copy-start | bytes 76
  5.4 1.3 %collective-permute-start = (f32[32,256]{1,0:T(8,128)S(1)}, f32[32,256]{1,0:T(8,128)S(1)}, u32[]{:S(2)}, u32[]{:S(2)}) collective-permute-start(f32[32,256]{1,0:T(8,128)S(1)} %get-tuple-element.5), channel_id=1, source_target_pairs={{0,1},{1,0},{2,3},{3,2},{4,5},{5,4},{6,7},{7,6},{8,9},{9,8},{10,11... | collective-permute-start | bytes 98312 | tf_op jit(solution)/shard_map/ppermute | solution.py:121
  6.7 4.3 %collective-permute-start.1 = (f32[32,256]{1,0:T(8,128)S(1)}, f32[32,256]{1,0:T(8,128)S(1)}, u32[]{:S(2)}, u32[]{:S(2)}) collective-permute-start(f32[32,256]{1,0:T(8,128)S(1)} %max.30), channel_id=1, source_target_pairs={{0,5},{1,4},{2,7},{3,6},{4,1},{5,0},{6,3},{7,2},{8,13},{9,12},{10,... | collective-permute-start | bytes 98312 | tf_op jit(solution)/shard_map/ppermute | solution.py:121
  11.0 3.3 %collective-permute-start.2 = (f32[32,256]{1,0:T(8,128)S(1)}, f32[32,256]{1,0:T(8,128)S(1)}, u32[]{:S(2)}, u32[]{:S(2)}) collective-permute-start(f32[32,256]{1,0:T(8,128)S(1)} %max.31), channel_id=1, source_target_pairs={{0,9},{1,8},{2,11},{3,10},{4,13},{5,12},{6,15},{7,14},{8,1},{9,0},... | collective-permute-start | bytes 98312 | tf_op jit(solution)/shard_map/ppermute | solution.py:121
  14.4 3.3 %collective-permute-start.3 = (f32[32,256]{1,0:T(8,128)S(1)}, f32[32,256]{1,0:T(8,128)S(1)}, u32[]{:S(2)}, u32[]{:S(2)}) collective-permute-start(f32[32,256]{1,0:T(8,128)S(1)} %max.32), channel_id=1, source_target_pairs={{0,3},{1,2},{2,1},{3,0},{4,7},{5,6},{6,5},{7,4},{8,11},{9,10},{10,... | collective-permute-start | bytes 98312 | tf_op jit(solution)/shard_map/ppermute | solution.py:121
  17.7 4.2 %collective-permute-start.4 = (f32[32,256]{1,0:T(8,128)S(1)}, f32[32,256]{1,0:T(8,128)S(1)}, u32[]{:S(2)}, u32[]{:S(2)}) collective-permute-start(f32[32,256]{1,0:T(8,128)S(1)} %max.33), channel_id=1, source_target_pairs={{0,17},{1,16},{2,19},{3,18},{4,21},{5,20},{6,23},{7,22},{8,25},{9,... | collective-permute-start | bytes 98312 | tf_op jit(solution)/shard_map/ppermute | solution.py:121
  23.5 1.3 %collective-permute-start.5 = (f32[32,256]{1,0:T(8,128)S(1)}, f32[32,256]{1,0:T(8,128)S(1)}, u32[]{:S(2)}, u32[]{:S(2)}) collective-permute-start(f32[32,256]{1,0:T(8,128)S(1)} %next_peaks.1), channel_id=1, source_target_pairs={{0,1},{1,0},{2,3},{3,2},{4,5},{5,4},{6,7},{7,6},{8,9},{9,8},{10,11... | collective-permute-start | bytes 98312 | tf_op jit(solution)/shard_map/ppermute | solution.py:121
  24.8 3.9 %collective-permute-start.6 = (f32[32,256]{1,0:T(8,128)S(1)}, f32[32,256]{1,0:T(8,128)S(1)}, u32[]{:S(2)}, u32[]{:S(2)}) collective-permute-start(f32[32,256]{1,0:T(8,128)S(1)} %max.35), channel_id=1, source_target_pairs={{0,5},{1,4},{2,7},{3,6},{4,1},{5,0},{6,3},{7,2},{8,13},{9,12},{10,... | collective-permute-start | bytes 98312 | tf_op jit(solution)/shard_map/ppermute | solution.py:121
  28.7 3.3 %collective-permute-start.7 = (f32[32,256]{1,0:T(8,128)S(1)}, f32[32,256]{1,0:T(8,128)S(1)}, u32[]{:S(2)}, u32[]{:S(2)}) collective-permute-start(f32[32,256]{1,0:T(8,128)S(1)} %max.36), channel_id=1, source_target_pairs={{0,9},{1,8},{2,11},{3,10},{4,13},{5,12},{6,15},{7,14},{8,1},{9,0},... | collective-permute-start | bytes 98312 | tf_op jit(solution)/shard_map/ppermute | solution.py:121
  32.1 3.3 %collective-permute-start.8 = (f32[32,256]{1,0:T(8,128)S(1)}, f32[32,256]{1,0:T(8,128)S(1)}, u32[]{:S(2)}, u32[]{:S(2)}) collective-permute-start(f32[32,256]{1,0:T(8,128)S(1)} %max.37), channel_id=1, source_target_pairs={{0,3},{1,2},{2,1},{3,0},{4,7},{5,6},{6,5},{7,4},{8,11},{9,10},{10,... | collective-permute-start | bytes 98312 | tf_op jit(solution)/shard_map/ppermute | solution.py:121
  35.4 4.2 %collective-permute-start.9 = (f32[32,256]{1,0:T(8,128)S(1)}, f32[32,256]{1,0:T(8,128)S(1)}, u32[]{:S(2)}, u32[]{:S(2)}) collective-permute-start(f32[32,256]{1,0:T(8,128)S(1)} %max.38), channel_id=1, source_target_pairs={{0,17},{1,16},{2,19},{3,18},{4,21},{5,20},{6,23},{7,22},{8,25},{9,... | collective-permute-start | bytes 98312 | tf_op jit(solution)/shard_map/ppermute | solution.py:121

commit v3 on v2

v3 whole, which is shorter than its diff:
```python
import functools

import jax
import jax.numpy as jnp
from jax import lax
from jax.experimental import pallas as pl
from jax.experimental.pallas import tpu as pltpu
from jax.sharding import PartitionSpec as P

ROWB = 4
ITERS = 2
PARAMS = pltpu.CompilerParams(vmem_limit_bytes=16 << 20)
BOTH = ("wide", "narrow")
SMEM = pl.BlockSpec(memory_space=pltpu.SMEM)
VMEM = pl.BlockSpec(memory_space=pltpu.VMEM)
HBM = pl.BlockSpec(memory_space=pltpu.HBM)


def kept(values, space):
    return [pltpu.with_memory_space_constraint(value, space) for value in values]


def raise_row(peak_ref, index, row):
    peak_ref[pl.ds(index, 1), :] = jnp.maximum(peak_ref[pl.ds(index, 1), :], row)


def lane_max(block):
    half = block.shape[1] // 2
    folded = jnp.maximum(block[:, :half], block[:, half:])
    return jnp.max(folded.T, axis=0, keepdims=True)


def as_column(row, half):
    return jnp.broadcast_to(row, (half, row.shape[1])).T


def scale_of(old_refs):
    scale = lax.rsqrt(old_refs[0][...])
    for old_ref in old_refs[1:]:
        scale = scale * lax.rsqrt(old_ref[...])
    return scale


def first_kernel(
    count_ref, rows_in, cols_in, tiles_ref, rows_ref, cols_ref, held_ref, peak_ref, sems
):
    slots = tiles_ref.shape[1]
    moves = [(rows_in, rows_ref), (cols_in, cols_ref)]
    moves += [(tiles_ref.at[0, s], held_ref.at[s]) for s in range(slots)]
    copies = [
        pltpu.make_async_copy(source, target, sems.at[k])
        for k, (source, target) in enumerate(moves)
    ]
    for copy in copies:
        copy.start()
    peak_ref[...] = jnp.zeros_like(peak_ref)
    for copy in copies[:2]:
        copy.wait()
    for s in range(slots):
        copies[2 + s].wait()
        live = s < count_ref[0, 0]
        size = jnp.abs(held_ref[s])
        column_max = jnp.max(size, axis=0, keepdims=True)
        raise_row(peak_ref, cols_ref[0, s], jnp.where(live, column_max, 0.0))
        raise_row(peak_ref, rows_ref[0, s], jnp.where(live, lane_max(size), 0.0))


def next_kernel(rows_ref, cols_ref, count_ref, held_ref, *refs):
    *old_refs, peak_ref, scale_ref = refs
    slots, _, tile = held_ref.shape
    half = tile // 2
    scale_ref[...] = scale_of(old_refs)
    peak_ref[...] = jnp.zeros_like(peak_ref)
    for s in range(slots):
        live = s < count_ref[0, 0]
        size = jnp.abs(held_ref[s])
        row, col = rows_ref[0, s], cols_ref[0, s]
        left = scale_ref[pl.ds(row, 1), :]
        right = scale_ref[pl.ds(col, 1), :]
        raise_row(peak_ref, row, jnp.where(live, lane_max(size * right) * left, 0.0))
        column = as_column(left, half)
        below = jnp.concatenate(
            [
                jnp.max(size[:, :half] * column, axis=0, keepdims=True),
                jnp.max(size[:, half:] * column, axis=0, keepdims=True),
            ],
            axis=1,
        )
        raise_row(peak_ref, col, jnp.where(live, below * right, 0.0))


def last_kernel(row_blocks, rows_ref, cols_ref, count_ref, held_ref, *refs):
    *old_refs, out_ref, own_out, scale_ref, own_ref, done_ref, sems = refs
    slots, _, tile = held_ref.shape
    half = tile // 2
    scale_ref[...] = scale_of(old_refs)
    start = lax.axis_index("wide") * row_blocks
    for k in range(row_blocks):
        own_ref[pl.ds(k, 1), :] = scale_ref[pl.ds(start + k, 1), :]
    copies = [pltpu.make_async_copy(own_ref, own_out, sems.at[slots])]
    copies[0].start()
    for s in range(slots):
        live = s < count_ref[0, 0]
        left = scale_ref[pl.ds(rows_ref[0, s], 1), :]
        right = scale_ref[pl.ds(cols_ref[0, s], 1), :]
        column = as_column(left, half)
        for part in (slice(0, half), slice(half, tile)):
            scaled = held_ref[s, :, part] * column * right[:, part]
            done_ref[s, :, part] = jnp.where(live, scaled, 0.0)
        copies.append(pltpu.make_async_copy(done_ref.at[s], out_ref.at[0, s], sems.at[s]))
        copies[-1].start()
    for copy in copies:
        copy.wait()


def swap(values, wide_size, narrow_size, wide_bit, narrow_bit):
    pairs = []
    for w in range(wide_size):
        for n in range(narrow_size):
            there = (w ^ wide_bit) * narrow_size + (n ^ narrow_bit)
            pairs.append((w * narrow_size + n, there))
    return jnp.maximum(values, lax.ppermute(values, BOTH, pairs))


def max_over_devices(values, wide_size, narrow_size):
    values = swap(values, wide_size, narrow_size, 0, 1)
    steps = []
    bit = 1
    while bit < wide_size:
        steps.append((bit, 1))
        bit *= 2
    bit = 2
    while bit < narrow_size:
        steps.insert(len(steps) - 1, (0, bit + 1))
        bit *= 2
    for wide_bit, narrow_bit in steps:
        values = swap(values, wide_size, narrow_size, wide_bit, narrow_bit)
    return values


def on_device(wide_size, narrow_size, tiles, tile_rows, tile_cols, tile_counts):
    slots, tile = tiles.shape[1], tiles.shape[2]
    blocks = ROWB * wide_size
    rows, cols, held, part = pl.pallas_call(
        first_kernel,
        out_shape=(
            pltpu.SMEM(tile_rows.shape, jnp.int32),
            pltpu.SMEM(tile_cols.shape, jnp.int32),
            pltpu.VMEM((slots, tile, tile), jnp.float32),
            pltpu.VMEM((blocks, tile), jnp.float32),
        ),
        in_specs=[SMEM, HBM, HBM, HBM],
        out_specs=(SMEM, SMEM, VMEM, VMEM),
        scratch_shapes=[pltpu.SemaphoreType.DMA((2 + slots,))],
        compiler_params=PARAMS,
        name="first_peaks",
    )(tile_counts, *kept((tile_rows, tile_cols, tiles), pltpu.HBM))
    places = (*kept((rows, cols), pltpu.SMEM), tile_counts)
    held = kept([held], pltpu.VMEM)
    peaks = []
    for iteration in range(ITERS):
        if iteration:
            part = pl.pallas_call(
                next_kernel,
                out_shape=pltpu.VMEM((blocks, tile), jnp.float32),
                in_specs=[SMEM] * 3 + [VMEM] * (1 + len(peaks)),
                out_specs=VMEM,
                scratch_shapes=[pltpu.VMEM((blocks, tile), jnp.float32)],
                compiler_params=PARAMS,
                name="next_peaks",
            )(*places, *held, *peaks)
        full = max_over_devices(part, wide_size, narrow_size)
        peaks += kept([full], pltpu.VMEM)
    return pl.pallas_call(
        functools.partial(last_kernel, ROWB),
        out_shape=(
            jax.ShapeDtypeStruct(tiles.shape, jnp.float32),
            jax.ShapeDtypeStruct((ROWB, tile), jnp.float32),
        ),
        in_specs=[SMEM] * 3 + [VMEM] * (1 + len(peaks)),
        out_specs=(HBM, HBM),
        scratch_shapes=[
            pltpu.VMEM((blocks, tile), jnp.float32),
            pltpu.VMEM((ROWB, tile), jnp.float32),
            pltpu.VMEM((slots, tile, tile), jnp.float32),
            pltpu.SemaphoreType.DMA((slots + 1,)),
        ],
        compiler_params=PARAMS,
        name="scaled_tiles",
    )(*places, *held, *peaks)


def solution(mesh):
    wide_size, narrow_size = mesh.shape["wide"], mesh.shape["narrow"]
    placed = (
        P("wide", "narrow", None, None),
        P("wide", "narrow"),
        P("wide", "narrow"),
        P("wide", "narrow"),
    )
    return jax.shard_map(
        functools.partial(on_device, wide_size, narrow_size),
        mesh=mesh,
        in_specs=placed,
        out_specs=(P("wide", "narrow", None, None), P("wide", None)),
        check_vma=False,
    )
```

time: 42.4 us -> 38 us (0.90)
  starting transfers between devices: 14.5 us -> 17.9 us
  waiting for transfers between devices: 18.1 us -> 15 us
  local copies, waits for them, and re-layouts: 2.71 us -> 0 us
  Pallas kernels: 5.53 us -> 3.57 us
    ppermute x10, starting transfers between devices: 14.5 us -> 17.9 us  [swap(): return jnp.maximum(values, lax.ppermute(values, BOTH, pairs))]
    ppermute x10, waiting for transfers between devices: 18.1 us -> 15 us  [swap(): return jnp.maximum(values, lax.ppermute(values, BOTH, pairs))]
    unnamed x6 -> x0, local copies, waits for them, and re-layouts: 2.71 us -> none
    pallas_call x3, Pallas kernels: 5.53 us -> 3.57 us  [the longest x1 1.73 us: on_device(): pl.pallas_call(first_kernel, out_shape=(pltpu.SMEM(tile_rows.shape, jnp.i...]
where the time goes in v3:
time: 38 us; the launch traced here: 37.8 us
  starting transfers between devices  17.9 us (47%)
  waiting for transfers between devices  15 us (39%)
  Pallas kernels  3.57 us (9%)
  between operations  1.3 us (3%)
    ppermute x10, starting transfers between devices, swap(): return jnp.maximum(values, lax.ppermute(values, BOTH, pairs))  17.9 us
    ppermute x10, waiting for transfers between devices, swap(): return jnp.maximum(values, lax.ppermute(values, BOTH, pairs))  15 us
    pallas_call x1, Pallas kernels, on_device(): pl.pallas_call(first_kernel, out_shape=(pltpu.SMEM(tile_rows.shape, jnp.i...  1.73 us
    pallas_call x1, Pallas kernels, on_device(): pl.pallas_call(functools.partial(last_kernel, ROWB), out_shape=(jax.Shape...  1.31 us
  transfers between devices with their start and end apart: 10, of which 10 were waited for; matrix products, arithmetic and copies ran while one was open for 0% of the time, Pallas kernels for 0%

profile of v3, /device:TPU:0, one launch (start us, length us, event | category | flops | bytes accessed | tf_op | source)
XLA Modules:
  0.0 37.8 jit_solution(16753712403478227095)
XLA Ops:
  1.3 1.7 %first_peaks.1 = (s32[1,6]{1,0:T(1,128)S(4)}, s32[1,6]{1,0:T(1,128)S(4)}, f32[6,256,256]{2,1,0:T(8,128)S(1)}, f32[32,256]{1,0:T(8,128)S(1)}) custom-call(s32[1,1]{1,0:T(1,128)S(6)} %copy.6.count_ref, s32[1,6]{1,0:T(1,128)} %rows_in.1, s32[1,6]{1,0:T(1,128)} %cols_in.1, f32[1,6,256,256]{3,2,1,0:T(8,128)} %tiles_ref.1), custom_call_target="tpu_custom_call" | custom-call | tf_op jit(solution)/shard_map/first_peaks/pallas_call | solution.py:144
  3.0 0.5 %collective-permute-start = (f32[32,256]{1,0:T(8,128)S(1)}, f32[32,256]{1,0:T(8,128)S(1)}, u32[]{:S(2)}, u32[]{:S(2)}) collective-permute-start(f32[32,256]{1,0:T(8,128)S(1)} %get-tuple-element.9), channel_id=1, source_target_pairs={{0,1},{1,0},{2,3},{3,2},{4,5},{5,4},{6,7},{7,6},{8,9},{9,8},{10,11... | collective-permute-start | bytes 98312 | tf_op jit(solution)/shard_map/ppermute | solution.py:122
  3.5 0.9 %collective-permute-done = f32[32,256]{1,0:T(8,128)S(1)} collective-permute-done((f32[32,256]{1,0:T(8,128)S(1)}, f32[32,256]{1,0:T(8,128)S(1)}, u32[]{:S(2)}, u32[]{:S(2)}) %collective-permute-start) | collective-permute-done | bytes 32800 | tf_op jit(solution)/shard_map/ppermute | solution.py:122
  4.4 2.6 %collective-permute-start.1 = (f32[32,256]{1,0:T(8,128)S(1)}, f32[32,256]{1,0:T(8,128)S(1)}, u32[]{:S(2)}, u32[]{:S(2)}) collective-permute-start(f32[32,256]{1,0:T(8,128)S(1)} %max.30), channel_id=1, source_target_pairs={{0,5},{1,4},{2,7},{3,6},{4,1},{5,0},{6,3},{7,2},{8,13},{9,12},{10,... | collective-permute-start | bytes 98312 | tf_op jit(solution)/shard_map/ppermute | solution.py:122
  7.0 1.6 %collective-permute-done.1 = f32[32,256]{1,0:T(8,128)S(1)} collective-permute-done((f32[32,256]{1,0:T(8,128)S(1)}, f32[32,256]{1,0:T(8,128)S(1)}, u32[]{:S(2)}, u32[]{:S(2)}) %collective-permute-start.1) | collective-permute-done | bytes 32800 | tf_op jit(solution)/shard_map/ppermute | solution.py:122
  8.6 1.8 %collective-permute-start.2 = (f32[32,256]{1,0:T(8,128)S(1)}, f32[32,256]{1,0:T(8,128)S(1)}, u32[]{:S(2)}, u32[]{:S(2)}) collective-permute-start(f32[32,256]{1,0:T(8,128)S(1)} %max.31), channel_id=1, source_target_pairs={{0,9},{1,8},{2,11},{3,10},{4,13},{5,12},{6,15},{7,14},{8,1},{9,0},... | collective-permute-start | bytes 98312 | tf_op jit(solution)/shard_map/ppermute | solution.py:122
  10.4 1.6 %collective-permute-done.2 = f32[32,256]{1,0:T(8,128)S(1)} collective-permute-done((f32[32,256]{1,0:T(8,128)S(1)}, f32[32,256]{1,0:T(8,128)S(1)}, u32[]{:S(2)}, u32[]{:S(2)}) %collective-permute-start.2) | collective-permute-done | bytes 32800 | tf_op jit(solution)/shard_map/ppermute | solution.py:122
  12.0 1.7 %collective-permute-start.3 = (f32[32,256]{1,0:T(8,128)S(1)}, f32[32,256]{1,0:T(8,128)S(1)}, u32[]{:S(2)}, u32[]{:S(2)}) collective-permute-start(f32[32,256]{1,0:T(8,128)S(1)} %max.32), channel_id=1, source_target_pairs={{0,3},{1,2},{2,1},{3,0},{4,7},{5,6},{6,5},{7,4},{8,11},{9,10},{10,... | collective-permute-start | bytes 98312 | tf_op jit(solution)/shard_map/ppermute | solution.py:122
  13.7 1.7 %collective-permute-done.3 = f32[32,256]{1,0:T(8,128)S(1)} collective-permute-done((f32[32,256]{1,0:T(8,128)S(1)}, f32[32,256]{1,0:T(8,128)S(1)}, u32[]{:S(2)}, u32[]{:S(2)}) %collective-permute-start.3) | collective-permute-done | bytes 32800 | tf_op jit(solution)/shard_map/ppermute | solution.py:122
  15.4 2.8 %collective-permute-start.4 = (f32[32,256]{1,0:T(8,128)S(1)}, f32[32,256]{1,0:T(8,128)S(1)}, u32[]{:S(2)}, u32[]{:S(2)}) collective-permute-start(f32[32,256]{1,0:T(8,128)S(1)} %max.33), channel_id=1, source_target_pairs={{0,17},{1,16},{2,19},{3,18},{4,21},{5,20},{6,23},{7,22},{8,25},{9,... | collective-permute-start | bytes 98312 | tf_op jit(solution)/shard_map/ppermute | solution.py:122
  18.2 1.6 %collective-permute-done.4 = f32[32,256]{1,0:T(8,128)S(1)} collective-permute-done((f32[32,256]{1,0:T(8,128)S(1)}, f32[32,256]{1,0:T(8,128)S(1)}, u32[]{:S(2)}, u32[]{:S(2)}) %collective-permute-start.4) | collective-permute-done | bytes 32800 | tf_op jit(solution)/shard_map/ppermute | solution.py:122
  19.8 0.5 %next_peaks.1 = f32[32,256]{1,0:T(8,128)S(1)} custom-call(s32[1,6]{1,0:T(1,128)S(4)} %get-tuple-element.6.rows_ref, s32[1,6]{1,0:T(1,128)S(4)} %get-tuple-element.7.cols_ref, s32[1,1]{1,0:T(1,128)S(6)} %copy.6.count_ref, f32[6,256,256]{2,1,0:T(8,128)S(1)} %get-tuple-element.8.held_ref, f32[32,256]{1,0:T(8,128)S(1)} %max.34.refs_0_), custom_call_target="tpu_custom_call" | custom-call | tf_op jit(solution)/shard_map/next_peaks/pallas_call | solution.py:163
  20.3 0.4 %collective-permute-start.5 = (f32[32,256]{1,0:T(8,128)S(1)}, f32[32,256]{1,0:T(8,128)S(1)}, u32[]{:S(2)}, u32[]{:S(2)}) collective-permute-start(f32[32,256]{1,0:T(8,128)S(1)} %next_peaks.1), channel_id=1, source_target_pairs={{0,1},{1,0},{2,3},{3,2},{4,5},{5,4},{6,7},{7,6},{8,9},{9,8},{10,11... | collective-permute-start | bytes 98312 | tf_op jit(solution)/shard_map/ppermute | solution.py:122
  20.7 0.9 %collective-permute-done.5 = f32[32,256]{1,0:T(8,128)S(1)} collective-permute-done((f32[32,256]{1,0:T(8,128)S(1)}, f32[32,256]{1,0:T(8,128)S(1)}, u32[]{:S(2)}, u32[]{:S(2)}) %collective-permute-start.5) | collective-permute-done | bytes 32800 | tf_op jit(solution)/shard_map/ppermute | solution.py:122
  21.6 1.6 %collective-permute-start.6 = (f32[32,256]{1,0:T(8,128)S(1)}, f32[32,256]{1,0:T(8,128)S(1)}, u32[]{:S(2)}, u32[]{:S(2)}) collective-permute-start(f32[32,256]{1,0:T(8,128)S(1)} %max.35), channel_id=1, source_target_pairs={{0,5},{1,4},{2,7},{3,6},{4,1},{5,0},{6,3},{7,2},{8,13},{9,12},{10,... | collective-permute-start | bytes 98312 | tf_op jit(solution)/shard_map/ppermute | solution.py:122
  23.1 1.8 %collective-permute-done.6 = f32[32,256]{1,0:T(8,128)S(1)} collective-permute-done((f32[32,256]{1,0:T(8,128)S(1)}, f32[32,256]{1,0:T(8,128)S(1)}, u32[]{:S(2)}, u32[]{:S(2)}) %collective-permute-start.6) | collective-permute-done | bytes 32800 | tf_op jit(solution)/shard_map/ppermute | solution.py:122
  24.9 1.8 %collective-permute-start.7 = (f32[32,256]{1,0:T(8,128)S(1)}, f32[32,256]{1,0:T(8,128)S(1)}, u32[]{:S(2)}, u32[]{:S(2)}) collective-permute-start(f32[32,256]{1,0:T(8,128)S(1)} %max.36), channel_id=1, source_target_pairs={{0,9},{1,8},{2,11},{3,10},{4,13},{5,12},{6,15},{7,14},{8,1},{9,0},... | collective-permute-start | bytes 98312 | tf_op jit(solution)/shard_map/ppermute | solution.py:122
  26.7 1.6 %collective-permute-done.7 = f32[32,256]{1,0:T(8,128)S(1)} collective-permute-done((f32[32,256]{1,0:T(8,128)S(1)}, f32[32,256]{1,0:T(8,128)S(1)}, u32[]{:S(2)}, u32[]{:S(2)}) %collective-permute-start.7) | collective-permute-done | bytes 32800 | tf_op jit(solution)/shard_map/ppermute | solution.py:122
  28.3 1.5 %collective-permute-start.8 = (f32[32,256]{1,0:T(8,128)S(1)}, f32[32,256]{1,0:T(8,128)S(1)}, u32[]{:S(2)}, u32[]{:S(2)}) collective-permute-start(f32[32,256]{1,0:T(8,128)S(1)} %max.37), channel_id=1, source_target_pairs={{0,3},{1,2},{2,1},{3,0},{4,7},{5,6},{6,5},{7,4},{8,11},{9,10},{10,... | collective-permute-start | bytes 98312 | tf_op jit(solution)/shard_map/ppermute | solution.py:122
  29.8 1.9 %collective-permute-done.8 = f32[32,256]{1,0:T(8,128)S(1)} collective-permute-done((f32[32,256]{1,0:T(8,128)S(1)}, f32[32,256]{1,0:T(8,128)S(1)}, u32[]{:S(2)}, u32[]{:S(2)}) %collective-permute-start.8) | collective-permute-done | bytes 32800 | tf_op jit(solution)/shard_map/ppermute | solution.py:122
  31.7 3.3 %collective-permute-start.9 = (f32[32,256]{1,0:T(8,128)S(1)}, f32[32,256]{1,0:T(8,128)S(1)}, u32[]{:S(2)}, u32[]{:S(2)}) collective-permute-start(f32[32,256]{1,0:T(8,128)S(1)} %max.38), channel_id=1, source_target_pairs={{0,17},{1,16},{2,19},{3,18},{4,21},{5,20},{6,23},{7,22},{8,25},{9,... | collective-permute-start | bytes 98312 | tf_op jit(solution)/shard_map/ppermute | solution.py:122
  34.9 1.6 %collective-permute-done.9 = f32[32,256]{1,0:T(8,128)S(1)} collective-permute-done((f32[32,256]{1,0:T(8,128)S(1)}, f32[32,256]{1,0:T(8,128)S(1)}, u32[]{:S(2)}, u32[]{:S(2)}) %collective-permute-start.9) | collective-permute-done | bytes 32800 | tf_op jit(solution)/shard_map/ppermute | solution.py:122
  36.5 1.3 %scaled_tiles.1 = (f32[1,6,256,256]{3,2,1,0:T(8,128)}, f32[4,256]{1,0:T(4,128)}) custom-call(s32[1,6]{1,0:T(1,128)S(4)} %get-tuple-element.6.rows_ref, s32[1,6]{1,0:T(1,128)S(4)} %get-tuple-element.7.cols_ref, s32[1,1]{1,0:T(1,128)S(6)} %copy.6.count_ref, f32[6,256,256]{2,1,0:T(8,128)S(1)} %get-tuple-element.8.held_ref, f32[32,256]{1,0:T(8,128)S(1)} %max.34.refs_0_, ...), custom_call_target="tpu_custom_call" | custom-call | tf_op jit(solution)/shard_map/scaled_tiles/pallas_call | solution.py:174
  (10 shorter events, 0.1 us)
Async XLA Ops:
  3.0 1.4 %collective-permute-start = (f32[32,256]{1,0:T(8,128)S(1)}, f32[32,256]{1,0:T(8,128)S(1)}, u32[]{:S(2)}, u32[]{:S(2)}) collective-permute-start(f32[32,256]{1,0:T(8,128)S(1)} %get-tuple-element.9), channel_id=1, source_target_pairs={{0,1},{1,0},{2,3},{3,2},{4,5},{5,4},{6,7},{7,6},{8,9},{9,8},{10,11... | collective-permute-start | bytes 98312 | tf_op jit(solution)/shard_map/ppermute | solution.py:122
  4.4 4.2 %collective-permute-start.1 = (f32[32,256]{1,0:T(8,128)S(1)}, f32[32,256]{1,0:T(8,128)S(1)}, u32[]{:S(2)}, u32[]{:S(2)}) collective-permute-start(f32[32,256]{1,0:T(8,128)S(1)} %max.30), channel_id=1, source_target_pairs={{0,5},{1,4},{2,7},{3,6},{4,1},{5,0},{6,3},{7,2},{8,13},{9,12},{10,... | collective-permute-start | bytes 98312 | tf_op jit(solution)/shard_map/ppermute | solution.py:122
  8.6 3.4 %collective-permute-start.2 = (f32[32,256]{1,0:T(8,128)S(1)}, f32[32,256]{1,0:T(8,128)S(1)}, u32[]{:S(2)}, u32[]{:S(2)}) collective-permute-start(f32[32,256]{1,0:T(8,128)S(1)} %max.31), channel_id=1, source_target_pairs={{0,9},{1,8},{2,11},{3,10},{4,13},{5,12},{6,15},{7,14},{8,1},{9,0},... | collective-permute-start | bytes 98312 | tf_op jit(solution)/shard_map/ppermute | solution.py:122
  12.0 3.3 %collective-permute-start.3 = (f32[32,256]{1,0:T(8,128)S(1)}, f32[32,256]{1,0:T(8,128)S(1)}, u32[]{:S(2)}, u32[]{:S(2)}) collective-permute-start(f32[32,256]{1,0:T(8,128)S(1)} %max.32), channel_id=1, source_target_pairs={{0,3},{1,2},{2,1},{3,0},{4,7},{5,6},{6,5},{7,4},{8,11},{9,10},{10,... | collective-permute-start | bytes 98312 | tf_op jit(solution)/shard_map/ppermute | solution.py:122
  15.4 4.4 %collective-permute-start.4 = (f32[32,256]{1,0:T(8,128)S(1)}, f32[32,256]{1,0:T(8,128)S(1)}, u32[]{:S(2)}, u32[]{:S(2)}) collective-permute-start(f32[32,256]{1,0:T(8,128)S(1)} %max.33), channel_id=1, source_target_pairs={{0,17},{1,16},{2,19},{3,18},{4,21},{5,20},{6,23},{7,22},{8,25},{9,... | collective-permute-start | bytes 98312 | tf_op jit(solution)/shard_map/ppermute | solution.py:122
  20.3 1.3 %collective-permute-start.5 = (f32[32,256]{1,0:T(8,128)S(1)}, f32[32,256]{1,0:T(8,128)S(1)}, u32[]{:S(2)}, u32[]{:S(2)}) collective-permute-start(f32[32,256]{1,0:T(8,128)S(1)} %next_peaks.1), channel_id=1, source_target_pairs={{0,1},{1,0},{2,3},{3,2},{4,5},{5,4},{6,7},{7,6},{8,9},{9,8},{10,11... | collective-permute-start | bytes 98312 | tf_op jit(solution)/shard_map/ppermute | solution.py:122
  21.6 3.3 %collective-permute-start.6 = (f32[32,256]{1,0:T(8,128)S(1)}, f32[32,256]{1,0:T(8,128)S(1)}, u32[]{:S(2)}, u32[]{:S(2)}) collective-permute-start(f32[32,256]{1,0:T(8,128)S(1)} %max.35), channel_id=1, source_target_pairs={{0,5},{1,4},{2,7},{3,6},{4,1},{5,0},{6,3},{7,2},{8,13},{9,12},{10,... | collective-permute-start | bytes 98312 | tf_op jit(solution)/shard_map/ppermute | solution.py:122
  24.9 3.4 %collective-permute-start.7 = (f32[32,256]{1,0:T(8,128)S(1)}, f32[32,256]{1,0:T(8,128)S(1)}, u32[]{:S(2)}, u32[]{:S(2)}) collective-permute-start(f32[32,256]{1,0:T(8,128)S(1)} %max.36), channel_id=1, source_target_pairs={{0,9},{1,8},{2,11},{3,10},{4,13},{5,12},{6,15},{7,14},{8,1},{9,0},... | collective-permute-start | bytes 98312 | tf_op jit(solution)/shard_map/ppermute | solution.py:122
  28.3 3.3 %collective-permute-start.8 = (f32[32,256]{1,0:T(8,128)S(1)}, f32[32,256]{1,0:T(8,128)S(1)}, u32[]{:S(2)}, u32[]{:S(2)}) collective-permute-start(f32[32,256]{1,0:T(8,128)S(1)} %max.37), channel_id=1, source_target_pairs={{0,3},{1,2},{2,1},{3,0},{4,7},{5,6},{6,5},{7,4},{8,11},{9,10},{10,... | collective-permute-start | bytes 98312 | tf_op jit(solution)/shard_map/ppermute | solution.py:122
  31.7 4.9 %collective-permute-start.9 = (f32[32,256]{1,0:T(8,128)S(1)}, f32[32,256]{1,0:T(8,128)S(1)}, u32[]{:S(2)}, u32[]{:S(2)}) collective-permute-start(f32[32,256]{1,0:T(8,128)S(1)} %max.38), channel_id=1, source_target_pairs={{0,17},{1,16},{2,19},{3,18},{4,21},{5,20},{6,23},{7,22},{8,25},{9,... | collective-permute-start | bytes 98312 | tf_op jit(solution)/shard_map/ppermute | solution.py:122

commit v4 on v3

--- a/solution.py
+++ b/solution.py
@@ -32,13 +32,6 @@
 
 def as_column(row, half):
     return jnp.broadcast_to(row, (half, row.shape[1])).T
-
-
-def scale_of(old_refs):
-    scale = lax.rsqrt(old_refs[0][...])
-    for old_ref in old_refs[1:]:
-        scale = scale * lax.rsqrt(old_ref[...])
-    return scale
 
 
 def first_kernel(
@@ -65,11 +58,10 @@
         raise_row(peak_ref, rows_ref[0, s], jnp.where(live, lane_max(size), 0.0))
 
 
-def next_kernel(rows_ref, cols_ref, count_ref, held_ref, *refs):
-    *old_refs, peak_ref, scale_ref = refs
+def next_kernel(rows_ref, cols_ref, count_ref, held_ref, old_ref, peak_ref, scale_ref):
     slots, _, tile = held_ref.shape
     half = tile // 2
-    scale_ref[...] = scale_of(old_refs)
+    scale_ref[...] = lax.rsqrt(old_ref[...])
     peak_ref[...] = jnp.zeros_like(peak_ref)
     for s in range(slots):
         live = s < count_ref[0, 0]
@@ -87,13 +79,26 @@
             axis=1,
         )
         raise_row(peak_ref, col, jnp.where(live, below * right, 0.0))
-
-
-def last_kernel(row_blocks, rows_ref, cols_ref, count_ref, held_ref, *refs):
-    *old_refs, out_ref, own_out, scale_ref, own_ref, done_ref, sems = refs
+    peak_ref[...] = peak_ref[...] * old_ref[...]
+
+
+def last_kernel(
+    row_blocks,
+    rows_ref,
+    cols_ref,
+    count_ref,
+    held_ref,
+    old_ref,
+    out_ref,
+    own_out,
+    scale_ref,
+    own_ref,
+    done_ref,
+    sems,
+):
     slots, _, tile = held_ref.shape
     half = tile // 2
-    scale_ref[...] = scale_of(old_refs)
+    scale_ref[...] = lax.rsqrt(old_ref[...])
     start = lax.axis_index("wide") * row_blocks
     for k in range(row_blocks):
         own_ref[pl.ds(k, 1), :] = scale_ref[pl.ds(start + k, 1), :]
@@ -113,29 +118,65 @@
         copy.wait()
 
 
-def swap(values, wide_size, narrow_size, wide_bit, narrow_bit):
+def swap(values, partner, wide_size, narrow_size):
     pairs = []
     for w in range(wide_size):
         for n in range(narrow_size):
-            there = (w ^ wide_bit) * narrow_size + (n ^ narrow_bit)
-            pairs.append((w * narrow_size + n, there))
-    return jnp.maximum(values, lax.ppermute(values, BOTH, pairs))
+            wide, narrow = partner(w, n)
+            pairs.append((w * narrow_size + n, wide * narrow_size + narrow))
+    return lax.ppermute(values, BOTH, pairs)
+
+
+def bits(first, last):
+    while first < last:
+        yield first
+        first *= 2
 
 
 def max_over_devices(values, wide_size, narrow_size):
-    values = swap(values, wide_size, narrow_size, 0, 1)
-    steps = []
-    bit = 1
-    while bit < wide_size:
-        steps.append((bit, 1))
-        bit *= 2
-    bit = 2
-    while bit < narrow_size:
-        steps.insert(len(steps) - 1, (0, bit + 1))
-        bit *= 2
+    steps = [(0, 1)]
+    steps += [(bit, 1) for bit in bits(1, wide_size)]
+    steps += [(0, bit + 1) for bit in bits(2, narrow_size)]
     for wide_bit, narrow_bit in steps:
-        values = swap(values, wide_size, narrow_size, wide_bit, narrow_bit)
+        other = swap(
+            values, lambda w, n: (w ^ wide_bit, n ^ narrow_bit), wide_size, narrow_size
+        )
+        values = jnp.maximum(values, other)
     return values
+
+
+def window_max(values, start, window):
+    old = lax.dynamic_slice_in_dim(values, start, window.shape[0], 0)
+    return lax.dynamic_update_slice_in_dim(values, jnp.maximum(old, window), start, 0)
+
+
+def max_over_users(values, wide_size, narrow_size):
+    share = wide_size // narrow_size
+    for wide_bit in (0, *bits(1, share)):
+        other = swap(values, lambda w, n: (w ^ wide_bit, n ^ 1), wide_size, narrow_size)
+        values = jnp.maximum(values, other)
+
+    def along_columns(w, n):
+        group = w // share
+        return (group ^ group >> 1 ^ n >> 1 ^ n) & 1 == 0
+
+    def first(w, n):
+        return (w ^ share, n ^ 1) if along_columns(w, n) else (w, n ^ 3)
+
+    def second(w, n):
+        return (w ^ 2 * share if along_columns(w, n) else w ^ share, n ^ 1)
+
+    pair = 2 * values.shape[0] // narrow_size
+    w, n = lax.axis_index("wide"), lax.axis_index("narrow")
+    column_start, row_start = (n >> 1) * pair, (w // (2 * share)) * pair
+    chosen = along_columns(w, n)
+    start = jnp.where(chosen, column_start, row_start)
+    window = lax.dynamic_slice_in_dim(values, start, pair, 0)
+    for partner in (first, second):
+        window = jnp.maximum(window, swap(window, partner, wide_size, narrow_size))
+    other = swap(window, lambda w, n: (w, n ^ 1), wide_size, narrow_size)
+    values = window_max(values, start, window)
+    return window_max(values, jnp.where(chosen, row_start, column_start), other)
 
 
 def on_device(wide_size, narrow_size, tiles, tile_rows, tile_cols, tile_counts):
@@ -157,27 +198,26 @@
     )(tile_counts, *kept((tile_rows, tile_cols, tiles), pltpu.HBM))
     places = (*kept((rows, cols), pltpu.SMEM), tile_counts)
     held = kept([held], pltpu.VMEM)
-    peaks = []
-    for iteration in range(ITERS):
-        if iteration:
-            part = pl.pallas_call(
-                next_kernel,
-                out_shape=pltpu.VMEM((blocks, tile), jnp.float32),
-                in_specs=[SMEM] * 3 + [VMEM] * (1 + len(peaks)),
-                out_specs=VMEM,
-                scratch_shapes=[pltpu.VMEM((blocks, tile), jnp.float32)],
-                compiler_params=PARAMS,
-                name="next_peaks",
-            )(*places, *held, *peaks)
-        full = max_over_devices(part, wide_size, narrow_size)
-        peaks += kept([full], pltpu.VMEM)
+    for iteration in range(1, ITERS):
+        reduce = max_over_users if narrow_size == 4 else max_over_devices
+        full = reduce(part, wide_size, narrow_size)
+        part = pl.pallas_call(
+            next_kernel,
+            out_shape=pltpu.VMEM((blocks, tile), jnp.float32),
+            in_specs=[SMEM] * 3 + [VMEM] * 2,
+            out_specs=VMEM,
+            scratch_shapes=[pltpu.VMEM((blocks, tile), jnp.float32)],
+            compiler_params=PARAMS,
+            name="next_peaks",
+        )(*places, *held, *kept([full], pltpu.VMEM))
+    full = max_over_devices(part, wide_size, narrow_size)
     return pl.pallas_call(
         functools.partial(last_kernel, ROWB),
         out_shape=(
             jax.ShapeDtypeStruct(tiles.shape, jnp.float32),
             jax.ShapeDtypeStruct((ROWB, tile), jnp.float32),
         ),
-        in_specs=[SMEM] * 3 + [VMEM] * (1 + len(peaks)),
+        in_specs=[SMEM] * 3 + [VMEM] * 2,
         out_specs=(HBM, HBM),
         scratch_shapes=[
             pltpu.VMEM((blocks, tile), jnp.float32),
@@ -187,7 +227,7 @@
         ],
         compiler_params=PARAMS,
         name="scaled_tiles",
-    )(*places, *held, *peaks)
+    )(*places, *held, *kept([full], pltpu.VMEM))
 
 
 def solution(mesh):

time: 38 us -> 34.9 us (0.918)
  starting transfers between devices: 17.9 us -> 15.3 us
  waiting for transfers between devices: 15 us -> 14.5 us
    ppermute x10, starting transfers between devices: 17.9 us -> 15.3 us  [swap(): return lax.ppermute(values, BOTH, pairs)]
    ppermute x10, waiting for transfers between devices: 15 us -> 14.5 us  [swap(): return lax.ppermute(values, BOTH, pairs)]
where the time goes in v4:
time: 34.9 us; the launch traced here: 34.7 us
  starting transfers between devices  15.3 us (44%)
  waiting for transfers between devices  14.5 us (42%)
  Pallas kernels  3.57 us (10%)
  between operations  1.31 us (4%)
    ppermute x10, starting transfers between devices, swap(): return lax.ppermute(values, BOTH, pairs)  15.3 us
    ppermute x10, waiting for transfers between devices, swap(): return lax.ppermute(values, BOTH, pairs)  14.5 us
    pallas_call x1, Pallas kernels, on_device(): pl.pallas_call(first_kernel, out_shape=(pltpu.SMEM(tile_rows.shape, jnp.i...  1.73 us
    pallas_call x1, Pallas kernels, on_device(): pl.pallas_call(functools.partial(last_kernel, ROWB), out_shape=(jax.Shape...  1.31 us
  transfers between devices with their start and end apart: 10, of which 10 were waited for; matrix products, arithmetic and copies ran while one was open for 0% of the time, Pallas kernels for 0%

profile of v4, /device:TPU:0, one launch (start us, length us, event | category | flops | bytes accessed | tf_op | source)
XLA Modules:
  0.0 34.7 jit_solution(8656236888711447884)
XLA Ops:
  1.3 1.7 %first_peaks.1 = (s32[1,6]{1,0:T(1,128)S(4)}, s32[1,6]{1,0:T(1,128)S(4)}, f32[6,256,256]{2,1,0:T(8,128)S(1)}, f32[32,256]{1,0:T(8,128)S(1)}) custom-call(s32[1,1]{1,0:T(1,128)S(6)} %copy.8.count_ref, s32[1,6]{1,0:T(1,128)} %rows_in.1, s32[1,6]{1,0:T(1,128)} %cols_in.1, f32[1,6,256,256]{3,2,1,0:T(8,128)} %tiles_ref.1), custom_call_target="tpu_custom_call" | custom-call | tf_op jit(solution)/shard_map/first_peaks/pallas_call | solution.py:185
  3.0 0.5 %collective-permute-start = (f32[32,256]{1,0:T(8,128)S(1)}, f32[32,256]{1,0:T(8,128)S(1)}, u32[]{:S(2)}, u32[]{:S(2)}) collective-permute-start(f32[32,256]{1,0:T(8,128)S(1)} %get-tuple-element.9), channel_id=1, source_target_pairs={{0,1},{1,0},{2,3},{3,2},{4,5},{5,4},{6,7},{7,6},{8,9},{9,8},{10,11... | collective-permute-start | bytes 98312 | tf_op jit(solution)/shard_map/ppermute | solution.py:127
  3.5 0.9 %collective-permute-done = f32[32,256]{1,0:T(8,128)S(1)} collective-permute-done((f32[32,256]{1,0:T(8,128)S(1)}, f32[32,256]{1,0:T(8,128)S(1)}, u32[]{:S(2)}, u32[]{:S(2)}) %collective-permute-start) | collective-permute-done | bytes 32800 | tf_op jit(solution)/shard_map/ppermute | solution.py:127
  4.4 2.6 %collective-permute-start.1 = (f32[32,256]{1,0:T(8,128)S(1)}, f32[32,256]{1,0:T(8,128)S(1)}, u32[]{:S(2)}, u32[]{:S(2)}) collective-permute-start(f32[32,256]{1,0:T(8,128)S(1)} %max.33), channel_id=1, source_target_pairs={{0,5},{1,4},{2,7},{3,6},{4,1},{5,0},{6,3},{7,2},{8,13},{9,12},{10,... | collective-permute-start | bytes 98312 | tf_op jit(solution)/shard_map/ppermute | solution.py:127
  7.0 1.6 %collective-permute-done.1 = f32[32,256]{1,0:T(8,128)S(1)} collective-permute-done((f32[32,256]{1,0:T(8,128)S(1)}, f32[32,256]{1,0:T(8,128)S(1)}, u32[]{:S(2)}, u32[]{:S(2)}) %collective-permute-start.1) | collective-permute-done | bytes 32800 | tf_op jit(solution)/shard_map/ppermute | solution.py:127
  8.6 1.9 %collective-permute-start.2 = (f32[16,256]{1,0:T(8,128)S(1)}, f32[16,256]{1,0:T(8,128)S(1)}, u32[]{:S(2)}, u32[]{:S(2)}) collective-permute-start(f32[16,256]{1,0:T(8,128)S(1)} %constant_dynamic-slice_fusion), channel_id=1, source_target_pairs={{0,9},{1,2},{2,1},{3,10},{4,13},{5,6},{6,5},{7,14},{8,11},{9,0},{1... | collective-permute-start | bytes 49160 | tf_op jit(solution)/shard_map/ppermute | solution.py:127
  10.5 1.4 %collective-permute-done.2 = f32[16,256]{1,0:T(8,128)S(1)} collective-permute-done((f32[16,256]{1,0:T(8,128)S(1)}, f32[16,256]{1,0:T(8,128)S(1)}, u32[]{:S(2)}, u32[]{:S(2)}) %collective-permute-start.2) | collective-permute-done | bytes 16416 | tf_op jit(solution)/shard_map/ppermute | solution.py:127
  12.0 2.7 %collective-permute-start.3 = (f32[16,256]{1,0:T(8,128)S(1)}, f32[16,256]{1,0:T(8,128)S(1)}, u32[]{:S(2)}, u32[]{:S(2)}) collective-permute-start(f32[16,256]{1,0:T(8,128)S(1)} %fusion), channel_id=1, source_target_pairs={{0,17},{1,8},{2,11},{3,18},{4,21},{5,12},{6,15},{7,22},{8,1},{9,24... | collective-permute-start | bytes 49160 | tf_op jit(solution)/shard_map/ppermute | solution.py:127
  14.7 1.4 %collective-permute-done.3 = f32[16,256]{1,0:T(8,128)S(1)} collective-permute-done((f32[16,256]{1,0:T(8,128)S(1)}, f32[16,256]{1,0:T(8,128)S(1)}, u32[]{:S(2)}, u32[]{:S(2)}) %collective-permute-start.3) | collective-permute-done | bytes 16416 | tf_op jit(solution)/shard_map/ppermute | solution.py:127
  16.1 0.0 collective-permute-start.4
  16.2 1.2 %collective-permute-done.4 = f32[16,256]{1,0:T(8,128)S(1)} collective-permute-done((f32[16,256]{1,0:T(8,128)S(1)}, f32[16,256]{1,0:T(8,128)S(1)}, u32[]{:S(2)}, u32[]{:S(2)}) %collective-permute-start.4) | collective-permute-done | bytes 16416 | tf_op jit(solution)/shard_map/ppermute | solution.py:127
  17.3 0.5 %next_peaks.1 = f32[32,256]{1,0:T(8,128)S(1)} custom-call(s32[1,6]{1,0:T(1,128)S(4)} %get-tuple-element.6.rows_ref, s32[1,6]{1,0:T(1,128)S(4)} %get-tuple-element.7.cols_ref, s32[1,1]{1,0:T(1,128)S(6)} %copy.8.count_ref, f32[6,256,256]{2,1,0:T(8,128)S(1)} %get-tuple-element.8.held_ref, f32[32,256]{1,0:T(8,128)S(1)} %maximum_dynamic-update-slice_fusion.old_ref), custom_call_target="tpu_custom_call" | custom-call | tf_op jit(solution)/shard_map/next_peaks/pallas_call | solution.py:204
  17.9 0.2 collective-permute-start.5
  18.1 1.0 %collective-permute-done.5 = f32[32,256]{1,0:T(8,128)S(1)} collective-permute-done((f32[32,256]{1,0:T(8,128)S(1)}, f32[32,256]{1,0:T(8,128)S(1)}, u32[]{:S(2)}, u32[]{:S(2)}) %collective-permute-start.5) | collective-permute-done | bytes 32800 | tf_op jit(solution)/shard_map/ppermute | solution.py:127
  19.1 1.6 %collective-permute-start.6 = (f32[32,256]{1,0:T(8,128)S(1)}, f32[32,256]{1,0:T(8,128)S(1)}, u32[]{:S(2)}, u32[]{:S(2)}) collective-permute-start(f32[32,256]{1,0:T(8,128)S(1)} %max.39), channel_id=1, source_target_pairs={{0,5},{1,4},{2,7},{3,6},{4,1},{5,0},{6,3},{7,2},{8,13},{9,12},{10,... | collective-permute-start | bytes 98312 | tf_op jit(solution)/shard_map/ppermute | solution.py:127
  20.7 1.8 %collective-permute-done.6 = f32[32,256]{1,0:T(8,128)S(1)} collective-permute-done((f32[32,256]{1,0:T(8,128)S(1)}, f32[32,256]{1,0:T(8,128)S(1)}, u32[]{:S(2)}, u32[]{:S(2)}) %collective-permute-start.6) | collective-permute-done | bytes 32800 | tf_op jit(solution)/shard_map/ppermute | solution.py:127
  22.5 1.6 %collective-permute-start.7 = (f32[32,256]{1,0:T(8,128)S(1)}, f32[32,256]{1,0:T(8,128)S(1)}, u32[]{:S(2)}, u32[]{:S(2)}) collective-permute-start(f32[32,256]{1,0:T(8,128)S(1)} %max.40), channel_id=1, source_target_pairs={{0,9},{1,8},{2,11},{3,10},{4,13},{5,12},{6,15},{7,14},{8,1},{9,0},... | collective-permute-start | bytes 98312 | tf_op jit(solution)/shard_map/ppermute | solution.py:127
  24.1 1.7 %collective-permute-done.7 = f32[32,256]{1,0:T(8,128)S(1)} collective-permute-done((f32[32,256]{1,0:T(8,128)S(1)}, f32[32,256]{1,0:T(8,128)S(1)}, u32[]{:S(2)}, u32[]{:S(2)}) %collective-permute-start.7) | collective-permute-done | bytes 32800 | tf_op jit(solution)/shard_map/ppermute | solution.py:127
  25.8 2.6 %collective-permute-start.8 = (f32[32,256]{1,0:T(8,128)S(1)}, f32[32,256]{1,0:T(8,128)S(1)}, u32[]{:S(2)}, u32[]{:S(2)}) collective-permute-start(f32[32,256]{1,0:T(8,128)S(1)} %max.41), channel_id=1, source_target_pairs={{0,17},{1,16},{2,19},{3,18},{4,21},{5,20},{6,23},{7,22},{8,25},{9,... | collective-permute-start | bytes 98312 | tf_op jit(solution)/shard_map/ppermute | solution.py:127
  28.5 1.6 %collective-permute-done.8 = f32[32,256]{1,0:T(8,128)S(1)} collective-permute-done((f32[32,256]{1,0:T(8,128)S(1)}, f32[32,256]{1,0:T(8,128)S(1)}, u32[]{:S(2)}, u32[]{:S(2)}) %collective-permute-start.8) | collective-permute-done | bytes 32800 | tf_op jit(solution)/shard_map/ppermute | solution.py:127
  30.1 1.5 %collective-permute-start.9 = (f32[32,256]{1,0:T(8,128)S(1)}, f32[32,256]{1,0:T(8,128)S(1)}, u32[]{:S(2)}, u32[]{:S(2)}) collective-permute-start(f32[32,256]{1,0:T(8,128)S(1)} %max.42), channel_id=1, source_target_pairs={{0,3},{1,2},{2,1},{3,0},{4,7},{5,6},{6,5},{7,4},{8,11},{9,10},{10,... | collective-permute-start | bytes 98312 | tf_op jit(solution)/shard_map/ppermute | solution.py:127
  31.6 1.8 %collective-permute-done.9 = f32[32,256]{1,0:T(8,128)S(1)} collective-permute-done((f32[32,256]{1,0:T(8,128)S(1)}, f32[32,256]{1,0:T(8,128)S(1)}, u32[]{:S(2)}, u32[]{:S(2)}) %collective-permute-start.9) | collective-permute-done | bytes 32800 | tf_op jit(solution)/shard_map/ppermute | solution.py:127
  33.4 1.3 %scaled_tiles.1 = (f32[1,6,256,256]{3,2,1,0:T(8,128)}, f32[4,256]{1,0:T(4,128)}) custom-call(s32[1,6]{1,0:T(1,128)S(4)} %get-tuple-element.6.rows_ref, s32[1,6]{1,0:T(1,128)S(4)} %get-tuple-element.7.cols_ref, s32[1,1]{1,0:T(1,128)S(6)} %copy.8.count_ref, f32[6,256,256]{2,1,0:T(8,128)S(1)} %get-tuple-element.8.held_ref, f32[32,256]{1,0:T(8,128)S(1)} %max.43.old_ref), custom_call_target="tpu_custom_call" | custom-call | tf_op jit(solution)/shard_map/scaled_tiles/pallas_call | solution.py:214
  (11 shorter events, 0.1 us)
Async XLA Ops:
  3.0 1.4 %collective-permute-start = (f32[32,256]{1,0:T(8,128)S(1)}, f32[32,256]{1,0:T(8,128)S(1)}, u32[]{:S(2)}, u32[]{:S(2)}) collective-permute-start(f32[32,256]{1,0:T(8,128)S(1)} %get-tuple-element.9), channel_id=1, source_target_pairs={{0,1},{1,0},{2,3},{3,2},{4,5},{5,4},{6,7},{7,6},{8,9},{9,8},{10,11... | collective-permute-start | bytes 98312 | tf_op jit(solution)/shard_map/ppermute | solution.py:127
  4.4 4.2 %collective-permute-start.1 = (f32[32,256]{1,0:T(8,128)S(1)}, f32[32,256]{1,0:T(8,128)S(1)}, u32[]{:S(2)}, u32[]{:S(2)}) collective-permute-start(f32[32,256]{1,0:T(8,128)S(1)} %max.33), channel_id=1, source_target_pairs={{0,5},{1,4},{2,7},{3,6},{4,1},{5,0},{6,3},{7,2},{8,13},{9,12},{10,... | collective-permute-start | bytes 98312 | tf_op jit(solution)/shard_map/ppermute | solution.py:127
  8.6 3.3 %collective-permute-start.2 = (f32[16,256]{1,0:T(8,128)S(1)}, f32[16,256]{1,0:T(8,128)S(1)}, u32[]{:S(2)}, u32[]{:S(2)}) collective-permute-start(f32[16,256]{1,0:T(8,128)S(1)} %constant_dynamic-slice_fusion), channel_id=1, source_target_pairs={{0,9},{1,2},{2,1},{3,10},{4,13},{5,6},{6,5},{7,14},{8,11},{9,0},{1... | collective-permute-start | bytes 49160 | tf_op jit(solution)/shard_map/ppermute | solution.py:127
  12.0 4.2 %collective-permute-start.3 = (f32[16,256]{1,0:T(8,128)S(1)}, f32[16,256]{1,0:T(8,128)S(1)}, u32[]{:S(2)}, u32[]{:S(2)}) collective-permute-start(f32[16,256]{1,0:T(8,128)S(1)} %fusion), channel_id=1, source_target_pairs={{0,17},{1,8},{2,11},{3,18},{4,21},{5,12},{6,15},{7,22},{8,1},{9,24... | collective-permute-start | bytes 49160 | tf_op jit(solution)/shard_map/ppermute | solution.py:127
  16.1 1.2 %collective-permute-start.4 = (f32[16,256]{1,0:T(8,128)S(1)}, f32[16,256]{1,0:T(8,128)S(1)}, u32[]{:S(2)}, u32[]{:S(2)}) collective-permute-start(f32[16,256]{1,0:T(8,128)S(1)} %get-tuple-element.11), channel_id=1, source_target_pairs={{0,1},{1,0},{2,3},{3,2},{4,5},{5,4},{6,7},{7,6},{8,9},{9,8},{10,11... | collective-permute-start | bytes 49160 | tf_op jit(solution)/shard_map/ppermute | solution.py:127
  17.9 1.3 %collective-permute-start.5 = (f32[32,256]{1,0:T(8,128)S(1)}, f32[32,256]{1,0:T(8,128)S(1)}, u32[]{:S(2)}, u32[]{:S(2)}) collective-permute-start(f32[32,256]{1,0:T(8,128)S(1)} %next_peaks.1), channel_id=1, source_target_pairs={{0,1},{1,0},{2,3},{3,2},{4,5},{5,4},{6,7},{7,6},{8,9},{9,8},{10,11... | collective-permute-start | bytes 98312 | tf_op jit(solution)/shard_map/ppermute | solution.py:127
  19.1 3.3 %collective-permute-start.6 = (f32[32,256]{1,0:T(8,128)S(1)}, f32[32,256]{1,0:T(8,128)S(1)}, u32[]{:S(2)}, u32[]{:S(2)}) collective-permute-start(f32[32,256]{1,0:T(8,128)S(1)} %max.39), channel_id=1, source_target_pairs={{0,5},{1,4},{2,7},{3,6},{4,1},{5,0},{6,3},{7,2},{8,13},{9,12},{10,... | collective-permute-start | bytes 98312 | tf_op jit(solution)/shard_map/ppermute | solution.py:127
  22.5 3.3 %collective-permute-start.7 = (f32[32,256]{1,0:T(8,128)S(1)}, f32[32,256]{1,0:T(8,128)S(1)}, u32[]{:S(2)}, u32[]{:S(2)}) collective-permute-start(f32[32,256]{1,0:T(8,128)S(1)} %max.40), channel_id=1, source_target_pairs={{0,9},{1,8},{2,11},{3,10},{4,13},{5,12},{6,15},{7,14},{8,1},{9,0},... | collective-permute-start | bytes 98312 | tf_op jit(solution)/shard_map/ppermute | solution.py:127
  25.8 4.2 %collective-permute-start.8 = (f32[32,256]{1,0:T(8,128)S(1)}, f32[32,256]{1,0:T(8,128)S(1)}, u32[]{:S(2)}, u32[]{:S(2)}) collective-permute-start(f32[32,256]{1,0:T(8,128)S(1)} %max.41), channel_id=1, source_target_pairs={{0,17},{1,16},{2,19},{3,18},{4,21},{5,20},{6,23},{7,22},{8,25},{9,... | collective-permute-start | bytes 98312 | tf_op jit(solution)/shard_map/ppermute | solution.py:127
  30.1 3.3 %collective-permute-start.9 = (f32[32,256]{1,0:T(8,128)S(1)}, f32[32,256]{1,0:T(8,128)S(1)}, u32[]{:S(2)}, u32[]{:S(2)}) collective-permute-start(f32[32,256]{1,0:T(8,128)S(1)} %max.42), channel_id=1, source_target_pairs={{0,3},{1,2},{2,1},{3,0},{4,7},{5,6},{6,5},{7,4},{8,11},{9,10},{10,... | collective-permute-start | bytes 98312 | tf_op jit(solution)/shard_map/ppermute | solution.py:127

commit v5 on v4

--- a/solution.py
+++ b/solution.py
@@ -150,15 +150,36 @@
     return lax.dynamic_update_slice_in_dim(values, jnp.maximum(old, window), start, 0)
 
 
+def swap_in_chip(values, wide_size, narrow_size):
+    columns = values.shape[0] // narrow_size
+    row_start = lax.axis_index("wide") * ROWB
+    n = lax.axis_index("narrow")
+    sent = jnp.concatenate(
+        [
+            lax.dynamic_slice_in_dim(values, n * columns, columns, 0),
+            lax.dynamic_slice_in_dim(values, row_start, ROWB, 0),
+        ]
+    )
+    other = swap(sent, lambda w, n: (w, n ^ 1), wide_size, narrow_size)
+    values = window_max(values, (n ^ 1) * columns, other[:columns])
+    return window_max(values, row_start, other[columns:])
+
+
+def windows(values, wide_size, narrow_size):
+    size = 2 * values.shape[0] // narrow_size
+    columns = (lax.axis_index("narrow") >> 1) * size
+    rows = lax.axis_index("wide") // (2 * wide_size // narrow_size) * size
+    return columns, rows, size
+
+
 def max_over_users(values, wide_size, narrow_size):
     share = wide_size // narrow_size
-    for wide_bit in (0, *bits(1, share)):
-        other = swap(values, lambda w, n: (w ^ wide_bit, n ^ 1), wide_size, narrow_size)
-        values = jnp.maximum(values, other)
 
     def along_columns(w, n):
-        group = w // share
-        return (group ^ group >> 1 ^ n >> 1 ^ n) & 1 == 0
+        lane = n ^ n >> 1
+        for bit in bits(1, wide_size):
+            lane = lane ^ w // bit
+        return lane & 1 == 0
 
     def first(w, n):
         return (w ^ share, n ^ 1) if along_columns(w, n) else (w, n ^ 3)
@@ -166,22 +187,41 @@
     def second(w, n):
         return (w ^ 2 * share if along_columns(w, n) else w ^ share, n ^ 1)
 
-    pair = 2 * values.shape[0] // narrow_size
-    w, n = lax.axis_index("wide"), lax.axis_index("narrow")
-    column_start, row_start = (n >> 1) * pair, (w // (2 * share)) * pair
-    chosen = along_columns(w, n)
-    start = jnp.where(chosen, column_start, row_start)
-    window = lax.dynamic_slice_in_dim(values, start, pair, 0)
+    values = swap_in_chip(values, wide_size, narrow_size)
+    columns, rows, size = windows(values, wide_size, narrow_size)
+    chosen = along_columns(lax.axis_index("wide"), lax.axis_index("narrow"))
+    start = jnp.where(chosen, columns, rows)
+    window = lax.dynamic_slice_in_dim(values, start, size, 0)
+    for bit in bits(1, share):
+        other = swap(window, lambda w, n: (w ^ bit, n ^ 1), wide_size, narrow_size)
+        window = jnp.maximum(window, other)
     for partner in (first, second):
         window = jnp.maximum(window, swap(window, partner, wide_size, narrow_size))
     other = swap(window, lambda w, n: (w, n ^ 1), wide_size, narrow_size)
     values = window_max(values, start, window)
-    return window_max(values, jnp.where(chosen, row_start, column_start), other)
+    return window_max(values, jnp.where(chosen, rows, columns), other)
+
+
+def max_of_rows_too(values, wide_size, narrow_size):
+    values = swap_in_chip(values, wide_size, narrow_size)
+    for bit in bits(1, wide_size // 2):
+        other = swap(values, lambda w, n: (w ^ bit, n ^ 1), wide_size, narrow_size)
+        values = jnp.maximum(values, other)
+    columns, rows, size = windows(values, wide_size, narrow_size)
+    for start, partner in (
+        (columns, lambda w, n: (w ^ wide_size // 2, n ^ 1)),
+        (rows, lambda w, n: (w, n ^ 3)),
+    ):
+        window = lax.dynamic_slice_in_dim(values, start, size, 0)
+        other = swap(window, partner, wide_size, narrow_size)
+        values = window_max(values, start, other)
+    return values
 
 
 def on_device(wide_size, narrow_size, tiles, tile_rows, tile_cols, tile_counts):
     slots, tile = tiles.shape[1], tiles.shape[2]
     blocks = ROWB * wide_size
+    four = narrow_size == 4
     rows, cols, held, part = pl.pallas_call(
         first_kernel,
         out_shape=(
@@ -199,8 +239,7 @@
     places = (*kept((rows, cols), pltpu.SMEM), tile_counts)
     held = kept([held], pltpu.VMEM)
     for iteration in range(1, ITERS):
-        reduce = max_over_users if narrow_size == 4 else max_over_devices
-        full = reduce(part, wide_size, narrow_size)
+        full = (max_over_users if four else max_over_devices)(part, wide_size, narrow_size)
         part = pl.pallas_call(
             next_kernel,
             out_shape=pltpu.VMEM((blocks, tile), jnp.float32),
@@ -210,7 +249,7 @@
             compiler_params=PARAMS,
             name="next_peaks",
         )(*places, *held, *kept([full], pltpu.VMEM))
-    full = max_over_devices(part, wide_size, narrow_size)
+    full = (max_of_rows_too if four else max_over_devices)(part, wide_size, narrow_size)
     return pl.pallas_call(
         functools.partial(last_kernel, ROWB),
         out_shape=(

time: 34.9 us -> 34.7 us (level)
  waiting for transfers between devices: 14.5 us -> 13.9 us
    ppermute x10, waiting for transfers between devices: 14.5 us -> 13.9 us  [swap(): return lax.ppermute(values, BOTH, pairs)]
where the time goes in v5:
time: 34.7 us; the launch traced here: 34.5 us
  starting transfers between devices  15.5 us (45%)
  waiting for transfers between devices  13.9 us (40%)
  Pallas kernels  3.57 us (10%)
  between operations  1.37 us (4%)
    ppermute x10, starting transfers between devices, swap(): return lax.ppermute(values, BOTH, pairs)  15.5 us
    ppermute x10, waiting for transfers between devices, swap(): return lax.ppermute(values, BOTH, pairs)  13.9 us
    pallas_call x1, Pallas kernels, on_device(): pl.pallas_call(first_kernel, out_shape=(pltpu.SMEM(tile_rows.shape, jnp.i...  1.73 us
    pallas_call x1, Pallas kernels, on_device(): pl.pallas_call(functools.partial(last_kernel, ROWB), out_shape=(jax.Shape...  1.31 us
  transfers between devices with their start and end apart: 10, of which 10 were waited for; matrix products, arithmetic and copies ran while one was open for 0% of the time, Pallas kernels for 0%

profile of v5, /device:TPU:0, one launch (start us, length us, event | category | flops | bytes accessed | tf_op | source)
XLA Modules:
  0.0 34.5 jit_solution(4069695482761730258)
XLA Ops:
  1.3 1.7 %first_peaks.1 = (s32[1,6]{1,0:T(1,128)S(4)}, s32[1,6]{1,0:T(1,128)S(4)}, f32[6,256,256]{2,1,0:T(8,128)S(1)}, f32[32,256]{1,0:T(8,128)S(1)}) custom-call(s32[1,1]{1,0:T(1,128)S(6)} %copy.14.count_ref, s32[1,6]{1,0:T(1,128)} %rows_in.1, s32[1,6]{1,0:T(1,128)} %cols_in.1, f32[1,6,256,256]{3,2,1,0:T(8,128)} %tiles_ref.1), custom_call_target="tpu_custom_call" | custom-call | tf_op jit(solution)/shard_map/first_peaks/pallas_call | solution.py:225
  3.1 0.5 %collective-permute-start = (f32[12,256]{1,0:T(8,128)S(1)}, f32[12,256]{1,0:T(8,128)S(1)}, u32[]{:S(2)}, u32[]{:S(2)}) collective-permute-start(f32[12,256]{1,0:T(8,128)S(1)} %pad_maximum_fusion), channel_id=1, source_target_pairs={{0,1},{1,0},{2,3},{3,2},{4,5},{5,4},{6,7},{7,6},{8,9},{9,8},{10,11... | collective-permute-start | bytes 36872 | tf_op jit(solution)/shard_map/ppermute | solution.py:127
  3.6 0.8 %collective-permute-done = f32[12,256]{1,0:T(8,128)S(1)} collective-permute-done((f32[12,256]{1,0:T(8,128)S(1)}, f32[12,256]{1,0:T(8,128)S(1)}, u32[]{:S(2)}, u32[]{:S(2)}) %collective-permute-start) | collective-permute-done | bytes 12320 | tf_op jit(solution)/shard_map/ppermute | solution.py:127
  4.5 2.7 %collective-permute-start.1 = (f32[16,256]{1,0:T(8,128)S(1)}, f32[16,256]{1,0:T(8,128)S(1)}, u32[]{:S(2)}, u32[]{:S(2)}) collective-permute-start(f32[16,256]{1,0:T(8,128)S(1)} %constant_dynamic-slice_fusion.5), channel_id=1, source_target_pairs={{0,5},{1,4},{2,7},{3,6},{4,1},{5,0},{6,3},{7,2},{8,13},{9,12},{10,... | collective-permute-start | bytes 49160 | tf_op jit(solution)/shard_map/ppermute | solution.py:127
  7.2 1.4 %collective-permute-done.1 = f32[16,256]{1,0:T(8,128)S(1)} collective-permute-done((f32[16,256]{1,0:T(8,128)S(1)}, f32[16,256]{1,0:T(8,128)S(1)}, u32[]{:S(2)}, u32[]{:S(2)}) %collective-permute-start.1) | collective-permute-done | bytes 16416 | tf_op jit(solution)/shard_map/ppermute | solution.py:127
  8.6 1.8 %collective-permute-start.2 = (f32[16,256]{1,0:T(8,128)S(1)}, f32[16,256]{1,0:T(8,128)S(1)}, u32[]{:S(2)}, u32[]{:S(2)}) collective-permute-start(f32[16,256]{1,0:T(8,128)S(1)} %fusion.4), channel_id=1, source_target_pairs={{0,9},{1,2},{2,1},{3,10},{4,7},{5,12},{6,15},{7,4},{8,11},{9,0},{1... | collective-permute-start | bytes 49160 | tf_op jit(solution)/shard_map/ppermute | solution.py:127
  10.4 1.4 %collective-permute-done.2 = f32[16,256]{1,0:T(8,128)S(1)} collective-permute-done((f32[16,256]{1,0:T(8,128)S(1)}, f32[16,256]{1,0:T(8,128)S(1)}, u32[]{:S(2)}, u32[]{:S(2)}) %collective-permute-start.2) | collective-permute-done | bytes 16416 | tf_op jit(solution)/shard_map/ppermute | solution.py:127
  11.8 2.7 %collective-permute-start.3 = (f32[16,256]{1,0:T(8,128)S(1)}, f32[16,256]{1,0:T(8,128)S(1)}, u32[]{:S(2)}, u32[]{:S(2)}) collective-permute-start(f32[16,256]{1,0:T(8,128)S(1)} %max.42), channel_id=1, source_target_pairs={{0,17},{1,8},{2,11},{3,18},{4,13},{5,20},{6,23},{7,14},{8,1},{9,24... | collective-permute-start | bytes 49160 | tf_op jit(solution)/shard_map/ppermute | solution.py:127
  14.6 1.4 %collective-permute-done.3 = f32[16,256]{1,0:T(8,128)S(1)} collective-permute-done((f32[16,256]{1,0:T(8,128)S(1)}, f32[16,256]{1,0:T(8,128)S(1)}, u32[]{:S(2)}, u32[]{:S(2)}) %collective-permute-start.3) | collective-permute-done | bytes 16416 | tf_op jit(solution)/shard_map/ppermute | solution.py:127
  16.0 0.0 collective-permute-start.4
  16.0 1.2 %collective-permute-done.4 = f32[16,256]{1,0:T(8,128)S(1)} collective-permute-done((f32[16,256]{1,0:T(8,128)S(1)}, f32[16,256]{1,0:T(8,128)S(1)}, u32[]{:S(2)}, u32[]{:S(2)}) %collective-permute-start.4) | collective-permute-done | bytes 16416 | tf_op jit(solution)/shard_map/ppermute | solution.py:127
  17.2 0.5 %next_peaks.1 = f32[32,256]{1,0:T(8,128)S(1)} custom-call(s32[1,6]{1,0:T(1,128)S(4)} %get-tuple-element.6.rows_ref, s32[1,6]{1,0:T(1,128)S(4)} %get-tuple-element.7.cols_ref, s32[1,1]{1,0:T(1,128)S(6)} %copy.14.count_ref, f32[6,256,256]{2,1,0:T(8,128)S(1)} %get-tuple-element.8.held_ref, f32[32,256]{1,0:T(8,128)S(1)} %maximum_dynamic-update-slice_fusion.2.old_ref), custom_call_target="tpu_custom_call" | custom-call | tf_op jit(solution)/shard_map/next_peaks/pallas_call | solution.py:243
  17.8 0.2 collective-permute-start.5
  18.0 1.0 %collective-permute-done.5 = f32[12,256]{1,0:T(8,128)S(1)} collective-permute-done((f32[12,256]{1,0:T(8,128)S(1)}, f32[12,256]{1,0:T(8,128)S(1)}, u32[]{:S(2)}, u32[]{:S(2)}) %collective-permute-start.5) | collective-permute-done | bytes 12320 | tf_op jit(solution)/shard_map/ppermute | solution.py:127
  19.1 1.6 %collective-permute-start.6 = (f32[32,256]{1,0:T(8,128)S(1)}, f32[32,256]{1,0:T(8,128)S(1)}, u32[]{:S(2)}, u32[]{:S(2)}) collective-permute-start(f32[32,256]{1,0:T(8,128)S(1)} %constant_dynamic-update-slice_fusion), channel_id=1, source_target_pairs={{0,5},{1,4},{2,7},{3,6},{4,1},{5,0},{6,3},{7,2},{8,13},{9,12},{10,... | collective-permute-start | bytes 98312 | tf_op jit(solution)/shard_map/ppermute | solution.py:127
  20.7 1.8 %collective-permute-done.6 = f32[32,256]{1,0:T(8,128)S(1)} collective-permute-done((f32[32,256]{1,0:T(8,128)S(1)}, f32[32,256]{1,0:T(8,128)S(1)}, u32[]{:S(2)}, u32[]{:S(2)}) %collective-permute-start.6) | collective-permute-done | bytes 32800 | tf_op jit(solution)/shard_map/ppermute | solution.py:127
  22.5 1.6 %collective-permute-start.7 = (f32[32,256]{1,0:T(8,128)S(1)}, f32[32,256]{1,0:T(8,128)S(1)}, u32[]{:S(2)}, u32[]{:S(2)}) collective-permute-start(f32[32,256]{1,0:T(8,128)S(1)} %max.48), channel_id=1, source_target_pairs={{0,9},{1,8},{2,11},{3,10},{4,13},{5,12},{6,15},{7,14},{8,1},{9,0},... | collective-permute-start | bytes 98312 | tf_op jit(solution)/shard_map/ppermute | solution.py:127
  24.1 1.7 %collective-permute-done.7 = f32[32,256]{1,0:T(8,128)S(1)} collective-permute-done((f32[32,256]{1,0:T(8,128)S(1)}, f32[32,256]{1,0:T(8,128)S(1)}, u32[]{:S(2)}, u32[]{:S(2)}) %collective-permute-start.7) | collective-permute-done | bytes 32800 | tf_op jit(solution)/shard_map/ppermute | solution.py:127
  25.8 2.7 %collective-permute-start.8 = (f32[16,256]{1,0:T(8,128)S(1)}, f32[16,256]{1,0:T(8,128)S(1)}, u32[]{:S(2)}, u32[]{:S(2)}) collective-permute-start(f32[16,256]{1,0:T(8,128)S(1)} %constant_dynamic-slice_fusion), channel_id=1, source_target_pairs={{0,17},{1,16},{2,19},{3,18},{4,21},{5,20},{6,23},{7,22},{8,25},{9,... | collective-permute-start | bytes 49160 | tf_op jit(solution)/shard_map/ppermute | solution.py:127
  28.5 1.4 %collective-permute-done.8 = f32[16,256]{1,0:T(8,128)S(1)} collective-permute-done((f32[16,256]{1,0:T(8,128)S(1)}, f32[16,256]{1,0:T(8,128)S(1)}, u32[]{:S(2)}, u32[]{:S(2)}) %collective-permute-start.8) | collective-permute-done | bytes 16416 | tf_op jit(solution)/shard_map/ppermute | solution.py:127
  30.0 1.6 %collective-permute-start.9 = (f32[16,256]{1,0:T(8,128)S(1)}, f32[16,256]{1,0:T(8,128)S(1)}, u32[]{:S(2)}, u32[]{:S(2)}) collective-permute-start(f32[16,256]{1,0:T(8,128)S(1)} %constant_dynamic-slice_fusion.4), channel_id=1, source_target_pairs={{0,3},{1,2},{2,1},{3,0},{4,7},{5,6},{6,5},{7,4},{8,11},{9,10},{10,... | collective-permute-start | bytes 49160 | tf_op jit(solution)/shard_map/ppermute | solution.py:127
  31.5 1.6 %collective-permute-done.9 = f32[16,256]{1,0:T(8,128)S(1)} collective-permute-done((f32[16,256]{1,0:T(8,128)S(1)}, f32[16,256]{1,0:T(8,128)S(1)}, u32[]{:S(2)}, u32[]{:S(2)}) %collective-permute-start.9) | collective-permute-done | bytes 16416 | tf_op jit(solution)/shard_map/ppermute | solution.py:127
  33.2 1.3 %scaled_tiles.1 = (f32[1,6,256,256]{3,2,1,0:T(8,128)}, f32[4,256]{1,0:T(4,128)}) custom-call(s32[1,6]{1,0:T(1,128)S(4)} %get-tuple-element.6.rows_ref, s32[1,6]{1,0:T(1,128)S(4)} %get-tuple-element.7.cols_ref, s32[1,1]{1,0:T(1,128)S(6)} %copy.14.count_ref, f32[6,256,256]{2,1,0:T(8,128)S(1)} %get-tuple-element.8.held_ref, ...), custom_call_target="tpu_custom_call" | custom-call | tf_op jit(solution)/shard_map/scaled_tiles/pallas_call | solution.py:253
  (21 shorter events, 0.1 us)
Async XLA Ops:
  3.1 1.4 %collective-permute-start = (f32[12,256]{1,0:T(8,128)S(1)}, f32[12,256]{1,0:T(8,128)S(1)}, u32[]{:S(2)}, u32[]{:S(2)}) collective-permute-start(f32[12,256]{1,0:T(8,128)S(1)} %pad_maximum_fusion), channel_id=1, source_target_pairs={{0,1},{1,0},{2,3},{3,2},{4,5},{5,4},{6,7},{7,6},{8,9},{9,8},{10,11... | collective-permute-start | bytes 36872 | tf_op jit(solution)/shard_map/ppermute | solution.py:127
  4.5 4.1 %collective-permute-start.1 = (f32[16,256]{1,0:T(8,128)S(1)}, f32[16,256]{1,0:T(8,128)S(1)}, u32[]{:S(2)}, u32[]{:S(2)}) collective-permute-start(f32[16,256]{1,0:T(8,128)S(1)} %constant_dynamic-slice_fusion.5), channel_id=1, source_target_pairs={{0,5},{1,4},{2,7},{3,6},{4,1},{5,0},{6,3},{7,2},{8,13},{9,12},{10,... | collective-permute-start | bytes 49160 | tf_op jit(solution)/shard_map/ppermute | solution.py:127
  8.6 3.2 %collective-permute-start.2 = (f32[16,256]{1,0:T(8,128)S(1)}, f32[16,256]{1,0:T(8,128)S(1)}, u32[]{:S(2)}, u32[]{:S(2)}) collective-permute-start(f32[16,256]{1,0:T(8,128)S(1)} %fusion.4), channel_id=1, source_target_pairs={{0,9},{1,2},{2,1},{3,10},{4,7},{5,12},{6,15},{7,4},{8,11},{9,0},{1... | collective-permute-start | bytes 49160 | tf_op jit(solution)/shard_map/ppermute | solution.py:127
  11.8 4.2 %collective-permute-start.3 = (f32[16,256]{1,0:T(8,128)S(1)}, f32[16,256]{1,0:T(8,128)S(1)}, u32[]{:S(2)}, u32[]{:S(2)}) collective-permute-start(f32[16,256]{1,0:T(8,128)S(1)} %max.42), channel_id=1, source_target_pairs={{0,17},{1,8},{2,11},{3,18},{4,13},{5,20},{6,23},{7,14},{8,1},{9,24... | collective-permute-start | bytes 49160 | tf_op jit(solution)/shard_map/ppermute | solution.py:127
  16.0 1.2 %collective-permute-start.4 = (f32[16,256]{1,0:T(8,128)S(1)}, f32[16,256]{1,0:T(8,128)S(1)}, u32[]{:S(2)}, u32[]{:S(2)}) collective-permute-start(f32[16,256]{1,0:T(8,128)S(1)} %get-tuple-element.11), channel_id=1, source_target_pairs={{0,1},{1,0},{2,3},{3,2},{4,5},{5,4},{6,7},{7,6},{8,9},{9,8},{10,11... | collective-permute-start | bytes 49160 | tf_op jit(solution)/shard_map/ppermute | solution.py:127
  17.8 1.2 %collective-permute-start.5 = (f32[12,256]{1,0:T(8,128)S(1)}, f32[12,256]{1,0:T(8,128)S(1)}, u32[]{:S(2)}, u32[]{:S(2)}) collective-permute-start(f32[12,256]{1,0:T(8,128)S(1)} %pad_maximum_fusion.1), channel_id=1, source_target_pairs={{0,1},{1,0},{2,3},{3,2},{4,5},{5,4},{6,7},{7,6},{8,9},{9,8},{10,11... | collective-permute-start | bytes 36872 | tf_op jit(solution)/shard_map/ppermute | solution.py:127
  19.1 3.4 %collective-permute-start.6 = (f32[32,256]{1,0:T(8,128)S(1)}, f32[32,256]{1,0:T(8,128)S(1)}, u32[]{:S(2)}, u32[]{:S(2)}) collective-permute-start(f32[32,256]{1,0:T(8,128)S(1)} %constant_dynamic-update-slice_fusion), channel_id=1, source_target_pairs={{0,5},{1,4},{2,7},{3,6},{4,1},{5,0},{6,3},{7,2},{8,13},{9,12},{10,... | collective-permute-start | bytes 98312 | tf_op jit(solution)/shard_map/ppermute | solution.py:127
  22.5 3.3 %collective-permute-start.7 = (f32[32,256]{1,0:T(8,128)S(1)}, f32[32,256]{1,0:T(8,128)S(1)}, u32[]{:S(2)}, u32[]{:S(2)}) collective-permute-start(f32[32,256]{1,0:T(8,128)S(1)} %max.48), channel_id=1, source_target_pairs={{0,9},{1,8},{2,11},{3,10},{4,13},{5,12},{6,15},{7,14},{8,1},{9,0},... | collective-permute-start | bytes 98312 | tf_op jit(solution)/shard_map/ppermute | solution.py:127
  25.8 4.1 %collective-permute-start.8 = (f32[16,256]{1,0:T(8,128)S(1)}, f32[16,256]{1,0:T(8,128)S(1)}, u32[]{:S(2)}, u32[]{:S(2)}) collective-permute-start(f32[16,256]{1,0:T(8,128)S(1)} %constant_dynamic-slice_fusion), channel_id=1, source_target_pairs={{0,17},{1,16},{2,19},{3,18},{4,21},{5,20},{6,23},{7,22},{8,25},{9,... | collective-permute-start | bytes 49160 | tf_op jit(solution)/shard_map/ppermute | solution.py:127
  30.0 3.2 %collective-permute-start.9 = (f32[16,256]{1,0:T(8,128)S(1)}, f32[16,256]{1,0:T(8,128)S(1)}, u32[]{:S(2)}, u32[]{:S(2)}) collective-permute-start(f32[16,256]{1,0:T(8,128)S(1)} %constant_dynamic-slice_fusion.4), channel_id=1, source_target_pairs={{0,3},{1,2},{2,1},{3,0},{4,7},{5,6},{6,5},{7,4},{8,11},{9,10},{10,... | collective-permute-start | bytes 49160 | tf_op jit(solution)/shard_map/ppermute | solution.py:127

commit v6 on v5

--- a/solution.py
+++ b/solution.py
@@ -49,13 +49,17 @@
     peak_ref[...] = jnp.zeros_like(peak_ref)
     for copy in copies[:2]:
         copy.wait()
-    for s in range(slots):
-        copies[2 + s].wait()
-        live = s < count_ref[0, 0]
-        size = jnp.abs(held_ref[s])
-        column_max = jnp.max(size, axis=0, keepdims=True)
-        raise_row(peak_ref, cols_ref[0, s], jnp.where(live, column_max, 0.0))
-        raise_row(peak_ref, rows_ref[0, s], jnp.where(live, lane_max(size), 0.0))
+    for first in range(0, slots, 2):
+        found = []
+        for copy in copies[2 + first : 4 + first]:
+            copy.wait()
+        for s in range(first, min(first + 2, slots)):
+            size = jnp.abs(held_ref[s])
+            found.append((s, jnp.max(size, axis=0, keepdims=True), lane_max(size)))
+        for s, column_max, row_max in found:
+            live = s < count_ref[0, 0]
+            raise_row(peak_ref, cols_ref[0, s], jnp.where(live, column_max, 0.0))
+            raise_row(peak_ref, rows_ref[0, s], jnp.where(live, row_max, 0.0))
 
 
 def next_kernel(rows_ref, cols_ref, count_ref, held_ref, old_ref, peak_ref, scale_ref):
@@ -63,13 +67,12 @@
     half = tile // 2
     scale_ref[...] = lax.rsqrt(old_ref[...])
     peak_ref[...] = jnp.zeros_like(peak_ref)
+    found = []
     for s in range(slots):
-        live = s < count_ref[0, 0]
         size = jnp.abs(held_ref[s])
-        row, col = rows_ref[0, s], cols_ref[0, s]
-        left = scale_ref[pl.ds(row, 1), :]
-        right = scale_ref[pl.ds(col, 1), :]
-        raise_row(peak_ref, row, jnp.where(live, lane_max(size * right) * left, 0.0))
+        left = scale_ref[pl.ds(rows_ref[0, s], 1), :]
+        right = scale_ref[pl.ds(cols_ref[0, s], 1), :]
+        row_max = lane_max(size * right) * left
         column = as_column(left, half)
         below = jnp.concatenate(
             [
@@ -78,7 +81,11 @@
             ],
             axis=1,
         )
-        raise_row(peak_ref, col, jnp.where(live, below * right, 0.0))
+        found.append((row_max, below * right))
+    for s, (row_max, column_max) in enumerate(found):
+        live = s < count_ref[0, 0]
+        raise_row(peak_ref, rows_ref[0, s], jnp.where(live, row_max, 0.0))
+        raise_row(peak_ref, cols_ref[0, s], jnp.where(live, column_max, 0.0))
     peak_ref[...] = peak_ref[...] * old_ref[...]
 
 
@@ -204,10 +211,20 @@
 
 def max_of_rows_too(values, wide_size, narrow_size):
     values = swap_in_chip(values, wide_size, narrow_size)
+    columns, rows, size = windows(values, wide_size, narrow_size)
+    share, group_size = wide_size // narrow_size, size // 2
+    group = lax.axis_index("wide") // share
     for bit in bits(1, wide_size // 2):
-        other = swap(values, lambda w, n: (w ^ bit, n ^ 1), wide_size, narrow_size)
-        values = jnp.maximum(values, other)
-    columns, rows, size = windows(values, wide_size, narrow_size)
+        group_start = (group if bit < share else group | 1) * group_size
+        sent = jnp.concatenate(
+            [
+                lax.dynamic_slice_in_dim(values, columns, size, 0),
+                lax.dynamic_slice_in_dim(values, group_start, group_size, 0),
+            ]
+        )
+        other = swap(sent, lambda w, n: (w ^ bit, n ^ 1), wide_size, narrow_size)
+        values = window_max(values, columns, other[:size])
+        values = window_max(values, group_start, other[size:])
     for start, partner in (
         (columns, lambda w, n: (w ^ wide_size // 2, n ^ 1)),
         (rows, lambda w, n: (w, n ^ 3)),

time: 34.7 us -> 34.5 us (level)
  no operation moved by 1% of the time
where the time goes in v6:
time: 34.5 us; the launch traced here: 34.3 us
  starting transfers between devices  15.5 us (45%)
  waiting for transfers between devices  13.8 us (40%)
  Pallas kernels  3.41 us (10%)
  between operations  1.43 us (4%)
    ppermute x10, starting transfers between devices, swap(): return lax.ppermute(values, BOTH, pairs)  15.5 us
    ppermute x10, waiting for transfers between devices, swap(): return lax.ppermute(values, BOTH, pairs)  13.8 us
    pallas_call x1, Pallas kernels, on_device(): pl.pallas_call(first_kernel, out_shape=(pltpu.SMEM(tile_rows.shape, jnp.i...  1.57 us
    pallas_call x1, Pallas kernels, on_device(): pl.pallas_call(functools.partial(last_kernel, ROWB), out_shape=(jax.Shape...  1.31 us
  transfers between devices with their start and end apart: 10, of which 10 were waited for; matrix products, arithmetic and copies ran while one was open for 0% of the time, Pallas kernels for 0%

profile of v6, /device:TPU:0, one launch (start us, length us, event | category | flops | bytes accessed | tf_op | source)
XLA Modules:
  0.0 34.3 jit_solution(17693347294438211613)
XLA Ops:
  1.3 1.6 %first_peaks.1 = (s32[1,6]{1,0:T(1,128)S(4)}, s32[1,6]{1,0:T(1,128)S(4)}, f32[6,256,256]{2,1,0:T(8,128)S(1)}, f32[32,256]{1,0:T(8,128)S(1)}) custom-call(s32[1,1]{1,0:T(1,128)S(6)} %copy.18.count_ref, s32[1,6]{1,0:T(1,128)} %rows_in.1, s32[1,6]{1,0:T(1,128)} %cols_in.1, f32[1,6,256,256]{3,2,1,0:T(8,128)} %tiles_ref.1), custom_call_target="tpu_custom_call" | custom-call | tf_op jit(solution)/shard_map/first_peaks/pallas_call | solution.py:242
  2.9 0.5 %collective-permute-start = (f32[12,256]{1,0:T(8,128)S(1)}, f32[12,256]{1,0:T(8,128)S(1)}, u32[]{:S(2)}, u32[]{:S(2)}) collective-permute-start(f32[12,256]{1,0:T(8,128)S(1)} %pad_maximum_fusion.2), channel_id=1, source_target_pairs={{0,1},{1,0},{2,3},{3,2},{4,5},{5,4},{6,7},{7,6},{8,9},{9,8},{10,11... | collective-permute-start | bytes 36872 | tf_op jit(solution)/shard_map/ppermute | solution.py:134
  3.4 0.8 %collective-permute-done = f32[12,256]{1,0:T(8,128)S(1)} collective-permute-done((f32[12,256]{1,0:T(8,128)S(1)}, f32[12,256]{1,0:T(8,128)S(1)}, u32[]{:S(2)}, u32[]{:S(2)}) %collective-permute-start) | collective-permute-done | bytes 12320 | tf_op jit(solution)/shard_map/ppermute | solution.py:134
  4.3 2.7 %collective-permute-start.1 = (f32[16,256]{1,0:T(8,128)S(1)}, f32[16,256]{1,0:T(8,128)S(1)}, u32[]{:S(2)}, u32[]{:S(2)}) collective-permute-start(f32[16,256]{1,0:T(8,128)S(1)} %constant_dynamic-slice_fusion.8), channel_id=1, source_target_pairs={{0,5},{1,4},{2,7},{3,6},{4,1},{5,0},{6,3},{7,2},{8,13},{9,12},{10,... | collective-permute-start | bytes 49160 | tf_op jit(solution)/shard_map/ppermute | solution.py:134
  7.0 1.4 %collective-permute-done.1 = f32[16,256]{1,0:T(8,128)S(1)} collective-permute-done((f32[16,256]{1,0:T(8,128)S(1)}, f32[16,256]{1,0:T(8,128)S(1)}, u32[]{:S(2)}, u32[]{:S(2)}) %collective-permute-start.1) | collective-permute-done | bytes 16416 | tf_op jit(solution)/shard_map/ppermute | solution.py:134
  8.4 1.8 %collective-permute-start.2 = (f32[16,256]{1,0:T(8,128)S(1)}, f32[16,256]{1,0:T(8,128)S(1)}, u32[]{:S(2)}, u32[]{:S(2)}) collective-permute-start(f32[16,256]{1,0:T(8,128)S(1)} %fusion.8), channel_id=1, source_target_pairs={{0,9},{1,2},{2,1},{3,10},{4,7},{5,12},{6,15},{7,4},{8,11},{9,0},{1... | collective-permute-start | bytes 49160 | tf_op jit(solution)/shard_map/ppermute | solution.py:134
  10.2 1.4 %collective-permute-done.2 = f32[16,256]{1,0:T(8,128)S(1)} collective-permute-done((f32[16,256]{1,0:T(8,128)S(1)}, f32[16,256]{1,0:T(8,128)S(1)}, u32[]{:S(2)}, u32[]{:S(2)}) %collective-permute-start.2) | collective-permute-done | bytes 16416 | tf_op jit(solution)/shard_map/ppermute | solution.py:134
  11.7 2.7 %collective-permute-start.3 = (f32[16,256]{1,0:T(8,128)S(1)}, f32[16,256]{1,0:T(8,128)S(1)}, u32[]{:S(2)}, u32[]{:S(2)}) collective-permute-start(f32[16,256]{1,0:T(8,128)S(1)} %max.48), channel_id=1, source_target_pairs={{0,17},{1,8},{2,11},{3,18},{4,13},{5,20},{6,23},{7,14},{8,1},{9,24... | collective-permute-start | bytes 49160 | tf_op jit(solution)/shard_map/ppermute | solution.py:134
  14.4 1.4 %collective-permute-done.3 = f32[16,256]{1,0:T(8,128)S(1)} collective-permute-done((f32[16,256]{1,0:T(8,128)S(1)}, f32[16,256]{1,0:T(8,128)S(1)}, u32[]{:S(2)}, u32[]{:S(2)}) %collective-permute-start.3) | collective-permute-done | bytes 16416 | tf_op jit(solution)/shard_map/ppermute | solution.py:134
  15.9 0.0 collective-permute-start.4
  15.9 1.2 %collective-permute-done.4 = f32[16,256]{1,0:T(8,128)S(1)} collective-permute-done((f32[16,256]{1,0:T(8,128)S(1)}, f32[16,256]{1,0:T(8,128)S(1)}, u32[]{:S(2)}, u32[]{:S(2)}) %collective-permute-start.4) | collective-permute-done | bytes 16416 | tf_op jit(solution)/shard_map/ppermute | solution.py:134
  17.0 0.5 %next_peaks.1 = f32[32,256]{1,0:T(8,128)S(1)} custom-call(s32[1,6]{1,0:T(1,128)S(4)} %get-tuple-element.6.rows_ref, s32[1,6]{1,0:T(1,128)S(4)} %get-tuple-element.7.cols_ref, s32[1,1]{1,0:T(1,128)S(6)} %copy.18.count_ref, f32[6,256,256]{2,1,0:T(8,128)S(1)} %get-tuple-element.8.held_ref, f32[32,256]{1,0:T(8,128)S(1)} %maximum_dynamic-update-slice_fusion.2.old_ref), custom_call_target="tpu_custom_call" | custom-call | tf_op jit(solution)/shard_map/next_peaks/pallas_call | solution.py:260
  17.6 0.2 collective-permute-start.5
  17.9 1.0 %collective-permute-done.5 = f32[12,256]{1,0:T(8,128)S(1)} collective-permute-done((f32[12,256]{1,0:T(8,128)S(1)}, f32[12,256]{1,0:T(8,128)S(1)}, u32[]{:S(2)}, u32[]{:S(2)}) %collective-permute-start.5) | collective-permute-done | bytes 12320 | tf_op jit(solution)/shard_map/ppermute | solution.py:134
  18.9 1.6 %collective-permute-start.6 = (f32[24,256]{1,0:T(8,128)S(1)}, f32[24,256]{1,0:T(8,128)S(1)}, u32[]{:S(2)}, u32[]{:S(2)}) collective-permute-start(f32[24,256]{1,0:T(8,128)S(1)} %pad_maximum_fusion), channel_id=1, source_target_pairs={{0,5},{1,4},{2,7},{3,6},{4,1},{5,0},{6,3},{7,2},{8,13},{9,12},{10,... | collective-permute-start | bytes 73736 | tf_op jit(solution)/shard_map/ppermute | solution.py:134
  20.6 1.7 %collective-permute-done.6 = f32[24,256]{1,0:T(8,128)S(1)} collective-permute-done((f32[24,256]{1,0:T(8,128)S(1)}, f32[24,256]{1,0:T(8,128)S(1)}, u32[]{:S(2)}, u32[]{:S(2)}) %collective-permute-start.6) | collective-permute-done | bytes 24608 | tf_op jit(solution)/shard_map/ppermute | solution.py:134
  22.3 1.7 %collective-permute-start.7 = (f32[24,256]{1,0:T(8,128)S(1)}, f32[24,256]{1,0:T(8,128)S(1)}, u32[]{:S(2)}, u32[]{:S(2)}) collective-permute-start(f32[24,256]{1,0:T(8,128)S(1)} %pad_maximum_fusion.1), channel_id=1, source_target_pairs={{0,9},{1,8},{2,11},{3,10},{4,13},{5,12},{6,15},{7,14},{8,1},{9,0},... | collective-permute-start | bytes 73736 | tf_op jit(solution)/shard_map/ppermute | solution.py:134
  24.0 1.6 %collective-permute-done.7 = f32[24,256]{1,0:T(8,128)S(1)} collective-permute-done((f32[24,256]{1,0:T(8,128)S(1)}, f32[24,256]{1,0:T(8,128)S(1)}, u32[]{:S(2)}, u32[]{:S(2)}) %collective-permute-start.7) | collective-permute-done | bytes 24608 | tf_op jit(solution)/shard_map/ppermute | solution.py:134
  25.7 2.7 %collective-permute-start.8 = (f32[16,256]{1,0:T(8,128)S(1)}, f32[16,256]{1,0:T(8,128)S(1)}, u32[]{:S(2)}, u32[]{:S(2)}) collective-permute-start(f32[16,256]{1,0:T(8,128)S(1)} %constant_dynamic-slice_fusion.12), channel_id=1, source_target_pairs={{0,17},{1,16},{2,19},{3,18},{4,21},{5,20},{6,23},{7,22},{8,25},{9,... | collective-permute-start | bytes 49160 | tf_op jit(solution)/shard_map/ppermute | solution.py:134
  28.4 1.4 %collective-permute-done.8 = f32[16,256]{1,0:T(8,128)S(1)} collective-permute-done((f32[16,256]{1,0:T(8,128)S(1)}, f32[16,256]{1,0:T(8,128)S(1)}, u32[]{:S(2)}, u32[]{:S(2)}) %collective-permute-start.8) | collective-permute-done | bytes 16416 | tf_op jit(solution)/shard_map/ppermute | solution.py:134
  29.8 1.6 %collective-permute-start.9 = (f32[16,256]{1,0:T(8,128)S(1)}, f32[16,256]{1,0:T(8,128)S(1)}, u32[]{:S(2)}, u32[]{:S(2)}) collective-permute-start(f32[16,256]{1,0:T(8,128)S(1)} %constant_dynamic-slice_fusion), channel_id=1, source_target_pairs={{0,3},{1,2},{2,1},{3,0},{4,7},{5,6},{6,5},{7,4},{8,11},{9,10},{10,... | collective-permute-start | bytes 49160 | tf_op jit(solution)/shard_map/ppermute | solution.py:134
  31.4 1.6 %collective-permute-done.9 = f32[16,256]{1,0:T(8,128)S(1)} collective-permute-done((f32[16,256]{1,0:T(8,128)S(1)}, f32[16,256]{1,0:T(8,128)S(1)}, u32[]{:S(2)}, u32[]{:S(2)}) %collective-permute-start.9) | collective-permute-done | bytes 16416 | tf_op jit(solution)/shard_map/ppermute | solution.py:134
  33.0 1.3 %scaled_tiles.1 = (f32[1,6,256,256]{3,2,1,0:T(8,128)}, f32[4,256]{1,0:T(4,128)}) custom-call(s32[1,6]{1,0:T(1,128)S(4)} %get-tuple-element.6.rows_ref, s32[1,6]{1,0:T(1,128)S(4)} %get-tuple-element.7.cols_ref, s32[1,1]{1,0:T(1,128)S(6)} %copy.18.count_ref, f32[6,256,256]{2,1,0:T(8,128)S(1)} %get-tuple-element.8.held_ref, ...), custom_call_target="tpu_custom_call" | custom-call | tf_op jit(solution)/shard_map/scaled_tiles/pallas_call | solution.py:270
  (29 shorter events, 0.2 us)
Async XLA Ops:
  2.9 1.4 %collective-permute-start = (f32[12,256]{1,0:T(8,128)S(1)}, f32[12,256]{1,0:T(8,128)S(1)}, u32[]{:S(2)}, u32[]{:S(2)}) collective-permute-start(f32[12,256]{1,0:T(8,128)S(1)} %pad_maximum_fusion.2), channel_id=1, source_target_pairs={{0,1},{1,0},{2,3},{3,2},{4,5},{5,4},{6,7},{7,6},{8,9},{9,8},{10,11... | collective-permute-start | bytes 36872 | tf_op jit(solution)/shard_map/ppermute | solution.py:134
  4.3 4.1 %collective-permute-start.1 = (f32[16,256]{1,0:T(8,128)S(1)}, f32[16,256]{1,0:T(8,128)S(1)}, u32[]{:S(2)}, u32[]{:S(2)}) collective-permute-start(f32[16,256]{1,0:T(8,128)S(1)} %constant_dynamic-slice_fusion.8), channel_id=1, source_target_pairs={{0,5},{1,4},{2,7},{3,6},{4,1},{5,0},{6,3},{7,2},{8,13},{9,12},{10,... | collective-permute-start | bytes 49160 | tf_op jit(solution)/shard_map/ppermute | solution.py:134
  8.4 3.2 %collective-permute-start.2 = (f32[16,256]{1,0:T(8,128)S(1)}, f32[16,256]{1,0:T(8,128)S(1)}, u32[]{:S(2)}, u32[]{:S(2)}) collective-permute-start(f32[16,256]{1,0:T(8,128)S(1)} %fusion.8), channel_id=1, source_target_pairs={{0,9},{1,2},{2,1},{3,10},{4,7},{5,12},{6,15},{7,4},{8,11},{9,0},{1... | collective-permute-start | bytes 49160 | tf_op jit(solution)/shard_map/ppermute | solution.py:134
  11.7 4.2 %collective-permute-start.3 = (f32[16,256]{1,0:T(8,128)S(1)}, f32[16,256]{1,0:T(8,128)S(1)}, u32[]{:S(2)}, u32[]{:S(2)}) collective-permute-start(f32[16,256]{1,0:T(8,128)S(1)} %max.48), channel_id=1, source_target_pairs={{0,17},{1,8},{2,11},{3,18},{4,13},{5,20},{6,23},{7,14},{8,1},{9,24... | collective-permute-start | bytes 49160 | tf_op jit(solution)/shard_map/ppermute | solution.py:134
  15.9 1.2 %collective-permute-start.4 = (f32[16,256]{1,0:T(8,128)S(1)}, f32[16,256]{1,0:T(8,128)S(1)}, u32[]{:S(2)}, u32[]{:S(2)}) collective-permute-start(f32[16,256]{1,0:T(8,128)S(1)} %get-tuple-element.11), channel_id=1, source_target_pairs={{0,1},{1,0},{2,3},{3,2},{4,5},{5,4},{6,7},{7,6},{8,9},{9,8},{10,11... | collective-permute-start | bytes 49160 | tf_op jit(solution)/shard_map/ppermute | solution.py:134
  17.6 1.2 %collective-permute-start.5 = (f32[12,256]{1,0:T(8,128)S(1)}, f32[12,256]{1,0:T(8,128)S(1)}, u32[]{:S(2)}, u32[]{:S(2)}) collective-permute-start(f32[12,256]{1,0:T(8,128)S(1)} %pad_maximum_fusion.3), channel_id=1, source_target_pairs={{0,1},{1,0},{2,3},{3,2},{4,5},{5,4},{6,7},{7,6},{8,9},{9,8},{10,11... | collective-permute-start | bytes 36872 | tf_op jit(solution)/shard_map/ppermute | solution.py:134
  18.9 3.3 %collective-permute-start.6 = (f32[24,256]{1,0:T(8,128)S(1)}, f32[24,256]{1,0:T(8,128)S(1)}, u32[]{:S(2)}, u32[]{:S(2)}) collective-permute-start(f32[24,256]{1,0:T(8,128)S(1)} %pad_maximum_fusion), channel_id=1, source_target_pairs={{0,5},{1,4},{2,7},{3,6},{4,1},{5,0},{6,3},{7,2},{8,13},{9,12},{10,... | collective-permute-start | bytes 73736 | tf_op jit(solution)/shard_map/ppermute | solution.py:134
  22.3 3.3 %collective-permute-start.7 = (f32[24,256]{1,0:T(8,128)S(1)}, f32[24,256]{1,0:T(8,128)S(1)}, u32[]{:S(2)}, u32[]{:S(2)}) collective-permute-start(f32[24,256]{1,0:T(8,128)S(1)} %pad_maximum_fusion.1), channel_id=1, source_target_pairs={{0,9},{1,8},{2,11},{3,10},{4,13},{5,12},{6,15},{7,14},{8,1},{9,0},... | collective-permute-start | bytes 73736 | tf_op jit(solution)/shard_map/ppermute | solution.py:134
  25.7 4.1 %collective-permute-start.8 = (f32[16,256]{1,0:T(8,128)S(1)}, f32[16,256]{1,0:T(8,128)S(1)}, u32[]{:S(2)}, u32[]{:S(2)}) collective-permute-start(f32[16,256]{1,0:T(8,128)S(1)} %constant_dynamic-slice_fusion.12), channel_id=1, source_target_pairs={{0,17},{1,16},{2,19},{3,18},{4,21},{5,20},{6,23},{7,22},{8,25},{9,... | collective-permute-start | bytes 49160 | tf_op jit(solution)/shard_map/ppermute | solution.py:134
  29.8 3.2 %collective-permute-start.9 = (f32[16,256]{1,0:T(8,128)S(1)}, f32[16,256]{1,0:T(8,128)S(1)}, u32[]{:S(2)}, u32[]{:S(2)}) collective-permute-start(f32[16,256]{1,0:T(8,128)S(1)} %constant_dynamic-slice_fusion), channel_id=1, source_target_pairs={{0,3},{1,2},{2,1},{3,0},{4,7},{5,6},{6,5},{7,4},{8,11},{9,10},{10,... | collective-permute-start | bytes 49160 | tf_op jit(solution)/shard_map/ppermute | solution.py:134

commit v7 on v6

--- a/solution.py
+++ b/solution.py
@@ -35,7 +35,16 @@
 
 
 def first_kernel(
-    count_ref, rows_in, cols_in, tiles_ref, rows_ref, cols_ref, held_ref, peak_ref, sems
+    count_ref,
+    rows_in,
+    cols_in,
+    tiles_ref,
+    rows_ref,
+    cols_ref,
+    held_ref,
+    peak_ref,
+    places_ref,
+    sems,
 ):
     slots = tiles_ref.shape[1]
     moves = [(rows_in, rows_ref), (cols_in, cols_ref)]
@@ -49,6 +58,13 @@
     peak_ref[...] = jnp.zeros_like(peak_ref)
     for copy in copies[:2]:
         copy.wait()
+    values = [count_ref[0, 0]]
+    values += [ref[0, s] for s in range(slots) for ref in (rows_ref, cols_ref)]
+    lane = lax.broadcasted_iota(jnp.int32, places_ref.shape, 1)
+    places = jnp.zeros(places_ref.shape, jnp.int32)
+    for k, value in enumerate(values):
+        places = jnp.where(lane == k, value, places)
+    places_ref[...] = places.astype(jnp.float32)
     for first in range(0, slots, 2):
         found = []
         for copy in copies[2 + first : 4 + first]:
@@ -62,30 +78,45 @@
             raise_row(peak_ref, rows_ref[0, s], jnp.where(live, row_max, 0.0))
 
 
-def next_kernel(rows_ref, cols_ref, count_ref, held_ref, old_ref, peak_ref, scale_ref):
+def places_kernel(index_ref, places_ref, whole_ref, sem):
+    whole_ref[...] = index_ref[...].astype(jnp.int32)
+    copy = pltpu.make_async_copy(whole_ref, places_ref, sem.at[0])
+    copy.start()
+    copy.wait()
+
+
+def next_kernel(
+    rows_ref, cols_ref, count_ref, mate_places, held_ref, mate_ref, old_ref, peak_ref, scale_ref
+):
     slots, _, tile = held_ref.shape
     half = tile // 2
     scale_ref[...] = lax.rsqrt(old_ref[...])
     peak_ref[...] = jnp.zeros_like(peak_ref)
-    found = []
-    for s in range(slots):
-        size = jnp.abs(held_ref[s])
-        left = scale_ref[pl.ds(rows_ref[0, s], 1), :]
-        right = scale_ref[pl.ds(cols_ref[0, s], 1), :]
-        row_max = lane_max(size * right) * left
-        column = as_column(left, half)
-        below = jnp.concatenate(
-            [
-                jnp.max(size[:, :half] * column, axis=0, keepdims=True),
-                jnp.max(size[:, half:] * column, axis=0, keepdims=True),
-            ],
-            axis=1,
-        )
-        found.append((row_max, below * right))
-    for s, (row_max, column_max) in enumerate(found):
-        live = s < count_ref[0, 0]
-        raise_row(peak_ref, rows_ref[0, s], jnp.where(live, row_max, 0.0))
-        raise_row(peak_ref, cols_ref[0, s], jnp.where(live, column_max, 0.0))
+
+    def add(tiles_ref, count, places):
+        found = []
+        for s, (row, col) in enumerate(places):
+            size = jnp.abs(tiles_ref[s])
+            left = scale_ref[pl.ds(row, 1), :]
+            right = scale_ref[pl.ds(col, 1), :]
+            row_max = lane_max(size * right) * left
+            column = as_column(left, half)
+            below = jnp.concatenate(
+                [
+                    jnp.max(size[:, :half] * column, axis=0, keepdims=True),
+                    jnp.max(size[:, half:] * column, axis=0, keepdims=True),
+                ],
+                axis=1,
+            )
+            found.append((row_max, below * right))
+        for s, (row_max, column_max) in enumerate(found):
+            raise_row(peak_ref, places[s][0], jnp.where(s < count, row_max, 0.0))
+            raise_row(peak_ref, places[s][1], jnp.where(s < count, column_max, 0.0))
+
+    given = [mate_places[0, k] for k in range(2 * slots + 1)]
+    own = [(rows_ref[0, s], cols_ref[0, s]) for s in range(slots)]
+    add(held_ref, count_ref[0, 0], own)
+    add(mate_ref, given[0], list(zip(given[1::2], given[2::2])))
     peak_ref[...] = peak_ref[...] * old_ref[...]
 
 
@@ -140,9 +171,8 @@
         first *= 2
 
 
-def max_over_devices(values, wide_size, narrow_size):
-    steps = [(0, 1)]
-    steps += [(bit, 1) for bit in bits(1, wide_size)]
+def max_over_chips(values, wide_size, narrow_size):
+    steps = [(bit, 1) for bit in bits(1, wide_size)]
     steps += [(0, bit + 1) for bit in bits(2, narrow_size)]
     for wide_bit, narrow_bit in steps:
         other = swap(
@@ -157,7 +187,7 @@
     return lax.dynamic_update_slice_in_dim(values, jnp.maximum(old, window), start, 0)
 
 
-def swap_in_chip(values, wide_size, narrow_size):
+def swap_in_chip(values, places, wide_size, narrow_size):
     columns = values.shape[0] // narrow_size
     row_start = lax.axis_index("wide") * ROWB
     n = lax.axis_index("narrow")
@@ -165,11 +195,12 @@
         [
             lax.dynamic_slice_in_dim(values, n * columns, columns, 0),
             lax.dynamic_slice_in_dim(values, row_start, ROWB, 0),
+            places,
         ]
     )
     other = swap(sent, lambda w, n: (w, n ^ 1), wide_size, narrow_size)
     values = window_max(values, (n ^ 1) * columns, other[:columns])
-    return window_max(values, row_start, other[columns:])
+    return window_max(values, row_start, other[columns:-1]), other[-1:]
 
 
 def windows(values, wide_size, narrow_size):
@@ -194,7 +225,6 @@
     def second(w, n):
         return (w ^ 2 * share if along_columns(w, n) else w ^ share, n ^ 1)
 
-    values = swap_in_chip(values, wide_size, narrow_size)
     columns, rows, size = windows(values, wide_size, narrow_size)
     chosen = along_columns(lax.axis_index("wide"), lax.axis_index("narrow"))
     start = jnp.where(chosen, columns, rows)
@@ -210,7 +240,6 @@
 
 
 def max_of_rows_too(values, wide_size, narrow_size):
-    values = swap_in_chip(values, wide_size, narrow_size)
     columns, rows, size = windows(values, wide_size, narrow_size)
     share, group_size = wide_size // narrow_size, size // 2
     group = lax.axis_index("wide") // share
@@ -239,34 +268,48 @@
     slots, tile = tiles.shape[1], tiles.shape[2]
     blocks = ROWB * wide_size
     four = narrow_size == 4
-    rows, cols, held, part = pl.pallas_call(
+    rows, cols, held, part, index = pl.pallas_call(
         first_kernel,
         out_shape=(
             pltpu.SMEM(tile_rows.shape, jnp.int32),
             pltpu.SMEM(tile_cols.shape, jnp.int32),
             pltpu.VMEM((slots, tile, tile), jnp.float32),
             pltpu.VMEM((blocks, tile), jnp.float32),
+            pltpu.VMEM((1, tile), jnp.float32),
         ),
         in_specs=[SMEM, HBM, HBM, HBM],
-        out_specs=(SMEM, SMEM, VMEM, VMEM),
+        out_specs=(SMEM, SMEM, VMEM, VMEM, VMEM),
         scratch_shapes=[pltpu.SemaphoreType.DMA((2 + slots,))],
         compiler_params=PARAMS,
         name="first_peaks",
     )(tile_counts, *kept((tile_rows, tile_cols, tiles), pltpu.HBM))
     places = (*kept((rows, cols), pltpu.SMEM), tile_counts)
+    part, index = swap_in_chip(part, index, wide_size, narrow_size)
+    part, sent = lax.optimization_barrier((part, held))
+    mate = swap(sent, lambda w, n: (w, n ^ 1), wide_size, narrow_size)
     held = kept([held], pltpu.VMEM)
+    mate_places = pl.pallas_call(
+        places_kernel,
+        out_shape=pltpu.SMEM(index.shape, jnp.int32),
+        in_specs=[VMEM],
+        out_specs=SMEM,
+        scratch_shapes=[pltpu.VMEM(index.shape, jnp.int32), pltpu.SemaphoreType.DMA((1,))],
+        compiler_params=PARAMS,
+        name="other_places",
+    )(*kept([index], pltpu.VMEM))
+    places_too = (*places, *kept([mate_places], pltpu.SMEM))
     for iteration in range(1, ITERS):
-        full = (max_over_users if four else max_over_devices)(part, wide_size, narrow_size)
+        full = (max_over_users if four else max_over_chips)(part, wide_size, narrow_size)
         part = pl.pallas_call(
             next_kernel,
             out_shape=pltpu.VMEM((blocks, tile), jnp.float32),
-            in_specs=[SMEM] * 3 + [VMEM] * 2,
+            in_specs=[SMEM] * 4 + [VMEM] * 3,
             out_specs=VMEM,
             scratch_shapes=[pltpu.VMEM((blocks, tile), jnp.float32)],
             compiler_params=PARAMS,
             name="next_peaks",
-        )(*places, *held, *kept([full], pltpu.VMEM))
-    full = (max_of_rows_too if four else max_over_devices)(part, wide_size, narrow_size)
+        )(*places_too, *held, *kept([mate, full], pltpu.VMEM))
+    full = (max_of_rows_too if four else max_over_chips)(part, wide_size, narrow_size)
     return pl.pallas_call(
         functools.partial(last_kernel, ROWB),
         out_shape=(

time: 34.5 us -> 34 us (0.986)
  waiting for transfers between devices: 13.8 us -> 12.2 us
  Pallas kernels: 3.41 us -> 4.41 us
    ppermute x10, waiting for transfers between devices: 13.8 us -> 12.2 us  [swap(): return lax.ppermute(values, BOTH, pairs)]
    pallas_call x0 -> x1, Pallas kernels: none -> 0.56 us  [on_device(): pl.pallas_call(places_kernel, out_shape=pltpu.SMEM(index.shape, jnp.int32...]
    pallas_call x1, Pallas kernels: 0.53 us -> 0.97 us  [on_device(): pl.pallas_call(next_kernel, out_shape=pltpu.VMEM((blocks, tile), jnp.floa...]
  transfers between devices with their start and end apart: 10 -> 10, of which waited for: 10 -> 9; matrix products, arithmetic and copies ran while one was open for 0% -> 0% of each run, Pallas kernels for 0% -> 2%
where the time goes in v7:
time: 34 us; the launch traced here: 33.8 us
  starting transfers between devices  15.6 us (46%)
  waiting for transfers between devices  12.2 us (36%)
  Pallas kernels  4.41 us (13%)
  between operations  1.42 us (4%)
    ppermute x10, starting transfers between devices, swap(): return lax.ppermute(values, BOTH, pairs)  15.6 us
    ppermute x10, waiting for transfers between devices, swap(): return lax.ppermute(values, BOTH, pairs)  12.2 us
    pallas_call x1, Pallas kernels, on_device(): pl.pallas_call(first_kernel, out_shape=(pltpu.SMEM(tile_rows.shape, jnp.i...  1.57 us
    pallas_call x1, Pallas kernels, on_device(): pl.pallas_call(functools.partial(last_kernel, ROWB), out_shape=(jax.Shape...  1.31 us
    pallas_call x1, Pallas kernels, on_device(): pl.pallas_call(next_kernel, out_shape=pltpu.VMEM((blocks, tile), jnp.floa...  0.97 us
  transfers between devices with their start and end apart: 10, of which 9 were waited for; matrix products, arithmetic and copies ran while one was open for 0% of the time, Pallas kernels for 2%

profile of v7, /device:TPU:0, one launch (start us, length us, event | category | flops | bytes accessed | tf_op | source)
XLA Modules:
  0.0 33.8 jit_solution(3581646251824346019)
XLA Ops:
  1.3 1.6 %first_peaks.1 = (s32[1,6]{1,0:T(1,128)S(4)}, s32[1,6]{1,0:T(1,128)S(4)}, f32[6,256,256]{2,1,0:T(8,128)S(1)}, f32[32,256]{1,0:T(8,128)S(1)}, f32[1,256]{1,0:T(1,128)S(1)}) custom-call(s32[1,1]{1,0:T(1,128)S(6)} %copy.16.count_ref, s32[1,6]{1,0:T(1,128)} %rows_in.1, s32[1,6]{1,0:T(1,128)} %cols_in.1, f32[1,6,256,256]{3,2,1,0:T(8,128)} %tiles_ref.1), custom_call_target="tpu_custom_call" | custom-call | tf_op jit(solution)/shard_map/first_peaks/pallas_call | solution.py:271
  2.9 0.5 %collective-permute-start = (f32[13,256]{1,0:T(8,128)S(1)}, f32[13,256]{1,0:T(8,128)S(1)}, u32[]{:S(2)}, u32[]{:S(2)}) collective-permute-start(f32[13,256]{1,0:T(8,128)S(1)} %pad_maximum_fusion.2), channel_id=1, source_target_pairs={{0,1},{1,0},{2,3},{3,2},{4,5},{5,4},{6,7},{7,6},{8,9},{9,8},{10,11... | collective-permute-start | bytes 39944 | tf_op jit(solution)/shard_map/ppermute | solution.py:165
  3.4 0.8 %collective-permute-done = f32[13,256]{1,0:T(8,128)S(1)} collective-permute-done((f32[13,256]{1,0:T(8,128)S(1)}, f32[13,256]{1,0:T(8,128)S(1)}, u32[]{:S(2)}, u32[]{:S(2)}) %collective-permute-start) | collective-permute-done | bytes 13344 | tf_op jit(solution)/shard_map/ppermute | solution.py:165
  4.3 0.4 %collective-permute-start.1 = (f32[6,256,256]{2,1,0:T(8,128)S(1)}, f32[6,256,256]{2,1,0:T(8,128)S(1)}, u32[]{:S(2)}, u32[]{:S(2)}) collective-permute-start(f32[6,256,256]{2,1,0:T(8,128)S(1)} %get-tuple-element.14.held_ref), channel_id=1, source_target_pairs={{0,1},{1,0},{2,3},{3,2},{4,5},{5,4},{6,7},{7,6},{8,9},{9,8},{10,11... | collective-permute-start | bytes 4718600 | tf_op jit(solution)/shard_map/ppermute | solution.py:165
  4.7 2.6 %collective-permute-start.2 = (f32[16,256]{1,0:T(8,128)S(1)}, f32[16,256]{1,0:T(8,128)S(1)}, u32[]{:S(2)}, u32[]{:S(2)}) collective-permute-start(f32[16,256]{1,0:T(8,128)S(1)} %constant_dynamic-slice_fusion.6), channel_id=1, source_target_pairs={{0,5},{1,4},{2,7},{3,6},{4,1},{5,0},{6,3},{7,2},{8,13},{9,12},{10,... | collective-permute-start | bytes 49160 | tf_op jit(solution)/shard_map/ppermute | solution.py:165
  7.3 1.4 %collective-permute-done.2 = f32[16,256]{1,0:T(8,128)S(1)} collective-permute-done((f32[16,256]{1,0:T(8,128)S(1)}, f32[16,256]{1,0:T(8,128)S(1)}, u32[]{:S(2)}, u32[]{:S(2)}) %collective-permute-start.2) | collective-permute-done | bytes 16416 | tf_op jit(solution)/shard_map/ppermute | solution.py:165
  8.8 1.8 %collective-permute-start.3 = (f32[16,256]{1,0:T(8,128)S(1)}, f32[16,256]{1,0:T(8,128)S(1)}, u32[]{:S(2)}, u32[]{:S(2)}) collective-permute-start(f32[16,256]{1,0:T(8,128)S(1)} %fusion.6), channel_id=1, source_target_pairs={{0,9},{1,2},{2,1},{3,10},{4,7},{5,12},{6,15},{7,4},{8,11},{9,0},{1... | collective-permute-start | bytes 49160 | tf_op jit(solution)/shard_map/ppermute | solution.py:165
  10.6 1.4 %collective-permute-done.3 = f32[16,256]{1,0:T(8,128)S(1)} collective-permute-done((f32[16,256]{1,0:T(8,128)S(1)}, f32[16,256]{1,0:T(8,128)S(1)}, u32[]{:S(2)}, u32[]{:S(2)}) %collective-permute-start.3) | collective-permute-done | bytes 16416 | tf_op jit(solution)/shard_map/ppermute | solution.py:165
  12.0 2.7 %collective-permute-start.4 = (f32[16,256]{1,0:T(8,128)S(1)}, f32[16,256]{1,0:T(8,128)S(1)}, u32[]{:S(2)}, u32[]{:S(2)}) collective-permute-start(f32[16,256]{1,0:T(8,128)S(1)} %max.42), channel_id=1, source_target_pairs={{0,17},{1,8},{2,11},{3,18},{4,13},{5,20},{6,23},{7,14},{8,1},{9,24... | collective-permute-start | bytes 49160 | tf_op jit(solution)/shard_map/ppermute | solution.py:165
  14.7 1.4 %collective-permute-done.4 = f32[16,256]{1,0:T(8,128)S(1)} collective-permute-done((f32[16,256]{1,0:T(8,128)S(1)}, f32[16,256]{1,0:T(8,128)S(1)}, u32[]{:S(2)}, u32[]{:S(2)}) %collective-permute-start.4) | collective-permute-done | bytes 16416 | tf_op jit(solution)/shard_map/ppermute | solution.py:165
  16.2 0.0 collective-permute-start.5
  16.2 0.6 %other_places.1.mate_places = s32[1,256]{1,0:T(1,128)S(4)} custom-call(f32[1,256]{1,0:T(1,128)S(1)} %slice.28.index_ref), custom_call_target="tpu_custom_call" | custom-call | tf_op jit(solution)/shard_map/other_places/pallas_call | solution.py:291
  16.8 0.6 %collective-permute-done.5 = f32[16,256]{1,0:T(8,128)S(1)} collective-permute-done((f32[16,256]{1,0:T(8,128)S(1)}, f32[16,256]{1,0:T(8,128)S(1)}, u32[]{:S(2)}, u32[]{:S(2)}) %collective-permute-start.5) | collective-permute-done | bytes 16416 | tf_op jit(solution)/shard_map/ppermute | solution.py:165
  17.4 0.0 collective-permute-done.1.mate_ref
  17.4 1.0 %next_peaks.1 = f32[32,256]{1,0:T(8,128)S(1)} custom-call(s32[1,6]{1,0:T(1,128)S(4)} %get-tuple-element.9.rows_ref, s32[1,6]{1,0:T(1,128)S(4)} %get-tuple-element.10.cols_ref, s32[1,1]{1,0:T(1,128)S(6)} %copy.16.count_ref, s32[1,256]{1,0:T(1,128)S(4)} %other_places.1.mate_places, f32[6,256,256]{2,1,0:T(8,128)S(1)} %get-tuple-element.14.held_ref, ...), custom_call_target="tpu_custom_call" | custom-call | tf_op jit(solution)/shard_map/next_peaks/pallas_call | solution.py:303
  18.4 1.6 %collective-permute-start.6 = (f32[24,256]{1,0:T(8,128)S(1)}, f32[24,256]{1,0:T(8,128)S(1)}, u32[]{:S(2)}, u32[]{:S(2)}) collective-permute-start(f32[24,256]{1,0:T(8,128)S(1)} %pad_maximum_fusion), channel_id=1, source_target_pairs={{0,5},{1,4},{2,7},{3,6},{4,1},{5,0},{6,3},{7,2},{8,13},{9,12},{10,... | collective-permute-start | bytes 73736 | tf_op jit(solution)/shard_map/ppermute | solution.py:165
  20.0 1.7 %collective-permute-done.6 = f32[24,256]{1,0:T(8,128)S(1)} collective-permute-done((f32[24,256]{1,0:T(8,128)S(1)}, f32[24,256]{1,0:T(8,128)S(1)}, u32[]{:S(2)}, u32[]{:S(2)}) %collective-permute-start.6) | collective-permute-done | bytes 24608 | tf_op jit(solution)/shard_map/ppermute | solution.py:165
  21.8 1.7 %collective-permute-start.7 = (f32[24,256]{1,0:T(8,128)S(1)}, f32[24,256]{1,0:T(8,128)S(1)}, u32[]{:S(2)}, u32[]{:S(2)}) collective-permute-start(f32[24,256]{1,0:T(8,128)S(1)} %pad_maximum_fusion.1), channel_id=1, source_target_pairs={{0,9},{1,8},{2,11},{3,10},{4,13},{5,12},{6,15},{7,14},{8,1},{9,0},... | collective-permute-start | bytes 73736 | tf_op jit(solution)/shard_map/ppermute | solution.py:165
  23.4 1.6 %collective-permute-done.7 = f32[24,256]{1,0:T(8,128)S(1)} collective-permute-done((f32[24,256]{1,0:T(8,128)S(1)}, f32[24,256]{1,0:T(8,128)S(1)}, u32[]{:S(2)}, u32[]{:S(2)}) %collective-permute-start.7) | collective-permute-done | bytes 24608 | tf_op jit(solution)/shard_map/ppermute | solution.py:165
  25.1 2.7 %collective-permute-start.8 = (f32[16,256]{1,0:T(8,128)S(1)}, f32[16,256]{1,0:T(8,128)S(1)}, u32[]{:S(2)}, u32[]{:S(2)}) collective-permute-start(f32[16,256]{1,0:T(8,128)S(1)} %constant_dynamic-slice_fusion), channel_id=1, source_target_pairs={{0,17},{1,16},{2,19},{3,18},{4,21},{5,20},{6,23},{7,22},{8,25},{9,... | collective-permute-start | bytes 49160 | tf_op jit(solution)/shard_map/ppermute | solution.py:165
  27.8 1.4 %collective-permute-done.8 = f32[16,256]{1,0:T(8,128)S(1)} collective-permute-done((f32[16,256]{1,0:T(8,128)S(1)}, f32[16,256]{1,0:T(8,128)S(1)}, u32[]{:S(2)}, u32[]{:S(2)}) %collective-permute-start.8) | collective-permute-done | bytes 16416 | tf_op jit(solution)/shard_map/ppermute | solution.py:165
  29.3 1.6 %collective-permute-start.9 = (f32[16,256]{1,0:T(8,128)S(1)}, f32[16,256]{1,0:T(8,128)S(1)}, u32[]{:S(2)}, u32[]{:S(2)}) collective-permute-start(f32[16,256]{1,0:T(8,128)S(1)} %constant_dynamic-slice_fusion.1), channel_id=1, source_target_pairs={{0,3},{1,2},{2,1},{3,0},{4,7},{5,6},{6,5},{7,4},{8,11},{9,10},{10,... | collective-permute-start | bytes 49160 | tf_op jit(solution)/shard_map/ppermute | solution.py:165
  30.8 1.6 %collective-permute-done.9 = f32[16,256]{1,0:T(8,128)S(1)} collective-permute-done((f32[16,256]{1,0:T(8,128)S(1)}, f32[16,256]{1,0:T(8,128)S(1)}, u32[]{:S(2)}, u32[]{:S(2)}) %collective-permute-start.9) | collective-permute-done | bytes 16416 | tf_op jit(solution)/shard_map/ppermute | solution.py:165
  32.5 1.3 %scaled_tiles.1 = (f32[1,6,256,256]{3,2,1,0:T(8,128)}, f32[4,256]{1,0:T(4,128)}) custom-call(s32[1,6]{1,0:T(1,128)S(4)} %get-tuple-element.9.rows_ref, s32[1,6]{1,0:T(1,128)S(4)} %get-tuple-element.10.cols_ref, s32[1,1]{1,0:T(1,128)S(6)} %copy.16.count_ref, f32[6,256,256]{2,1,0:T(8,128)S(1)} %get-tuple-element.14.held_ref, ...), custom_call_target="tpu_custom_call" | custom-call | tf_op jit(solution)/shard_map/scaled_tiles/pallas_call | solution.py:313
  (25 shorter events, 0.2 us)
Async XLA Ops:
  2.9 1.4 %collective-permute-start = (f32[13,256]{1,0:T(8,128)S(1)}, f32[13,256]{1,0:T(8,128)S(1)}, u32[]{:S(2)}, u32[]{:S(2)}) collective-permute-start(f32[13,256]{1,0:T(8,128)S(1)} %pad_maximum_fusion.2), channel_id=1, source_target_pairs={{0,1},{1,0},{2,3},{3,2},{4,5},{5,4},{6,7},{7,6},{8,9},{9,8},{10,11... | collective-permute-start | bytes 39944 | tf_op jit(solution)/shard_map/ppermute | solution.py:165
  4.3 13.1 %collective-permute-start.1 = (f32[6,256,256]{2,1,0:T(8,128)S(1)}, f32[6,256,256]{2,1,0:T(8,128)S(1)}, u32[]{:S(2)}, u32[]{:S(2)}) collective-permute-start(f32[6,256,256]{2,1,0:T(8,128)S(1)} %get-tuple-element.14.held_ref), channel_id=1, source_target_pairs={{0,1},{1,0},{2,3},{3,2},{4,5},{5,4},{6,7},{7,6},{8,9},{9,8},{10,11... | collective-permute-start | bytes 4718600 | tf_op jit(solution)/shard_map/ppermute | solution.py:165
  4.7 4.1 %collective-permute-start.2 = (f32[16,256]{1,0:T(8,128)S(1)}, f32[16,256]{1,0:T(8,128)S(1)}, u32[]{:S(2)}, u32[]{:S(2)}) collective-permute-start(f32[16,256]{1,0:T(8,128)S(1)} %constant_dynamic-slice_fusion.6), channel_id=1, source_target_pairs={{0,5},{1,4},{2,7},{3,6},{4,1},{5,0},{6,3},{7,2},{8,13},{9,12},{10,... | collective-permute-start | bytes 49160 | tf_op jit(solution)/shard_map/ppermute | solution.py:165
  8.8 3.2 %collective-permute-start.3 = (f32[16,256]{1,0:T(8,128)S(1)}, f32[16,256]{1,0:T(8,128)S(1)}, u32[]{:S(2)}, u32[]{:S(2)}) collective-permute-start(f32[16,256]{1,0:T(8,128)S(1)} %fusion.6), channel_id=1, source_target_pairs={{0,9},{1,2},{2,1},{3,10},{4,7},{5,12},{6,15},{7,4},{8,11},{9,0},{1... | collective-permute-start | bytes 49160 | tf_op jit(solution)/shard_map/ppermute | solution.py:165
  12.0 4.2 %collective-permute-start.4 = (f32[16,256]{1,0:T(8,128)S(1)}, f32[16,256]{1,0:T(8,128)S(1)}, u32[]{:S(2)}, u32[]{:S(2)}) collective-permute-start(f32[16,256]{1,0:T(8,128)S(1)} %max.42), channel_id=1, source_target_pairs={{0,17},{1,8},{2,11},{3,18},{4,13},{5,20},{6,23},{7,14},{8,1},{9,24... | collective-permute-start | bytes 49160 | tf_op jit(solution)/shard_map/ppermute | solution.py:165
  16.2 1.2 %collective-permute-start.5 = (f32[16,256]{1,0:T(8,128)S(1)}, f32[16,256]{1,0:T(8,128)S(1)}, u32[]{:S(2)}, u32[]{:S(2)}) collective-permute-start(f32[16,256]{1,0:T(8,128)S(1)} %get-tuple-element.17), channel_id=1, source_target_pairs={{0,1},{1,0},{2,3},{3,2},{4,5},{5,4},{6,7},{7,6},{8,9},{9,8},{10,11... | collective-permute-start | bytes 49160 | tf_op jit(solution)/shard_map/ppermute | solution.py:165
  18.4 3.3 %collective-permute-start.6 = (f32[24,256]{1,0:T(8,128)S(1)}, f32[24,256]{1,0:T(8,128)S(1)}, u32[]{:S(2)}, u32[]{:S(2)}) collective-permute-start(f32[24,256]{1,0:T(8,128)S(1)} %pad_maximum_fusion), channel_id=1, source_target_pairs={{0,5},{1,4},{2,7},{3,6},{4,1},{5,0},{6,3},{7,2},{8,13},{9,12},{10,... | collective-permute-start | bytes 73736 | tf_op jit(solution)/shard_map/ppermute | solution.py:165
  21.8 3.3 %collective-permute-start.7 = (f32[24,256]{1,0:T(8,128)S(1)}, f32[24,256]{1,0:T(8,128)S(1)}, u32[]{:S(2)}, u32[]{:S(2)}) collective-permute-start(f32[24,256]{1,0:T(8,128)S(1)} %pad_maximum_fusion.1), channel_id=1, source_target_pairs={{0,9},{1,8},{2,11},{3,10},{4,13},{5,12},{6,15},{7,14},{8,1},{9,0},... | collective-permute-start | bytes 73736 | tf_op jit(solution)/shard_map/ppermute | solution.py:165
  25.1 4.1 %collective-permute-start.8 = (f32[16,256]{1,0:T(8,128)S(1)}, f32[16,256]{1,0:T(8,128)S(1)}, u32[]{:S(2)}, u32[]{:S(2)}) collective-permute-start(f32[16,256]{1,0:T(8,128)S(1)} %constant_dynamic-slice_fusion), channel_id=1, source_target_pairs={{0,17},{1,16},{2,19},{3,18},{4,21},{5,20},{6,23},{7,22},{8,25},{9,... | collective-permute-start | bytes 49160 | tf_op jit(solution)/shard_map/ppermute | solution.py:165
  29.3 3.2 %collective-permute-start.9 = (f32[16,256]{1,0:T(8,128)S(1)}, f32[16,256]{1,0:T(8,128)S(1)}, u32[]{:S(2)}, u32[]{:S(2)}) collective-permute-start(f32[16,256]{1,0:T(8,128)S(1)} %constant_dynamic-slice_fusion.1), channel_id=1, source_target_pairs={{0,3},{1,2},{2,1},{3,0},{4,7},{5,6},{6,5},{7,4},{8,11},{9,10},{10,... | collective-permute-start | bytes 49160 | tf_op jit(solution)/shard_map/ppermute | solution.py:165

commit v8 on v7

--- a/solution.py
+++ b/solution.py
@@ -9,6 +9,7 @@
 
 ROWB = 4
 ITERS = 2
+PIECE = 2
 PARAMS = pltpu.CompilerParams(vmem_limit_bytes=16 << 20)
 BOTH = ("wide", "narrow")
 SMEM = pl.BlockSpec(memory_space=pltpu.SMEM)
@@ -41,14 +42,15 @@
     tiles_ref,
     rows_ref,
     cols_ref,
-    held_ref,
     peak_ref,
     places_ref,
-    sems,
+    *refs,
 ):
+    *held_refs, sems = refs
     slots = tiles_ref.shape[1]
+    held = [ref.at[s] for ref in held_refs for s in range(ref.shape[0])]
     moves = [(rows_in, rows_ref), (cols_in, cols_ref)]
-    moves += [(tiles_ref.at[0, s], held_ref.at[s]) for s in range(slots)]
+    moves += [(tiles_ref.at[0, s], held[s]) for s in range(slots)]
     copies = [
         pltpu.make_async_copy(source, target, sems.at[k])
         for k, (source, target) in enumerate(moves)
@@ -70,7 +72,7 @@
         for copy in copies[2 + first : 4 + first]:
             copy.wait()
         for s in range(first, min(first + 2, slots)):
-            size = jnp.abs(held_ref[s])
+            size = jnp.abs(held[s][...])
             found.append((s, jnp.max(size, axis=0, keepdims=True), lane_max(size)))
         for s, column_max, row_max in found:
             live = s < count_ref[0, 0]
@@ -85,22 +87,25 @@
     copy.wait()
 
 
-def next_kernel(
-    rows_ref, cols_ref, count_ref, mate_places, held_ref, mate_ref, old_ref, peak_ref, scale_ref
-):
-    slots, _, tile = held_ref.shape
+def next_kernel(row_blocks, rows_ref, cols_ref, count_ref, mate_places, old_ref, *refs):
+    *tile_refs, peak_ref, scale_ref, column_ref = refs
+    tiles = [ref.at[s] for ref in tile_refs for s in range(ref.shape[0])]
+    slots, tile = len(tiles) // 2, tiles[0].shape[0]
     half = tile // 2
     scale_ref[...] = lax.rsqrt(old_ref[...])
     peak_ref[...] = jnp.zeros_like(peak_ref)
-
-    def add(tiles_ref, count, places):
+    start = lax.axis_index("wide") * row_blocks
+    for k in range(row_blocks):
+        column_ref[k] = as_column(scale_ref[pl.ds(start + k, 1), :], half)
+
+    def add(tiles, count, places):
         found = []
-        for s, (row, col) in enumerate(places):
-            size = jnp.abs(tiles_ref[s])
+        for tile_ref, (row, col) in zip(tiles, places):
+            size = jnp.abs(tile_ref[...])
             left = scale_ref[pl.ds(row, 1), :]
             right = scale_ref[pl.ds(col, 1), :]
             row_max = lane_max(size * right) * left
-            column = as_column(left, half)
+            column = column_ref[row - start]
             below = jnp.concatenate(
                 [
                     jnp.max(size[:, :half] * column, axis=0, keepdims=True),
@@ -115,26 +120,15 @@
 
     given = [mate_places[0, k] for k in range(2 * slots + 1)]
     own = [(rows_ref[0, s], cols_ref[0, s]) for s in range(slots)]
-    add(held_ref, count_ref[0, 0], own)
-    add(mate_ref, given[0], list(zip(given[1::2], given[2::2])))
+    add(tiles[:slots], count_ref[0, 0], own)
+    add(tiles[slots:], given[0], list(zip(given[1::2], given[2::2])))
     peak_ref[...] = peak_ref[...] * old_ref[...]
 
 
-def last_kernel(
-    row_blocks,
-    rows_ref,
-    cols_ref,
-    count_ref,
-    held_ref,
-    old_ref,
-    out_ref,
-    own_out,
-    scale_ref,
-    own_ref,
-    done_ref,
-    sems,
-):
-    slots, _, tile = held_ref.shape
+def last_kernel(row_blocks, rows_ref, cols_ref, count_ref, old_ref, *refs):
+    *held_refs, out_ref, own_out, scale_ref, own_ref, done_ref, sems = refs
+    held = [ref.at[s] for ref in held_refs for s in range(ref.shape[0])]
+    slots, tile = len(held), held[0].shape[0]
     half = tile // 2
     scale_ref[...] = lax.rsqrt(old_ref[...])
     start = lax.axis_index("wide") * row_blocks
@@ -148,7 +142,7 @@
         right = scale_ref[pl.ds(cols_ref[0, s], 1), :]
         column = as_column(left, half)
         for part in (slice(0, half), slice(half, tile)):
-            scaled = held_ref[s, :, part] * column * right[:, part]
+            scaled = held[s][:, part] * column * right[:, part]
             done_ref[s, :, part] = jnp.where(live, scaled, 0.0)
         copies.append(pltpu.make_async_copy(done_ref.at[s], out_ref.at[0, s], sems.at[s]))
         copies[-1].start()
@@ -268,26 +262,27 @@
     slots, tile = tiles.shape[1], tiles.shape[2]
     blocks = ROWB * wide_size
     four = narrow_size == 4
-    rows, cols, held, part, index = pl.pallas_call(
+    sizes = [min(PIECE, slots - s) for s in range(0, slots, PIECE)]
+    rows, cols, part, index, *held = pl.pallas_call(
         first_kernel,
         out_shape=(
             pltpu.SMEM(tile_rows.shape, jnp.int32),
             pltpu.SMEM(tile_cols.shape, jnp.int32),
-            pltpu.VMEM((slots, tile, tile), jnp.float32),
             pltpu.VMEM((blocks, tile), jnp.float32),
             pltpu.VMEM((1, tile), jnp.float32),
+            *[pltpu.VMEM((size, tile, tile), jnp.float32) for size in sizes],
         ),
         in_specs=[SMEM, HBM, HBM, HBM],
-        out_specs=(SMEM, SMEM, VMEM, VMEM, VMEM),
+        out_specs=(SMEM, SMEM, VMEM, VMEM, *[VMEM for size in sizes]),
         scratch_shapes=[pltpu.SemaphoreType.DMA((2 + slots,))],
         compiler_params=PARAMS,
         name="first_peaks",
     )(tile_counts, *kept((tile_rows, tile_cols, tiles), pltpu.HBM))
     places = (*kept((rows, cols), pltpu.SMEM), tile_counts)
     part, index = swap_in_chip(part, index, wide_size, narrow_size)
-    part, sent = lax.optimization_barrier((part, held))
-    mate = swap(sent, lambda w, n: (w, n ^ 1), wide_size, narrow_size)
-    held = kept([held], pltpu.VMEM)
+    part, *sent = lax.optimization_barrier((part, *held))
+    mates = [swap(piece, lambda w, n: (w, n ^ 1), wide_size, narrow_size) for piece in sent]
+    held = kept(held, pltpu.VMEM)
     mate_places = pl.pallas_call(
         places_kernel,
         out_shape=pltpu.SMEM(index.shape, jnp.int32),
@@ -301,14 +296,17 @@
     for iteration in range(1, ITERS):
         full = (max_over_users if four else max_over_chips)(part, wide_size, narrow_size)
         part = pl.pallas_call(
-            next_kernel,
+            functools.partial(next_kernel, ROWB),
             out_shape=pltpu.VMEM((blocks, tile), jnp.float32),
-            in_specs=[SMEM] * 4 + [VMEM] * 3,
+            in_specs=[SMEM] * 4 + [VMEM] * (1 + 2 * len(held)),
             out_specs=VMEM,
-            scratch_shapes=[pltpu.VMEM((blocks, tile), jnp.float32)],
+            scratch_shapes=[
+                pltpu.VMEM((blocks, tile), jnp.float32),
+                pltpu.VMEM((ROWB, tile, tile // 2), jnp.float32),
+            ],
             compiler_params=PARAMS,
             name="next_peaks",
-        )(*places_too, *held, *kept([mate, full], pltpu.VMEM))
+        )(*places_too, *kept([full], pltpu.VMEM), *held, *kept(mates, pltpu.VMEM))
     full = (max_of_rows_too if four else max_over_chips)(part, wide_size, narrow_size)
     return pl.pallas_call(
         functools.partial(last_kernel, ROWB),
@@ -316,7 +314,7 @@
             jax.ShapeDtypeStruct(tiles.shape, jnp.float32),
             jax.ShapeDtypeStruct((ROWB, tile), jnp.float32),
         ),
-        in_specs=[SMEM] * 3 + [VMEM] * 2,
+        in_specs=[SMEM] * 3 + [VMEM] * (1 + len(held)),
         out_specs=(HBM, HBM),
         scratch_shapes=[
             pltpu.VMEM((blocks, tile), jnp.float32),
@@ -326,7 +324,7 @@
         ],
         compiler_params=PARAMS,
         name="scaled_tiles",
-    )(*places, *held, *kept([full], pltpu.VMEM))
+    )(*places, *kept([full], pltpu.VMEM), *held)
 
 
 def solution(mesh):

time: 34 us -> 33.6 us (0.988)
  waiting for transfers between devices: 12.2 us -> 11.3 us
  starting transfers between devices: 15.6 us -> 16.1 us
    ppermute x10 -> x12, waiting for transfers between devices: 12.2 us -> 11.3 us  [swap(): return lax.ppermute(values, BOTH, pairs)]
    ppermute x10 -> x12, starting transfers between devices: 15.6 us -> 16.1 us  [swap(): return lax.ppermute(values, BOTH, pairs)]
  transfers between devices with their start and end apart: 10 -> 12, of which waited for: 9 -> 9; matrix products, arithmetic and copies ran while one was open for 0% -> 0% of each run, Pallas kernels for 2% -> 2%
where the time goes in v8:
time: 33.6 us; the launch traced here: 33.4 us
  starting transfers between devices  16.1 us (48%)
  waiting for transfers between devices  11.3 us (34%)
  Pallas kernels  4.3 us (13%)
  between operations  1.45 us (4%)
    ppermute x12, starting transfers between devices, swap(): return lax.ppermute(values, BOTH, pairs)  16.1 us
    ppermute x12, waiting for transfers between devices, swap(): return lax.ppermute(values, BOTH, pairs)  11.3 us
    pallas_call x1, Pallas kernels, on_device(): pl.pallas_call(first_kernel, out_shape=(pltpu.SMEM(tile_rows.shape, jnp.i...  1.57 us
    pallas_call x1, Pallas kernels, on_device(): pl.pallas_call(functools.partial(last_kernel, ROWB), out_shape=(jax.Shape...  1.31 us
    pallas_call x1, Pallas kernels, on_device(): pl.pallas_call(functools.partial(next_kernel, ROWB), out_shape=pltpu.VMEM...  0.86 us
  transfers between devices with their start and end apart: 12, of which 9 were waited for; matrix products, arithmetic and copies ran while one was open for 0% of the time, Pallas kernels for 2%

profile of v8, /device:TPU:0, one launch (start us, length us, event | category | flops | bytes accessed | tf_op | source)
XLA Modules:
  0.0 33.4 jit_solution(12449952263669173859)
XLA Ops:
  1.3 1.6 %first_peaks.1 = (s32[1,6]{1,0:T(1,128)S(4)}, s32[1,6]{1,0:T(1,128)S(4)}, f32[32,256]{1,0:T(8,128)S(1)}, f32[1,256]{1,0:T(1,128)S(1)}, f32[2,256,256]{2,1,0:T(8,...) custom-call(s32[1,1]{1,0:T(1,128)S(6)} %copy.16.count_ref, s32[1,6]{1,0:T(1,128)} %rows_in.1, ...), custom_call_target="tpu_custom_call" | custom-call | tf_op jit(solution)/shard_map/first_peaks/pallas_call | solution.py:266
  2.9 0.5 %collective-permute-start = (f32[13,256]{1,0:T(8,128)S(1)}, f32[13,256]{1,0:T(8,128)S(1)}, u32[]{:S(2)}, u32[]{:S(2)}) collective-permute-start(f32[13,256]{1,0:T(8,128)S(1)} %pad_maximum_fusion.2), channel_id=1, source_target_pairs={{0,1},{1,0},{2,3},{3,2},{4,5},{5,4},{6,7},{7,6},{8,9},{9,8},{10,11... | collective-permute-start | bytes 39944 | tf_op jit(solution)/shard_map/ppermute | solution.py:159
  3.4 0.8 %collective-permute-done = f32[13,256]{1,0:T(8,128)S(1)} collective-permute-done((f32[13,256]{1,0:T(8,128)S(1)}, f32[13,256]{1,0:T(8,128)S(1)}, u32[]{:S(2)}, u32[]{:S(2)}) %collective-permute-start) | collective-permute-done | bytes 13344 | tf_op jit(solution)/shard_map/ppermute | solution.py:159
  4.3 2.7 %collective-permute-start.1 = (f32[16,256]{1,0:T(8,128)S(1)}, f32[16,256]{1,0:T(8,128)S(1)}, u32[]{:S(2)}, u32[]{:S(2)}) collective-permute-start(f32[16,256]{1,0:T(8,128)S(1)} %constant_dynamic-slice_fusion.6), channel_id=1, source_target_pairs={{0,5},{1,4},{2,7},{3,6},{4,1},{5,0},{6,3},{7,2},{8,13},{9,12},{10,... | collective-permute-start | bytes 49160 | tf_op jit(solution)/shard_map/ppermute | solution.py:159
  7.0 0.3 %collective-permute-start.5 = (f32[2,256,256]{2,1,0:T(8,128)S(1)}, f32[2,256,256]{2,1,0:T(8,128)S(1)}, u32[]{:S(2)}, u32[]{:S(2)}) collective-permute-start(f32[2,256,256]{2,1,0:T(8,128)S(1)} %get-tuple-element.21.refs_0_), channel_id=1, source_target_pairs={{0,1},{1,0},{2,3},{3,2},{4,5},{5,4},{6,7},{7,6},{8,9},{9,8},{10,11... | collective-permute-start | bytes 1572872 | tf_op jit(solution)/shard_map/ppermute | solution.py:159
  7.3 0.2 collective-permute-start.6
  7.5 0.3 %collective-permute-start.7 = (f32[2,256,256]{2,1,0:T(8,128)S(1)}, f32[2,256,256]{2,1,0:T(8,128)S(1)}, u32[]{:S(2)}, u32[]{:S(2)}) collective-permute-start(f32[2,256,256]{2,1,0:T(8,128)S(1)} %get-tuple-element.23.refs_2_), channel_id=1, source_target_pairs={{0,1},{1,0},{2,3},{3,2},{4,5},{5,4},{6,7},{7,6},{8,9},{9,8},{10,11... | collective-permute-start | bytes 1572872 | tf_op jit(solution)/shard_map/ppermute | solution.py:159
  7.9 0.6 %collective-permute-done.1 = f32[16,256]{1,0:T(8,128)S(1)} collective-permute-done((f32[16,256]{1,0:T(8,128)S(1)}, f32[16,256]{1,0:T(8,128)S(1)}, u32[]{:S(2)}, u32[]{:S(2)}) %collective-permute-start.1) | collective-permute-done | bytes 16416 | tf_op jit(solution)/shard_map/ppermute | solution.py:159
  8.4 1.8 %collective-permute-start.2 = (f32[16,256]{1,0:T(8,128)S(1)}, f32[16,256]{1,0:T(8,128)S(1)}, u32[]{:S(2)}, u32[]{:S(2)}) collective-permute-start(f32[16,256]{1,0:T(8,128)S(1)} %fusion.6), channel_id=1, source_target_pairs={{0,9},{1,2},{2,1},{3,10},{4,7},{5,12},{6,15},{7,4},{8,11},{9,0},{1... | collective-permute-start | bytes 49160 | tf_op jit(solution)/shard_map/ppermute | solution.py:159
  10.2 1.4 %collective-permute-done.2 = f32[16,256]{1,0:T(8,128)S(1)} collective-permute-done((f32[16,256]{1,0:T(8,128)S(1)}, f32[16,256]{1,0:T(8,128)S(1)}, u32[]{:S(2)}, u32[]{:S(2)}) %collective-permute-start.2) | collective-permute-done | bytes 16416 | tf_op jit(solution)/shard_map/ppermute | solution.py:159
  11.7 2.7 %collective-permute-start.3 = (f32[16,256]{1,0:T(8,128)S(1)}, f32[16,256]{1,0:T(8,128)S(1)}, u32[]{:S(2)}, u32[]{:S(2)}) collective-permute-start(f32[16,256]{1,0:T(8,128)S(1)} %max.42), channel_id=1, source_target_pairs={{0,17},{1,8},{2,11},{3,18},{4,13},{5,20},{6,23},{7,14},{8,1},{9,24... | collective-permute-start | bytes 49160 | tf_op jit(solution)/shard_map/ppermute | solution.py:159
  14.4 1.4 %collective-permute-done.3 = f32[16,256]{1,0:T(8,128)S(1)} collective-permute-done((f32[16,256]{1,0:T(8,128)S(1)}, f32[16,256]{1,0:T(8,128)S(1)}, u32[]{:S(2)}, u32[]{:S(2)}) %collective-permute-start.3) | collective-permute-done | bytes 16416 | tf_op jit(solution)/shard_map/ppermute | solution.py:159
  15.9 0.0 collective-permute-start.4
  15.9 0.6 %other_places.1.mate_places = s32[1,256]{1,0:T(1,128)S(4)} custom-call(f32[1,256]{1,0:T(1,128)S(1)} %slice.28.index_ref), custom_call_target="tpu_custom_call" | custom-call | tf_op jit(solution)/shard_map/other_places/pallas_call | solution.py:286
  16.5 0.6 %collective-permute-done.4 = f32[16,256]{1,0:T(8,128)S(1)} collective-permute-done((f32[16,256]{1,0:T(8,128)S(1)}, f32[16,256]{1,0:T(8,128)S(1)}, u32[]{:S(2)}, u32[]{:S(2)}) %collective-permute-start.4) | collective-permute-done | bytes 16416 | tf_op jit(solution)/shard_map/ppermute | solution.py:159
  17.0 0.0 collective-permute-done.5.refs_3_
  17.1 0.0 collective-permute-done.6.refs_4_
  17.1 0.0 collective-permute-done.7.refs_5_
  17.1 0.9 %next_peaks.1 = f32[32,256]{1,0:T(8,128)S(1)} custom-call(s32[1,6]{1,0:T(1,128)S(4)} %get-tuple-element.13.rows_ref, s32[1,6]{1,0:T(1,128)S(4)} %get-tuple-element.14.cols_ref, s32[1,1]{1,0:T(1,128)S(6)} %copy.16.count_ref, s32[1,256]{1,0:T(1,128)S(4)} %other_places.1.mate_places, f32[32,256]{1,0:T(8,128)S(1)} %maximum_dynamic-update-slice_fusion.2.old_ref, ...), custom_call_target="tpu_custom_call" | custom-call | tf_op jit(solution)/shard_map/next_peaks/pallas_call | solution.py:298
  18.0 1.6 %collective-permute-start.8 = (f32[24,256]{1,0:T(8,128)S(1)}, f32[24,256]{1,0:T(8,128)S(1)}, u32[]{:S(2)}, u32[]{:S(2)}) collective-permute-start(f32[24,256]{1,0:T(8,128)S(1)} %pad_maximum_fusion), channel_id=1, source_target_pairs={{0,5},{1,4},{2,7},{3,6},{4,1},{5,0},{6,3},{7,2},{8,13},{9,12},{10,... | collective-permute-start | bytes 73736 | tf_op jit(solution)/shard_map/ppermute | solution.py:159
  19.6 1.7 %collective-permute-done.8 = f32[24,256]{1,0:T(8,128)S(1)} collective-permute-done((f32[24,256]{1,0:T(8,128)S(1)}, f32[24,256]{1,0:T(8,128)S(1)}, u32[]{:S(2)}, u32[]{:S(2)}) %collective-permute-start.8) | collective-permute-done | bytes 24608 | tf_op jit(solution)/shard_map/ppermute | solution.py:159
  21.4 1.7 %collective-permute-start.9 = (f32[24,256]{1,0:T(8,128)S(1)}, f32[24,256]{1,0:T(8,128)S(1)}, u32[]{:S(2)}, u32[]{:S(2)}) collective-permute-start(f32[24,256]{1,0:T(8,128)S(1)} %pad_maximum_fusion.1), channel_id=1, source_target_pairs={{0,9},{1,8},{2,11},{3,10},{4,13},{5,12},{6,15},{7,14},{8,1},{9,0},... | collective-permute-start | bytes 73736 | tf_op jit(solution)/shard_map/ppermute | solution.py:159
  23.0 1.6 %collective-permute-done.9 = f32[24,256]{1,0:T(8,128)S(1)} collective-permute-done((f32[24,256]{1,0:T(8,128)S(1)}, f32[24,256]{1,0:T(8,128)S(1)}, u32[]{:S(2)}, u32[]{:S(2)}) %collective-permute-start.9) | collective-permute-done | bytes 24608 | tf_op jit(solution)/shard_map/ppermute | solution.py:159
  24.7 2.7 %collective-permute-start.10 = (f32[16,256]{1,0:T(8,128)S(1)}, f32[16,256]{1,0:T(8,128)S(1)}, u32[]{:S(2)}, u32[]{:S(2)}) collective-permute-start(f32[16,256]{1,0:T(8,128)S(1)} %constant_dynamic-slice_fusion), channel_id=1, source_target_pairs={{0,17},{1,16},{2,19},{3,18},{4,21},{5,20},{6,23},{7,22},{8,25},{9,... | collective-permute-start | bytes 49160 | tf_op jit(solution)/shard_map/ppermute | solution.py:159
  27.4 1.4 %collective-permute-done.10 = f32[16,256]{1,0:T(8,128)S(1)} collective-permute-done((f32[16,256]{1,0:T(8,128)S(1)}, f32[16,256]{1,0:T(8,128)S(1)}, u32[]{:S(2)}, u32[]{:S(2)}) %collective-permute-start.10) | collective-permute-done | bytes 16416 | tf_op jit(solution)/shard_map/ppermute | solution.py:159
  28.9 1.6 %collective-permute-start.11 = (f32[16,256]{1,0:T(8,128)S(1)}, f32[16,256]{1,0:T(8,128)S(1)}, u32[]{:S(2)}, u32[]{:S(2)}) collective-permute-start(f32[16,256]{1,0:T(8,128)S(1)} %constant_dynamic-slice_fusion.1), channel_id=1, source_target_pairs={{0,3},{1,2},{2,1},{3,0},{4,7},{5,6},{6,5},{7,4},{8,11},{9,10},{10,... | collective-permute-start | bytes 49160 | tf_op jit(solution)/shard_map/ppermute | solution.py:159
  30.4 1.6 %collective-permute-done.11 = f32[16,256]{1,0:T(8,128)S(1)} collective-permute-done((f32[16,256]{1,0:T(8,128)S(1)}, f32[16,256]{1,0:T(8,128)S(1)}, u32[]{:S(2)}, u32[]{:S(2)}) %collective-permute-start.11) | collective-permute-done | bytes 16416 | tf_op jit(solution)/shard_map/ppermute | solution.py:159
  32.1 1.3 %scaled_tiles.1 = (f32[1,6,256,256]{3,2,1,0:T(8,128)}, f32[4,256]{1,0:T(4,128)}) custom-call(s32[1,6]{1,0:T(1,128)S(4)} %get-tuple-element.13.rows_ref, s32[1,6]{1,0:T(1,128)S(4)} %get-tuple-element.14.cols_ref, s32[1,1]{1,0:T(1,128)S(6)} %copy.16.count_ref, f32[32,256]{1,0:T(8,128)S(1)} %maximum_dynamic-update-slice_fusion.old_ref, ...), custom_call_target="tpu_custom_call" | custom-call | tf_op jit(solution)/shard_map/scaled_tiles/pallas_call | solution.py:311
  (25 shorter events, 0.2 us)
Async XLA Ops:
  2.9 1.4 %collective-permute-start = (f32[13,256]{1,0:T(8,128)S(1)}, f32[13,256]{1,0:T(8,128)S(1)}, u32[]{:S(2)}, u32[]{:S(2)}) collective-permute-start(f32[13,256]{1,0:T(8,128)S(1)} %pad_maximum_fusion.2), channel_id=1, source_target_pairs={{0,1},{1,0},{2,3},{3,2},{4,5},{5,4},{6,7},{7,6},{8,9},{9,8},{10,11... | collective-permute-start | bytes 39944 | tf_op jit(solution)/shard_map/ppermute | solution.py:159
  4.3 4.1 %collective-permute-start.1 = (f32[16,256]{1,0:T(8,128)S(1)}, f32[16,256]{1,0:T(8,128)S(1)}, u32[]{:S(2)}, u32[]{:S(2)}) collective-permute-start(f32[16,256]{1,0:T(8,128)S(1)} %constant_dynamic-slice_fusion.6), channel_id=1, source_target_pairs={{0,5},{1,4},{2,7},{3,6},{4,1},{5,0},{6,3},{7,2},{8,13},{9,12},{10,... | collective-permute-start | bytes 49160 | tf_op jit(solution)/shard_map/ppermute | solution.py:159
  7.0 10.1 %collective-permute-start.5 = (f32[2,256,256]{2,1,0:T(8,128)S(1)}, f32[2,256,256]{2,1,0:T(8,128)S(1)}, u32[]{:S(2)}, u32[]{:S(2)}) collective-permute-start(f32[2,256,256]{2,1,0:T(8,128)S(1)} %get-tuple-element.21.refs_0_), channel_id=1, source_target_pairs={{0,1},{1,0},{2,3},{3,2},{4,5},{5,4},{6,7},{7,6},{8,9},{9,8},{10,11... | collective-permute-start | bytes 1572872 | tf_op jit(solution)/shard_map/ppermute | solution.py:159
  7.3 9.7 %collective-permute-start.6 = (f32[2,256,256]{2,1,0:T(8,128)S(1)}, f32[2,256,256]{2,1,0:T(8,128)S(1)}, u32[]{:S(2)}, u32[]{:S(2)}) collective-permute-start(f32[2,256,256]{2,1,0:T(8,128)S(1)} %get-tuple-element.22.refs_1_), channel_id=1, source_target_pairs={{0,1},{1,0},{2,3},{3,2},{4,5},{5,4},{6,7},{7,6},{8,9},{9,8},{10,11... | collective-permute-start | bytes 1572872 | tf_op jit(solution)/shard_map/ppermute | solution.py:159
  7.5 9.6 %collective-permute-start.7 = (f32[2,256,256]{2,1,0:T(8,128)S(1)}, f32[2,256,256]{2,1,0:T(8,128)S(1)}, u32[]{:S(2)}, u32[]{:S(2)}) collective-permute-start(f32[2,256,256]{2,1,0:T(8,128)S(1)} %get-tuple-element.23.refs_2_), channel_id=1, source_target_pairs={{0,1},{1,0},{2,3},{3,2},{4,5},{5,4},{6,7},{7,6},{8,9},{9,8},{10,11... | collective-permute-start | bytes 1572872 | tf_op jit(solution)/shard_map/ppermute | solution.py:159
  8.4 3.2 %collective-permute-start.2 = (f32[16,256]{1,0:T(8,128)S(1)}, f32[16,256]{1,0:T(8,128)S(1)}, u32[]{:S(2)}, u32[]{:S(2)}) collective-permute-start(f32[16,256]{1,0:T(8,128)S(1)} %fusion.6), channel_id=1, source_target_pairs={{0,9},{1,2},{2,1},{3,10},{4,7},{5,12},{6,15},{7,4},{8,11},{9,0},{1... | collective-permute-start | bytes 49160 | tf_op jit(solution)/shard_map/ppermute | solution.py:159
  11.7 4.2 %collective-permute-start.3 = (f32[16,256]{1,0:T(8,128)S(1)}, f32[16,256]{1,0:T(8,128)S(1)}, u32[]{:S(2)}, u32[]{:S(2)}) collective-permute-start(f32[16,256]{1,0:T(8,128)S(1)} %max.42), channel_id=1, source_target_pairs={{0,17},{1,8},{2,11},{3,18},{4,13},{5,20},{6,23},{7,14},{8,1},{9,24... | collective-permute-start | bytes 49160 | tf_op jit(solution)/shard_map/ppermute | solution.py:159
  15.9 1.2 %collective-permute-start.4 = (f32[16,256]{1,0:T(8,128)S(1)}, f32[16,256]{1,0:T(8,128)S(1)}, u32[]{:S(2)}, u32[]{:S(2)}) collective-permute-start(f32[16,256]{1,0:T(8,128)S(1)} %get-tuple-element.25), channel_id=1, source_target_pairs={{0,1},{1,0},{2,3},{3,2},{4,5},{5,4},{6,7},{7,6},{8,9},{9,8},{10,11... | collective-permute-start | bytes 49160 | tf_op jit(solution)/shard_map/ppermute | solution.py:159
  18.0 3.3 %collective-permute-start.8 = (f32[24,256]{1,0:T(8,128)S(1)}, f32[24,256]{1,0:T(8,128)S(1)}, u32[]{:S(2)}, u32[]{:S(2)}) collective-permute-start(f32[24,256]{1,0:T(8,128)S(1)} %pad_maximum_fusion), channel_id=1, source_target_pairs={{0,5},{1,4},{2,7},{3,6},{4,1},{5,0},{6,3},{7,2},{8,13},{9,12},{10,... | collective-permute-start | bytes 73736 | tf_op jit(solution)/shard_map/ppermute | solution.py:159
  21.4 3.3 %collective-permute-start.9 = (f32[24,256]{1,0:T(8,128)S(1)}, f32[24,256]{1,0:T(8,128)S(1)}, u32[]{:S(2)}, u32[]{:S(2)}) collective-permute-start(f32[24,256]{1,0:T(8,128)S(1)} %pad_maximum_fusion.1), channel_id=1, source_target_pairs={{0,9},{1,8},{2,11},{3,10},{4,13},{5,12},{6,15},{7,14},{8,1},{9,0},... | collective-permute-start | bytes 73736 | tf_op jit(solution)/shard_map/ppermute | solution.py:159
  24.7 4.1 %collective-permute-start.10 = (f32[16,256]{1,0:T(8,128)S(1)}, f32[16,256]{1,0:T(8,128)S(1)}, u32[]{:S(2)}, u32[]{:S(2)}) collective-permute-start(f32[16,256]{1,0:T(8,128)S(1)} %constant_dynamic-slice_fusion), channel_id=1, source_target_pairs={{0,17},{1,16},{2,19},{3,18},{4,21},{5,20},{6,23},{7,22},{8,25},{9,... | collective-permute-start | bytes 49160 | tf_op jit(solution)/shard_map/ppermute | solution.py:159
  28.9 3.2 %collective-permute-start.11 = (f32[16,256]{1,0:T(8,128)S(1)}, f32[16,256]{1,0:T(8,128)S(1)}, u32[]{:S(2)}, u32[]{:S(2)}) collective-permute-start(f32[16,256]{1,0:T(8,128)S(1)} %constant_dynamic-slice_fusion.1), channel_id=1, source_target_pairs={{0,3},{1,2},{2,1},{3,0},{4,7},{5,6},{6,5},{7,4},{8,11},{9,10},{10,... | collective-permute-start | bytes 49160 | tf_op jit(solution)/shard_map/ppermute | solution.py:159

commit v9 on v8

--- a/solution.py
+++ b/solution.py
@@ -125,17 +125,13 @@
     peak_ref[...] = peak_ref[...] * old_ref[...]
 
 
-def last_kernel(row_blocks, rows_ref, cols_ref, count_ref, old_ref, *refs):
-    *held_refs, out_ref, own_out, scale_ref, own_ref, done_ref, sems = refs
+def last_kernel(rows_ref, cols_ref, count_ref, old_ref, *refs):
+    *held_refs, out_ref, scale_ref, done_ref, sems = refs
     held = [ref.at[s] for ref in held_refs for s in range(ref.shape[0])]
     slots, tile = len(held), held[0].shape[0]
     half = tile // 2
     scale_ref[...] = lax.rsqrt(old_ref[...])
-    start = lax.axis_index("wide") * row_blocks
-    for k in range(row_blocks):
-        own_ref[pl.ds(k, 1), :] = scale_ref[pl.ds(start + k, 1), :]
-    copies = [pltpu.make_async_copy(own_ref, own_out, sems.at[slots])]
-    copies[0].start()
+    copies = []
     for s in range(slots):
         live = s < count_ref[0, 0]
         left = scale_ref[pl.ds(rows_ref[0, s], 1), :]
@@ -236,7 +232,8 @@
 def max_of_rows_too(values, wide_size, narrow_size):
     columns, rows, size = windows(values, wide_size, narrow_size)
     share, group_size = wide_size // narrow_size, size // 2
-    group = lax.axis_index("wide") // share
+    w, n = lax.axis_index("wide"), lax.axis_index("narrow")
+    group = w // share
     for bit in bits(1, wide_size // 2):
         group_start = (group if bit < share else group | 1) * group_size
         sent = jnp.concatenate(
@@ -248,14 +245,31 @@
         other = swap(sent, lambda w, n: (w ^ bit, n ^ 1), wide_size, narrow_size)
         values = window_max(values, columns, other[:size])
         values = window_max(values, group_start, other[size:])
-    for start, partner in (
-        (columns, lambda w, n: (w ^ wide_size // 2, n ^ 1)),
-        (rows, lambda w, n: (w, n ^ 3)),
-    ):
-        window = lax.dynamic_slice_in_dim(values, start, size, 0)
-        other = swap(window, partner, wide_size, narrow_size)
-        values = window_max(values, start, other)
-    return values
+    half = wide_size // 2
+    by_columns = swap(
+        lax.dynamic_slice_in_dim(values, columns, size, 0),
+        lambda w, n: (w ^ half if n > 1 else w, n ^ 1),
+        wide_size,
+        narrow_size,
+    )
+    by_rows = swap(
+        lax.dynamic_slice_in_dim(values, rows, size, 0),
+        lambda w, n: (w, n ^ 3 if w < half else n ^ 1),
+        wide_size,
+        narrow_size,
+    )
+    by_columns, by_rows = lax.optimization_barrier((by_columns, by_rows))
+    values = window_max(values, columns, by_columns)
+    row_start = w * ROWB
+    given = swap(
+        lax.dynamic_slice_in_dim(values, row_start, ROWB, 0),
+        lambda w, n: (w, n ^ 1 if w < half else n ^ 3),
+        wide_size,
+        narrow_size,
+    )
+    values = window_max(values, rows, by_rows)
+    own = lax.dynamic_slice_in_dim(values, row_start, ROWB, 0)
+    return values, jnp.where((w >= half) & (n < 2), given, own)
 
 
 def on_device(wide_size, narrow_size, tiles, tile_rows, tile_cols, tile_counts):
@@ -307,24 +321,28 @@
             compiler_params=PARAMS,
             name="next_peaks",
         )(*places_too, *kept([full], pltpu.VMEM), *held, *kept(mates, pltpu.VMEM))
-    full = (max_of_rows_too if four else max_over_chips)(part, wide_size, narrow_size)
-    return pl.pallas_call(
-        functools.partial(last_kernel, ROWB),
-        out_shape=(
-            jax.ShapeDtypeStruct(tiles.shape, jnp.float32),
-            jax.ShapeDtypeStruct((ROWB, tile), jnp.float32),
-        ),
+    if four:
+        full, own = max_of_rows_too(part, wide_size, narrow_size)
+    else:
+        full = max_over_chips(part, wide_size, narrow_size)
+        own = lax.dynamic_slice_in_dim(full, lax.axis_index("wide") * ROWB, ROWB, 0)
+    result = pl.pallas_call(
+        last_kernel,
+        out_shape=jax.ShapeDtypeStruct(tiles.shape, jnp.float32),
         in_specs=[SMEM] * 3 + [VMEM] * (1 + len(held)),
-        out_specs=(HBM, HBM),
+        out_specs=HBM,
         scratch_shapes=[
             pltpu.VMEM((blocks, tile), jnp.float32),
-            pltpu.VMEM((ROWB, tile), jnp.float32),
             pltpu.VMEM((slots, tile, tile), jnp.float32),
-            pltpu.SemaphoreType.DMA((slots + 1,)),
+            pltpu.SemaphoreType.DMA((slots,)),
         ],
+        cost_estimate=pl.CostEstimate(
+            flops=2 * tiles.size, bytes_accessed=8 * tiles.size, transcendentals=0
+        ),
         compiler_params=PARAMS,
         name="scaled_tiles",
     )(*places, *kept([full], pltpu.VMEM), *held)
+    return result, lax.rsqrt(own)
 
 
 def solution(mesh):

time: 33.6 us -> 32.2 us (0.958)
  the two profiles are of different devices: /device:TPU:0 before, /device:TPU:31 now
where the time goes in v9:
time: 32.2 us; the launch traced here: 32.1 us
  waiting for transfers between devices  20.1 us (62%)
  starting transfers between devices  5.42 us (17%)
  Pallas kernels  4.31 us (13%)
  between operations  1.44 us (4%)
  other arithmetic  0.69 us (2%)
    ppermute x13, waiting for transfers between devices, swap(): return lax.ppermute(values, BOTH, pairs)  20.1 us
    ppermute x13, starting transfers between devices, swap(): return lax.ppermute(values, BOTH, pairs)  5.42 us
    pallas_call x1, Pallas kernels, on_device(): pl.pallas_call(first_kernel, out_shape=(pltpu.SMEM(tile_rows.shape, jnp.i...  1.57 us
    pallas_call x1, Pallas kernels, on_device(): pl.pallas_call(last_kernel, out_shape=jax.ShapeDtypeStruct(tiles.shape, j...  1.31 us
    pallas_call x1, Pallas kernels, on_device(): pl.pallas_call(functools.partial(next_kernel, ROWB), out_shape=pltpu.VMEM...  0.87 us
  transfers between devices with their start and end apart: 13, of which 10 were waited for; matrix products, arithmetic and copies ran while one was open for 0% of the time, Pallas kernels for 6%

profile of v9, /device:TPU:31, one launch (start us, length us, event | category | flops | bytes accessed | tf_op | source)
XLA Modules:
  0.0 32.1 jit_solution(18443079892824737330)
XLA Ops:
  1.3 1.6 %first_peaks.1 = (s32[1,6]{1,0:T(1,128)S(4)}, s32[1,6]{1,0:T(1,128)S(4)}, f32[32,256]{1,0:T(8,128)S(1)}, f32[1,256]{1,0:T(1,128)S(1)}, f32[2,256,256]{2,1,0:T(8,...) custom-call(s32[1,1]{1,0:T(1,128)S(6)} %copy.16.count_ref, s32[1,6]{1,0:T(1,128)} %rows_in.1, ...), custom_call_target="tpu_custom_call" | custom-call | tf_op jit(solution)/shard_map/first_peaks/pallas_call | solution.py:280
  2.9 0.7 %collective-permute-start = (f32[13,256]{1,0:T(8,128)S(1)}, f32[13,256]{1,0:T(8,128)S(1)}, u32[]{:S(2)}, u32[]{:S(2)}) collective-permute-start(f32[13,256]{1,0:T(8,128)S(1)} %pad_maximum_fusion.2), channel_id=1, source_target_pairs={{0,1},{1,0},{2,3},{3,2},{4,5},{5,4},{6,7},{7,6},{8,9},{9,8},{10,11... | collective-permute-start | bytes 39944 | tf_op jit(solution)/shard_map/ppermute | solution.py:155
  3.7 0.8 %collective-permute-done = f32[13,256]{1,0:T(8,128)S(1)} collective-permute-done((f32[13,256]{1,0:T(8,128)S(1)}, f32[13,256]{1,0:T(8,128)S(1)}, u32[]{:S(2)}, u32[]{:S(2)}) %collective-permute-start) | collective-permute-done | bytes 13344 | tf_op jit(solution)/shard_map/ppermute | solution.py:155
  4.5 0.5 %collective-permute-start.1 = (f32[16,256]{1,0:T(8,128)S(1)}, f32[16,256]{1,0:T(8,128)S(1)}, u32[]{:S(2)}, u32[]{:S(2)}) collective-permute-start(f32[16,256]{1,0:T(8,128)S(1)} %constant_dynamic-slice_fusion.8), channel_id=1, source_target_pairs={{0,5},{1,4},{2,7},{3,6},{4,1},{5,0},{6,3},{7,2},{8,13},{9,12},{10,... | collective-permute-start | bytes 49160 | tf_op jit(solution)/shard_map/ppermute | solution.py:155
  5.0 0.2 collective-permute-start.5
  5.2 0.3 %collective-permute-start.6 = (f32[2,256,256]{2,1,0:T(8,128)S(1)}, f32[2,256,256]{2,1,0:T(8,128)S(1)}, u32[]{:S(2)}, u32[]{:S(2)}) collective-permute-start(f32[2,256,256]{2,1,0:T(8,128)S(1)} %get-tuple-element.24.refs_1_), channel_id=1, source_target_pairs={{0,1},{1,0},{2,3},{3,2},{4,5},{5,4},{6,7},{7,6},{8,9},{9,8},{10,11... | collective-permute-start | bytes 1572872 | tf_op jit(solution)/shard_map/ppermute | solution.py:155
  5.6 0.2 collective-permute-start.7
  5.7 2.0 %collective-permute-done.1 = f32[16,256]{1,0:T(8,128)S(1)} collective-permute-done((f32[16,256]{1,0:T(8,128)S(1)}, f32[16,256]{1,0:T(8,128)S(1)}, u32[]{:S(2)}, u32[]{:S(2)}) %collective-permute-start.1) | collective-permute-done | bytes 16416 | tf_op jit(solution)/shard_map/ppermute | solution.py:155
  7.8 0.5 %collective-permute-start.2 = (f32[16,256]{1,0:T(8,128)S(1)}, f32[16,256]{1,0:T(8,128)S(1)}, u32[]{:S(2)}, u32[]{:S(2)}) collective-permute-start(f32[16,256]{1,0:T(8,128)S(1)} %fusion.8), channel_id=1, source_target_pairs={{0,9},{1,2},{2,1},{3,10},{4,7},{5,12},{6,15},{7,4},{8,11},{9,0},{1... | collective-permute-start | bytes 49160 | tf_op jit(solution)/shard_map/ppermute | solution.py:155
  8.2 2.7 %collective-permute-done.2 = f32[16,256]{1,0:T(8,128)S(1)} collective-permute-done((f32[16,256]{1,0:T(8,128)S(1)}, f32[16,256]{1,0:T(8,128)S(1)}, u32[]{:S(2)}, u32[]{:S(2)}) %collective-permute-start.2) | collective-permute-done | bytes 16416 | tf_op jit(solution)/shard_map/ppermute | solution.py:155
  10.9 0.4 %collective-permute-start.3 = (f32[16,256]{1,0:T(8,128)S(1)}, f32[16,256]{1,0:T(8,128)S(1)}, u32[]{:S(2)}, u32[]{:S(2)}) collective-permute-start(f32[16,256]{1,0:T(8,128)S(1)} %max.42), channel_id=1, source_target_pairs={{0,17},{1,8},{2,11},{3,18},{4,13},{5,20},{6,23},{7,14},{8,1},{9,24... | collective-permute-start | bytes 49160 | tf_op jit(solution)/shard_map/ppermute | solution.py:155
  11.3 2.8 %collective-permute-done.3 = f32[16,256]{1,0:T(8,128)S(1)} collective-permute-done((f32[16,256]{1,0:T(8,128)S(1)}, f32[16,256]{1,0:T(8,128)S(1)}, u32[]{:S(2)}, u32[]{:S(2)}) %collective-permute-start.3) | collective-permute-done | bytes 16416 | tf_op jit(solution)/shard_map/ppermute | solution.py:155
  14.1 1.2 %collective-permute-start.4 = (f32[16,256]{1,0:T(8,128)S(1)}, f32[16,256]{1,0:T(8,128)S(1)}, u32[]{:S(2)}, u32[]{:S(2)}) collective-permute-start(f32[16,256]{1,0:T(8,128)S(1)} %get-tuple-element.29), channel_id=1, source_target_pairs={{0,1},{1,0},{2,3},{3,2},{4,5},{5,4},{6,7},{7,6},{8,9},{9,8},{10,11... | collective-permute-start | bytes 49160 | tf_op jit(solution)/shard_map/ppermute | solution.py:155
  15.4 0.6 %other_places.1.mate_places = s32[1,256]{1,0:T(1,128)S(4)} custom-call(f32[1,256]{1,0:T(1,128)S(1)} %slice.28.index_ref), custom_call_target="tpu_custom_call" | custom-call | tf_op jit(solution)/shard_map/other_places/pallas_call | solution.py:300
  15.9 0.3 collective-permute-done.4
  16.2 0.0 collective-permute-done.5.refs_3_
  16.2 0.0 collective-permute-done.6.refs_4_
  16.2 0.0 collective-permute-done.7.refs_5_
  16.2 0.9 %next_peaks.1 = f32[32,256]{1,0:T(8,128)S(1)} custom-call(s32[1,6]{1,0:T(1,128)S(4)} %get-tuple-element.15.rows_ref, s32[1,6]{1,0:T(1,128)S(4)} %get-tuple-element.16.cols_ref, s32[1,1]{1,0:T(1,128)S(6)} %copy.16.count_ref, s32[1,256]{1,0:T(1,128)S(4)} %other_places.1.mate_places, f32[32,256]{1,0:T(8,128)S(1)} %maximum_dynamic-update-slice_fusion.2.old_ref, ...), custom_call_target="tpu_custom_call" | custom-call | tf_op jit(solution)/shard_map/next_peaks/pallas_call | solution.py:312
  17.1 0.3 %collective-permute-start.8 = (f32[24,256]{1,0:T(8,128)S(1)}, f32[24,256]{1,0:T(8,128)S(1)}, u32[]{:S(2)}, u32[]{:S(2)}) collective-permute-start(f32[24,256]{1,0:T(8,128)S(1)} %pad_maximum_fusion), channel_id=1, source_target_pairs={{0,5},{1,4},{2,7},{3,6},{4,1},{5,0},{6,3},{7,2},{8,13},{9,12},{10,... | collective-permute-start | bytes 73736 | tf_op jit(solution)/shard_map/ppermute | solution.py:155
  17.5 3.0 %collective-permute-done.8 = f32[24,256]{1,0:T(8,128)S(1)} collective-permute-done((f32[24,256]{1,0:T(8,128)S(1)}, f32[24,256]{1,0:T(8,128)S(1)}, u32[]{:S(2)}, u32[]{:S(2)}) %collective-permute-start.8) | collective-permute-done | bytes 24608 | tf_op jit(solution)/shard_map/ppermute | solution.py:155
  20.5 0.3 collective-permute-start.9
  20.8 3.0 %collective-permute-done.9 = f32[24,256]{1,0:T(8,128)S(1)} collective-permute-done((f32[24,256]{1,0:T(8,128)S(1)}, f32[24,256]{1,0:T(8,128)S(1)}, u32[]{:S(2)}, u32[]{:S(2)}) %collective-permute-start.9) | collective-permute-done | bytes 24608 | tf_op jit(solution)/shard_map/ppermute | solution.py:155
  23.9 0.4 %collective-permute-start.11 = (f32[16,256]{1,0:T(8,128)S(1)}, f32[16,256]{1,0:T(8,128)S(1)}, u32[]{:S(2)}, u32[]{:S(2)}) collective-permute-start(f32[16,256]{1,0:T(8,128)S(1)} %get-tuple-element.30), channel_id=1, source_target_pairs={{0,3},{1,2},{2,1},{3,0},{4,7},{5,6},{6,5},{7,4},{8,11},{9,10},{10,... | collective-permute-start | bytes 49160 | tf_op jit(solution)/shard_map/ppermute | solution.py:155
  24.3 0.2 collective-permute-start.10
  24.5 0.6 %collective-permute-done.11 = f32[16,256]{1,0:T(8,128)S(1)} collective-permute-done((f32[16,256]{1,0:T(8,128)S(1)}, f32[16,256]{1,0:T(8,128)S(1)}, u32[]{:S(2)}, u32[]{:S(2)}) %collective-permute-start.11) | collective-permute-done | bytes 16416 | tf_op jit(solution)/shard_map/ppermute | solution.py:155
  25.1 3.2 %collective-permute-done.10 = f32[16,256]{1,0:T(8,128)S(1)} collective-permute-done((f32[16,256]{1,0:T(8,128)S(1)}, f32[16,256]{1,0:T(8,128)S(1)}, u32[]{:S(2)}, u32[]{:S(2)}) %collective-permute-start.10) | collective-permute-done | bytes 16416 | tf_op jit(solution)/shard_map/ppermute | solution.py:155
  28.4 0.1 collective-permute-start.12
  28.5 1.3 %scaled_tiles.1 = f32[1,6,256,256]{3,2,1,0:T(8,128)} custom-call(s32[1,6]{1,0:T(1,128)S(4)} %get-tuple-element.15.rows_ref, s32[1,6]{1,0:T(1,128)S(4)} %get-tuple-element.16.cols_ref, s32[1,1]{1,0:T(1,128)S(6)} %copy.16.count_ref, f32[32,256]{1,0:T(8,128)S(1)} %maximum_dynamic-update-slice_fusion.old_ref, f32[2,256,256]{2,1,0:T(8,128)S(1)} %get-tuple-element.23.refs_0_, ...), custom_call_target="tpu_custom_call" | custom-call | flops 786432 | bytes 3145728 | tf_op jit(solution)/shard_map/scaled_tiles/pallas_call | solution.py:329
  29.8 1.7 %collective-permute-done.12 = f32[4,256]{1,0:T(4,128)S(1)} collective-permute-done((f32[4,256]{1,0:T(4,128)S(1)}, f32[4,256]{1,0:T(4,128)S(1)}, u32[]{:S(2)}, u32[]{:S(2)}) %collective-permute-start.12) | collective-permute-done | bytes 4128 | tf_op jit(solution)/shard_map/ppermute | solution.py:155
  31.5 0.6 %fusion.7 = f32[4,256]{1,0:T(4,128)} fusion(f32[4,256]{1,0:T(4,128)S(1)} %collective-permute-done.12, f32[32,256]{1,0:T(8,128)S(1)} %maximum_dynamic-update-slice_fusion.old_ref, s32[]{:T(128)S(6)} %select_n.76, pred[]{:T(512)S(6)} %and.25), kind=kLoop, calls=%fused_computation.32 | loop fusion | flops 1024 | bytes 12293 | tf_op jit(solution)/shard_map/rsqrt | solution.py:345
  (25 shorter events, 0.2 us)
Async XLA Ops:
  2.9 1.6 %collective-permute-start = (f32[13,256]{1,0:T(8,128)S(1)}, f32[13,256]{1,0:T(8,128)S(1)}, u32[]{:S(2)}, u32[]{:S(2)}) collective-permute-start(f32[13,256]{1,0:T(8,128)S(1)} %pad_maximum_fusion.2), channel_id=1, source_target_pairs={{0,1},{1,0},{2,3},{3,2},{4,5},{5,4},{6,7},{7,6},{8,9},{9,8},{10,11... | collective-permute-start | bytes 39944 | tf_op jit(solution)/shard_map/ppermute | solution.py:155
  4.5 3.2 %collective-permute-start.1 = (f32[16,256]{1,0:T(8,128)S(1)}, f32[16,256]{1,0:T(8,128)S(1)}, u32[]{:S(2)}, u32[]{:S(2)}) collective-permute-start(f32[16,256]{1,0:T(8,128)S(1)} %constant_dynamic-slice_fusion.8), channel_id=1, source_target_pairs={{0,5},{1,4},{2,7},{3,6},{4,1},{5,0},{6,3},{7,2},{8,13},{9,12},{10,... | collective-permute-start | bytes 49160 | tf_op jit(solution)/shard_map/ppermute | solution.py:155
  5.0 11.1 %collective-permute-start.5 = (f32[2,256,256]{2,1,0:T(8,128)S(1)}, f32[2,256,256]{2,1,0:T(8,128)S(1)}, u32[]{:S(2)}, u32[]{:S(2)}) collective-permute-start(f32[2,256,256]{2,1,0:T(8,128)S(1)} %get-tuple-element.23.refs_0_), channel_id=1, source_target_pairs={{0,1},{1,0},{2,3},{3,2},{4,5},{5,4},{6,7},{7,6},{8,9},{9,8},{10,11... | collective-permute-start | bytes 1572872 | tf_op jit(solution)/shard_map/ppermute | solution.py:155
  5.2 11.0 %collective-permute-start.6 = (f32[2,256,256]{2,1,0:T(8,128)S(1)}, f32[2,256,256]{2,1,0:T(8,128)S(1)}, u32[]{:S(2)}, u32[]{:S(2)}) collective-permute-start(f32[2,256,256]{2,1,0:T(8,128)S(1)} %get-tuple-element.24.refs_1_), channel_id=1, source_target_pairs={{0,1},{1,0},{2,3},{3,2},{4,5},{5,4},{6,7},{7,6},{8,9},{9,8},{10,11... | collective-permute-start | bytes 1572872 | tf_op jit(solution)/shard_map/ppermute | solution.py:155
  5.6 10.6 %collective-permute-start.7 = (f32[2,256,256]{2,1,0:T(8,128)S(1)}, f32[2,256,256]{2,1,0:T(8,128)S(1)}, u32[]{:S(2)}, u32[]{:S(2)}) collective-permute-start(f32[2,256,256]{2,1,0:T(8,128)S(1)} %get-tuple-element.25.refs_2_), channel_id=1, source_target_pairs={{0,1},{1,0},{2,3},{3,2},{4,5},{5,4},{6,7},{7,6},{8,9},{9,8},{10,11... | collective-permute-start | bytes 1572872 | tf_op jit(solution)/shard_map/ppermute | solution.py:155
  7.8 3.2 %collective-permute-start.2 = (f32[16,256]{1,0:T(8,128)S(1)}, f32[16,256]{1,0:T(8,128)S(1)}, u32[]{:S(2)}, u32[]{:S(2)}) collective-permute-start(f32[16,256]{1,0:T(8,128)S(1)} %fusion.8), channel_id=1, source_target_pairs={{0,9},{1,2},{2,1},{3,10},{4,7},{5,12},{6,15},{7,4},{8,11},{9,0},{1... | collective-permute-start | bytes 49160 | tf_op jit(solution)/shard_map/ppermute | solution.py:155
  10.9 3.2 %collective-permute-start.3 = (f32[16,256]{1,0:T(8,128)S(1)}, f32[16,256]{1,0:T(8,128)S(1)}, u32[]{:S(2)}, u32[]{:S(2)}) collective-permute-start(f32[16,256]{1,0:T(8,128)S(1)} %max.42), channel_id=1, source_target_pairs={{0,17},{1,8},{2,11},{3,18},{4,13},{5,20},{6,23},{7,14},{8,1},{9,24... | collective-permute-start | bytes 49160 | tf_op jit(solution)/shard_map/ppermute | solution.py:155
  14.1 2.1 %collective-permute-start.4 = (f32[16,256]{1,0:T(8,128)S(1)}, f32[16,256]{1,0:T(8,128)S(1)}, u32[]{:S(2)}, u32[]{:S(2)}) collective-permute-start(f32[16,256]{1,0:T(8,128)S(1)} %get-tuple-element.29), channel_id=1, source_target_pairs={{0,1},{1,0},{2,3},{3,2},{4,5},{5,4},{6,7},{7,6},{8,9},{9,8},{10,11... | collective-permute-start | bytes 49160 | tf_op jit(solution)/shard_map/ppermute | solution.py:155
  17.1 3.3 %collective-permute-start.8 = (f32[24,256]{1,0:T(8,128)S(1)}, f32[24,256]{1,0:T(8,128)S(1)}, u32[]{:S(2)}, u32[]{:S(2)}) collective-permute-start(f32[24,256]{1,0:T(8,128)S(1)} %pad_maximum_fusion), channel_id=1, source_target_pairs={{0,5},{1,4},{2,7},{3,6},{4,1},{5,0},{6,3},{7,2},{8,13},{9,12},{10,... | collective-permute-start | bytes 73736 | tf_op jit(solution)/shard_map/ppermute | solution.py:155
  20.5 3.3 %collective-permute-start.9 = (f32[24,256]{1,0:T(8,128)S(1)}, f32[24,256]{1,0:T(8,128)S(1)}, u32[]{:S(2)}, u32[]{:S(2)}) collective-permute-start(f32[24,256]{1,0:T(8,128)S(1)} %pad_maximum_fusion.1), channel_id=1, source_target_pairs={{0,9},{1,8},{2,11},{3,10},{4,13},{5,12},{6,15},{7,14},{8,1},{9,0},... | collective-permute-start | bytes 73736 | tf_op jit(solution)/shard_map/ppermute | solution.py:155
  23.9 1.3 %collective-permute-start.11 = (f32[16,256]{1,0:T(8,128)S(1)}, f32[16,256]{1,0:T(8,128)S(1)}, u32[]{:S(2)}, u32[]{:S(2)}) collective-permute-start(f32[16,256]{1,0:T(8,128)S(1)} %get-tuple-element.30), channel_id=1, source_target_pairs={{0,3},{1,2},{2,1},{3,0},{4,7},{5,6},{6,5},{7,4},{8,11},{9,10},{10,... | collective-permute-start | bytes 49160 | tf_op jit(solution)/shard_map/ppermute | solution.py:155
  24.3 4.1 %collective-permute-start.10 = (f32[16,256]{1,0:T(8,128)S(1)}, f32[16,256]{1,0:T(8,128)S(1)}, u32[]{:S(2)}, u32[]{:S(2)}) collective-permute-start(f32[16,256]{1,0:T(8,128)S(1)} %get-tuple-element.31), channel_id=1, source_target_pairs={{0,1},{1,0},{2,19},{3,18},{4,5},{5,4},{6,23},{7,22},{8,9},{9,8},{1... | collective-permute-start | bytes 49160 | tf_op jit(solution)/shard_map/ppermute | solution.py:155
  28.4 3.1 %collective-permute-start.12 = (f32[4,256]{1,0:T(4,128)S(1)}, f32[4,256]{1,0:T(4,128)S(1)}, u32[]{:S(2)}, u32[]{:S(2)}) collective-permute-start(f32[4,256]{1,0:T(4,128)S(1)} %constant_dynamic-slice_fusion.7), channel_id=1, source_target_pairs={{0,1},{1,0},{2,3},{3,2},{4,5},{5,4},{6,7},{7,6},{8,9},{9,8},{10,11... | collective-permute-start | bytes 12296 | tf_op jit(solution)/shard_map/ppermute | solution.py:155

commit v10 on v9

--- a/solution.py
+++ b/solution.py
@@ -125,13 +125,17 @@
     peak_ref[...] = peak_ref[...] * old_ref[...]
 
 
-def last_kernel(rows_ref, cols_ref, count_ref, old_ref, *refs):
-    *held_refs, out_ref, scale_ref, done_ref, sems = refs
+def last_kernel(row_blocks, rows_ref, cols_ref, count_ref, old_ref, *refs):
+    *held_refs, out_ref, own_out, scale_ref, own_ref, done_ref, sems = refs
     held = [ref.at[s] for ref in held_refs for s in range(ref.shape[0])]
     slots, tile = len(held), held[0].shape[0]
     half = tile // 2
     scale_ref[...] = lax.rsqrt(old_ref[...])
-    copies = []
+    start = lax.axis_index("wide") * row_blocks
+    for k in range(row_blocks):
+        own_ref[pl.ds(k, 1), :] = scale_ref[pl.ds(start + k, 1), :]
+    copies = [pltpu.make_async_copy(own_ref, own_out, sems.at[slots])]
+    copies[0].start()
     for s in range(slots):
         live = s < count_ref[0, 0]
         left = scale_ref[pl.ds(rows_ref[0, s], 1), :]
@@ -146,6 +150,18 @@
         copy.wait()
 
 
+def given_kernel(half, given_ref, own_ref, out_ref, scale_ref, sem):
+    del own_ref
+    w, n = lax.axis_index("wide"), lax.axis_index("narrow")
+
+    @pl.when((w >= half) & (n < 2))
+    def _():
+        scale_ref[...] = lax.rsqrt(given_ref[...])
+        copy = pltpu.make_async_copy(scale_ref, out_ref, sem.at[0])
+        copy.start()
+        copy.wait()
+
+
 def swap(values, partner, wide_size, narrow_size):
     pairs = []
     for w in range(wide_size):
@@ -201,40 +217,12 @@
 
 
 def max_over_users(values, wide_size, narrow_size):
-    share = wide_size // narrow_size
-
-    def along_columns(w, n):
-        lane = n ^ n >> 1
-        for bit in bits(1, wide_size):
-            lane = lane ^ w // bit
-        return lane & 1 == 0
-
-    def first(w, n):
-        return (w ^ share, n ^ 1) if along_columns(w, n) else (w, n ^ 3)
-
-    def second(w, n):
-        return (w ^ 2 * share if along_columns(w, n) else w ^ share, n ^ 1)
-
-    columns, rows, size = windows(values, wide_size, narrow_size)
-    chosen = along_columns(lax.axis_index("wide"), lax.axis_index("narrow"))
-    start = jnp.where(chosen, columns, rows)
-    window = lax.dynamic_slice_in_dim(values, start, size, 0)
-    for bit in bits(1, share):
-        other = swap(window, lambda w, n: (w ^ bit, n ^ 1), wide_size, narrow_size)
-        window = jnp.maximum(window, other)
-    for partner in (first, second):
-        window = jnp.maximum(window, swap(window, partner, wide_size, narrow_size))
-    other = swap(window, lambda w, n: (w, n ^ 1), wide_size, narrow_size)
-    values = window_max(values, start, window)
-    return window_max(values, jnp.where(chosen, rows, columns), other)
-
-
-def max_of_rows_too(values, wide_size, narrow_size):
     columns, rows, size = windows(values, wide_size, narrow_size)
     share, group_size = wide_size // narrow_size, size // 2
+    half = wide_size // 2
     w, n = lax.axis_index("wide"), lax.axis_index("narrow")
     group = w // share
-    for bit in bits(1, wide_size // 2):
+    for bit in bits(1, half):
         group_start = (group if bit < share else group | 1) * group_size
         sent = jnp.concatenate(
             [
@@ -245,7 +233,6 @@
         other = swap(sent, lambda w, n: (w ^ bit, n ^ 1), wide_size, narrow_size)
         values = window_max(values, columns, other[:size])
         values = window_max(values, group_start, other[size:])
-    half = wide_size // 2
     by_columns = swap(
         lax.dynamic_slice_in_dim(values, columns, size, 0),
         lambda w, n: (w ^ half if n > 1 else w, n ^ 1),
@@ -259,17 +246,15 @@
         narrow_size,
     )
     by_columns, by_rows = lax.optimization_barrier((by_columns, by_rows))
-    values = window_max(values, columns, by_columns)
-    row_start = w * ROWB
-    given = swap(
-        lax.dynamic_slice_in_dim(values, row_start, ROWB, 0),
-        lambda w, n: (w, n ^ 1 if w < half else n ^ 3),
-        wide_size,
-        narrow_size,
-    )
-    values = window_max(values, rows, by_rows)
-    own = lax.dynamic_slice_in_dim(values, row_start, ROWB, 0)
-    return values, jnp.where((w >= half) & (n < 2), given, own)
+    merged = window_max(values, columns, by_columns)
+
+    def rows_too():
+        own = lax.dynamic_slice_in_dim(merged, w * ROWB, ROWB, 0)
+        return swap(
+            own, lambda w, n: (w, n ^ 1 if w < half else n ^ 3), wide_size, narrow_size
+        )
+
+    return window_max(merged, rows, by_rows), rows_too
 
 
 def on_device(wide_size, narrow_size, tiles, tile_rows, tile_cols, tile_counts):
@@ -308,7 +293,10 @@
     )(*kept([index], pltpu.VMEM))
     places_too = (*places, *kept([mate_places], pltpu.SMEM))
     for iteration in range(1, ITERS):
-        full = (max_over_users if four else max_over_chips)(part, wide_size, narrow_size)
+        if four:
+            full, _ = max_over_users(part, wide_size, narrow_size)
+        else:
+            full = max_over_chips(part, wide_size, narrow_size)
         part = pl.pallas_call(
             functools.partial(next_kernel, ROWB),
             out_shape=pltpu.VMEM((blocks, tile), jnp.float32),
@@ -322,19 +310,20 @@
             name="next_peaks",
         )(*places_too, *kept([full], pltpu.VMEM), *held, *kept(mates, pltpu.VMEM))
     if four:
-        full, own = max_of_rows_too(part, wide_size, narrow_size)
+        full, rows_too = max_over_users(part, wide_size, narrow_size)
     else:
         full = max_over_chips(part, wide_size, narrow_size)
-        own = lax.dynamic_slice_in_dim(full, lax.axis_index("wide") * ROWB, ROWB, 0)
-    result = pl.pallas_call(
-        last_kernel,
-        out_shape=jax.ShapeDtypeStruct(tiles.shape, jnp.float32),
+    own_shape = jax.ShapeDtypeStruct((ROWB, tile), jnp.float32)
+    result, own = pl.pallas_call(
+        functools.partial(last_kernel, ROWB),
+        out_shape=(jax.ShapeDtypeStruct(tiles.shape, jnp.float32), own_shape),
         in_specs=[SMEM] * 3 + [VMEM] * (1 + len(held)),
-        out_specs=HBM,
+        out_specs=(HBM, HBM),
         scratch_shapes=[
             pltpu.VMEM((blocks, tile), jnp.float32),
+            pltpu.VMEM((ROWB, tile), jnp.float32),
             pltpu.VMEM((slots, tile, tile), jnp.float32),
-            pltpu.SemaphoreType.DMA((slots,)),
+            pltpu.SemaphoreType.DMA((slots + 1,)),
         ],
         cost_estimate=pl.CostEstimate(
             flops=2 * tiles.size, bytes_accessed=8 * tiles.size, transcendentals=0
@@ -342,7 +331,21 @@
         compiler_params=PARAMS,
         name="scaled_tiles",
     )(*places, *kept([full], pltpu.VMEM), *held)
-    return result, lax.rsqrt(own)
+    if four:
+        own = pl.pallas_call(
+            functools.partial(given_kernel, wide_size // 2),
+            out_shape=own_shape,
+            in_specs=[VMEM, HBM],
+            out_specs=HBM,
+            scratch_shapes=[
+                pltpu.VMEM((ROWB, tile), jnp.float32),
+                pltpu.SemaphoreType.DMA((1,)),
+            ],
+            input_output_aliases={1: 0},
+            compiler_params=PARAMS,
+            name="given_scaling",
+        )(*kept([rows_too()], pltpu.VMEM), own)
+    return result, own
 
 
 def solution(mesh):

time: 32.2 us -> 31.5 us (0.978)
  the two profiles are of different devices: /device:TPU:31 before, /device:TPU:25 now
where the time goes in v10:
time: 31.5 us; the launch traced here: 31.3 us
  starting transfers between devices  13.6 us (43%)
  waiting for transfers between devices  11 us (35%)
  Pallas kernels  4.94 us (16%)
  between operations  1.5 us (5%)
    ppermute x13, starting transfers between devices, swap(): return lax.ppermute(values, BOTH, pairs)  13.6 us
    ppermute x13, waiting for transfers between devices, swap(): return lax.ppermute(values, BOTH, pairs)  11 us
    pallas_call x1, Pallas kernels, on_device(): pl.pallas_call(first_kernel, out_shape=(pltpu.SMEM(tile_rows.shape, jnp.i...  1.57 us
    pallas_call x1, Pallas kernels, on_device(): pl.pallas_call(functools.partial(last_kernel, ROWB), out_shape=(jax.Shape...  1.31 us
    pallas_call x1, Pallas kernels, on_device(): pl.pallas_call(functools.partial(next_kernel, ROWB), out_shape=pltpu.VMEM...  0.87 us
  transfers between devices with their start and end apart: 13, of which 9 were waited for; matrix products, arithmetic and copies ran while one was open for 0% of the time, Pallas kernels for 6%

profile of v10, /device:TPU:25, one launch (start us, length us, event | category | flops | bytes accessed | tf_op | source)
XLA Modules:
  0.0 31.3 jit_solution(13370055125676675043)
XLA Ops:
  1.3 1.6 %first_peaks.1 = (s32[1,6]{1,0:T(1,128)S(4)}, s32[1,6]{1,0:T(1,128)S(4)}, f32[32,256]{1,0:T(8,128)S(1)}, f32[1,256]{1,0:T(1,128)S(1)}, f32[2,256,256]{2,1,0:T(8,...) custom-call(s32[1,1]{1,0:T(1,128)S(6)} %copy.22.count_ref, s32[1,6]{1,0:T(1,128)} %rows_in.1, ...), custom_call_target="tpu_custom_call" | custom-call | tf_op jit(solution)/shard_map/first_peaks/pallas_call | solution.py:265
  2.9 0.7 %collective-permute-start = (f32[13,256]{1,0:T(8,128)S(1)}, f32[13,256]{1,0:T(8,128)S(1)}, u32[]{:S(2)}, u32[]{:S(2)}) collective-permute-start(f32[13,256]{1,0:T(8,128)S(1)} %pad_maximum_fusion.4), channel_id=1, source_target_pairs={{0,1},{1,0},{2,3},{3,2},{4,5},{5,4},{6,7},{7,6},{8,9},{9,8},{10,11... | collective-permute-start | bytes 39944 | tf_op jit(solution)/shard_map/ppermute | solution.py:171
  3.7 0.8 %collective-permute-done = f32[13,256]{1,0:T(8,128)S(1)} collective-permute-done((f32[13,256]{1,0:T(8,128)S(1)}, f32[13,256]{1,0:T(8,128)S(1)}, u32[]{:S(2)}, u32[]{:S(2)}) %collective-permute-start) | collective-permute-done | bytes 13344 | tf_op jit(solution)/shard_map/ppermute | solution.py:171
  4.6 1.5 %collective-permute-start.1 = (f32[24,256]{1,0:T(8,128)S(1)}, f32[24,256]{1,0:T(8,128)S(1)}, u32[]{:S(2)}, u32[]{:S(2)}) collective-permute-start(f32[24,256]{1,0:T(8,128)S(1)} %pad_maximum_fusion), channel_id=1, source_target_pairs={{0,5},{1,4},{2,7},{3,6},{4,1},{5,0},{6,3},{7,2},{8,13},{9,12},{10,... | collective-permute-start | bytes 73736 | tf_op jit(solution)/shard_map/ppermute | solution.py:171
  6.1 1.8 %collective-permute-done.1 = f32[24,256]{1,0:T(8,128)S(1)} collective-permute-done((f32[24,256]{1,0:T(8,128)S(1)}, f32[24,256]{1,0:T(8,128)S(1)}, u32[]{:S(2)}, u32[]{:S(2)}) %collective-permute-start.1) | collective-permute-done | bytes 24608 | tf_op jit(solution)/shard_map/ppermute | solution.py:171
  7.9 0.5 %collective-permute-start.2 = (f32[24,256]{1,0:T(8,128)S(1)}, f32[24,256]{1,0:T(8,128)S(1)}, u32[]{:S(2)}, u32[]{:S(2)}) collective-permute-start(f32[24,256]{1,0:T(8,128)S(1)} %pad_maximum_fusion.1), channel_id=1, source_target_pairs={{0,9},{1,8},{2,11},{3,10},{4,13},{5,12},{6,15},{7,14},{8,1},{9,0},... | collective-permute-start | bytes 73736 | tf_op jit(solution)/shard_map/ppermute | solution.py:171
  8.4 0.2 collective-permute-start.5
  8.6 0.3 %collective-permute-start.6 = (f32[2,256,256]{2,1,0:T(8,128)S(1)}, f32[2,256,256]{2,1,0:T(8,128)S(1)}, u32[]{:S(2)}, u32[]{:S(2)}) collective-permute-start(f32[2,256,256]{2,1,0:T(8,128)S(1)} %get-tuple-element.30.refs_1_), channel_id=1, source_target_pairs={{0,1},{1,0},{2,3},{3,2},{4,5},{5,4},{6,7},{7,6},{8,9},{9,8},{10,11... | collective-permute-start | bytes 1572872 | tf_op jit(solution)/shard_map/ppermute | solution.py:171
  8.9 0.2 collective-permute-start.7
  9.1 2.2 %collective-permute-done.2 = f32[24,256]{1,0:T(8,128)S(1)} collective-permute-done((f32[24,256]{1,0:T(8,128)S(1)}, f32[24,256]{1,0:T(8,128)S(1)}, u32[]{:S(2)}, u32[]{:S(2)}) %collective-permute-start.2) | collective-permute-done | bytes 24608 | tf_op jit(solution)/shard_map/ppermute | solution.py:171
  11.3 0.4 %collective-permute-start.4 = (f32[16,256]{1,0:T(8,128)S(1)}, f32[16,256]{1,0:T(8,128)S(1)}, u32[]{:S(2)}, u32[]{:S(2)}) collective-permute-start(f32[16,256]{1,0:T(8,128)S(1)} %get-tuple-element.38), channel_id=1, source_target_pairs={{0,3},{1,2},{2,1},{3,0},{4,7},{5,6},{6,5},{7,4},{8,11},{9,10},{10,... | collective-permute-start | bytes 49160 | tf_op jit(solution)/shard_map/ppermute | solution.py:171
  11.7 0.2 collective-permute-start.3
  11.9 0.6 %other_places.1.mate_places = s32[1,256]{1,0:T(1,128)S(4)} custom-call(f32[1,256]{1,0:T(1,128)S(1)} %slice.44.index_ref), custom_call_target="tpu_custom_call" | custom-call | tf_op jit(solution)/shard_map/other_places/pallas_call | solution.py:285
  12.4 0.1 collective-permute-done.4
  12.5 0.3 %collective-permute-done.3 = f32[16,256]{1,0:T(8,128)S(1)} collective-permute-done((f32[16,256]{1,0:T(8,128)S(1)}, f32[16,256]{1,0:T(8,128)S(1)}, u32[]{:S(2)}, u32[]{:S(2)}) %collective-permute-start.3) | collective-permute-done | bytes 16416 | tf_op jit(solution)/shard_map/ppermute | solution.py:171
  12.9 0.0 collective-permute-done.5.refs_3_
  12.9 0.0 collective-permute-done.6.refs_4_
  12.9 0.0 collective-permute-done.7.refs_5_
  12.9 0.9 %next_peaks.1 = f32[32,256]{1,0:T(8,128)S(1)} custom-call(s32[1,6]{1,0:T(1,128)S(4)} %get-tuple-element.19.rows_ref, s32[1,6]{1,0:T(1,128)S(4)} %get-tuple-element.20.cols_ref, s32[1,1]{1,0:T(1,128)S(6)} %copy.22.count_ref, s32[1,256]{1,0:T(1,128)S(4)} %other_places.1.mate_places, f32[32,256]{1,0:T(8,128)S(1)} %maximum_dynamic-update-slice_fusion.2.old_ref, ...), custom_call_target="tpu_custom_call" | custom-call | tf_op jit(solution)/shard_map/next_peaks/pallas_call | solution.py:300
  13.8 1.4 %collective-permute-start.8 = (f32[24,256]{1,0:T(8,128)S(1)}, f32[24,256]{1,0:T(8,128)S(1)}, u32[]{:S(2)}, u32[]{:S(2)}) collective-permute-start(f32[24,256]{1,0:T(8,128)S(1)} %pad_maximum_fusion.2), channel_id=1, source_target_pairs={{0,5},{1,4},{2,7},{3,6},{4,1},{5,0},{6,3},{7,2},{8,13},{9,12},{10,... | collective-permute-start | bytes 73736 | tf_op jit(solution)/shard_map/ppermute | solution.py:171
  15.2 2.0 %collective-permute-done.8 = f32[24,256]{1,0:T(8,128)S(1)} collective-permute-done((f32[24,256]{1,0:T(8,128)S(1)}, f32[24,256]{1,0:T(8,128)S(1)}, u32[]{:S(2)}, u32[]{:S(2)}) %collective-permute-start.8) | collective-permute-done | bytes 24608 | tf_op jit(solution)/shard_map/ppermute | solution.py:171
  17.2 0.4 %collective-permute-start.9 = (f32[24,256]{1,0:T(8,128)S(1)}, f32[24,256]{1,0:T(8,128)S(1)}, u32[]{:S(2)}, u32[]{:S(2)}) collective-permute-start(f32[24,256]{1,0:T(8,128)S(1)} %pad_maximum_fusion.3), channel_id=1, source_target_pairs={{0,9},{1,8},{2,11},{3,10},{4,13},{5,12},{6,15},{7,14},{8,1},{9,0},... | collective-permute-start | bytes 73736 | tf_op jit(solution)/shard_map/ppermute | solution.py:171
  17.6 2.9 %collective-permute-done.9 = f32[24,256]{1,0:T(8,128)S(1)} collective-permute-done((f32[24,256]{1,0:T(8,128)S(1)}, f32[24,256]{1,0:T(8,128)S(1)}, u32[]{:S(2)}, u32[]{:S(2)}) %collective-permute-start.9) | collective-permute-done | bytes 24608 | tf_op jit(solution)/shard_map/ppermute | solution.py:171
  20.6 0.2 collective-permute-start.11
  20.8 0.3 %collective-permute-start.10 = (f32[16,256]{1,0:T(8,128)S(1)}, f32[16,256]{1,0:T(8,128)S(1)}, u32[]{:S(2)}, u32[]{:S(2)}) collective-permute-start(f32[16,256]{1,0:T(8,128)S(1)} %get-tuple-element.37), channel_id=1, source_target_pairs={{0,1},{1,0},{2,19},{3,18},{4,5},{5,4},{6,23},{7,22},{8,9},{9,8},{1... | collective-permute-start | bytes 49160 | tf_op jit(solution)/shard_map/ppermute | solution.py:171
  21.1 0.7 %collective-permute-done.11 = f32[16,256]{1,0:T(8,128)S(1)} collective-permute-done((f32[16,256]{1,0:T(8,128)S(1)}, f32[16,256]{1,0:T(8,128)S(1)}, u32[]{:S(2)}, u32[]{:S(2)}) %collective-permute-start.11) | collective-permute-done | bytes 16416 | tf_op jit(solution)/shard_map/ppermute | solution.py:171
  21.8 0.2 collective-permute-done.10
  22.0 7.3 %collective-permute-start.12 = (f32[4,256]{1,0:T(4,128)S(1)}, f32[4,256]{1,0:T(4,128)S(1)}, u32[]{:S(2)}, u32[]{:S(2)}) collective-permute-start(f32[4,256]{1,0:T(4,128)S(1)} %constant_dynamic-slice_fusion), channel_id=1, source_target_pairs={{0,1},{1,0},{2,3},{3,2},{4,5},{5,4},{6,7},{7,6},{8,9},{9,8},{10,11... | collective-permute-start | bytes 12296 | tf_op jit(solution)/shard_map/ppermute | solution.py:171
  29.3 1.3 %scaled_tiles.1 = (f32[1,6,256,256]{3,2,1,0:T(8,128)}, f32[4,256]{1,0:T(4,128)}) custom-call(s32[1,6]{1,0:T(1,128)S(4)} %get-tuple-element.19.rows_ref, s32[1,6]{1,0:T(1,128)S(4)} %get-tuple-element.20.cols_ref, s32[1,1]{1,0:T(1,128)S(6)} %copy.22.count_ref, f32[32,256]{1,0:T(8,128)S(1)} %maximum_dynamic-update-slice_fusion.old_ref, ...), custom_call_target="tpu_custom_call" | custom-call | flops 786432 | bytes 3145728 | tf_op jit(solution)/shard_map/scaled_tiles/pallas_call | solution.py:317
  30.7 0.0 collective-permute-done.12.given_ref
  30.7 0.6 %given_scaling.1 = f32[4,256]{1,0:T(4,128)} custom-call(f32[4,256]{1,0:T(4,128)S(1)} %collective-permute-done.12.given_ref, f32[4,256]{1,0:T(4,128)} %get-tuple-element.35.own_ref), custom_call_target="tpu_custom_call", output_to_operand_aliasing={{}: (1, {})} | custom-call | tf_op jit(solution)/shard_map/given_scaling/pallas_call | solution.py:335
  (33 shorter events, 0.2 us)
Async XLA Ops:
  2.9 1.6 %collective-permute-start = (f32[13,256]{1,0:T(8,128)S(1)}, f32[13,256]{1,0:T(8,128)S(1)}, u32[]{:S(2)}, u32[]{:S(2)}) collective-permute-start(f32[13,256]{1,0:T(8,128)S(1)} %pad_maximum_fusion.4), channel_id=1, source_target_pairs={{0,1},{1,0},{2,3},{3,2},{4,5},{5,4},{6,7},{7,6},{8,9},{9,8},{10,11... | collective-permute-start | bytes 39944 | tf_op jit(solution)/shard_map/ppermute | solution.py:171
  4.6 3.3 %collective-permute-start.1 = (f32[24,256]{1,0:T(8,128)S(1)}, f32[24,256]{1,0:T(8,128)S(1)}, u32[]{:S(2)}, u32[]{:S(2)}) collective-permute-start(f32[24,256]{1,0:T(8,128)S(1)} %pad_maximum_fusion), channel_id=1, source_target_pairs={{0,5},{1,4},{2,7},{3,6},{4,1},{5,0},{6,3},{7,2},{8,13},{9,12},{10,... | collective-permute-start | bytes 73736 | tf_op jit(solution)/shard_map/ppermute | solution.py:171
  7.9 3.3 %collective-permute-start.2 = (f32[24,256]{1,0:T(8,128)S(1)}, f32[24,256]{1,0:T(8,128)S(1)}, u32[]{:S(2)}, u32[]{:S(2)}) collective-permute-start(f32[24,256]{1,0:T(8,128)S(1)} %pad_maximum_fusion.1), channel_id=1, source_target_pairs={{0,9},{1,8},{2,11},{3,10},{4,13},{5,12},{6,15},{7,14},{8,1},{9,0},... | collective-permute-start | bytes 73736 | tf_op jit(solution)/shard_map/ppermute | solution.py:171
  8.4 4.5 %collective-permute-start.5 = (f32[2,256,256]{2,1,0:T(8,128)S(1)}, f32[2,256,256]{2,1,0:T(8,128)S(1)}, u32[]{:S(2)}, u32[]{:S(2)}) collective-permute-start(f32[2,256,256]{2,1,0:T(8,128)S(1)} %get-tuple-element.29.refs_0_), channel_id=1, source_target_pairs={{0,1},{1,0},{2,3},{3,2},{4,5},{5,4},{6,7},{7,6},{8,9},{9,8},{10,11... | collective-permute-start | bytes 1572872 | tf_op jit(solution)/shard_map/ppermute | solution.py:171
  8.6 4.3 %collective-permute-start.6 = (f32[2,256,256]{2,1,0:T(8,128)S(1)}, f32[2,256,256]{2,1,0:T(8,128)S(1)}, u32[]{:S(2)}, u32[]{:S(2)}) collective-permute-start(f32[2,256,256]{2,1,0:T(8,128)S(1)} %get-tuple-element.30.refs_1_), channel_id=1, source_target_pairs={{0,1},{1,0},{2,3},{3,2},{4,5},{5,4},{6,7},{7,6},{8,9},{9,8},{10,11... | collective-permute-start | bytes 1572872 | tf_op jit(solution)/shard_map/ppermute | solution.py:171
  8.9 4.0 %collective-permute-start.7 = (f32[2,256,256]{2,1,0:T(8,128)S(1)}, f32[2,256,256]{2,1,0:T(8,128)S(1)}, u32[]{:S(2)}, u32[]{:S(2)}) collective-permute-start(f32[2,256,256]{2,1,0:T(8,128)S(1)} %get-tuple-element.31.refs_2_), channel_id=1, source_target_pairs={{0,1},{1,0},{2,3},{3,2},{4,5},{5,4},{6,7},{7,6},{8,9},{9,8},{10,11... | collective-permute-start | bytes 1572872 | tf_op jit(solution)/shard_map/ppermute | solution.py:171
  11.3 1.2 %collective-permute-start.4 = (f32[16,256]{1,0:T(8,128)S(1)}, f32[16,256]{1,0:T(8,128)S(1)}, u32[]{:S(2)}, u32[]{:S(2)}) collective-permute-start(f32[16,256]{1,0:T(8,128)S(1)} %get-tuple-element.38), channel_id=1, source_target_pairs={{0,3},{1,2},{2,1},{3,0},{4,7},{5,6},{6,5},{7,4},{8,11},{9,10},{10,... | collective-permute-start | bytes 49160 | tf_op jit(solution)/shard_map/ppermute | solution.py:171
  11.7 1.2 %collective-permute-start.3 = (f32[16,256]{1,0:T(8,128)S(1)}, f32[16,256]{1,0:T(8,128)S(1)}, u32[]{:S(2)}, u32[]{:S(2)}) collective-permute-start(f32[16,256]{1,0:T(8,128)S(1)} %get-tuple-element.39), channel_id=1, source_target_pairs={{0,1},{1,0},{2,19},{3,18},{4,5},{5,4},{6,23},{7,22},{8,9},{9,8},{1... | collective-permute-start | bytes 49160 | tf_op jit(solution)/shard_map/ppermute | solution.py:171
  13.8 3.3 %collective-permute-start.8 = (f32[24,256]{1,0:T(8,128)S(1)}, f32[24,256]{1,0:T(8,128)S(1)}, u32[]{:S(2)}, u32[]{:S(2)}) collective-permute-start(f32[24,256]{1,0:T(8,128)S(1)} %pad_maximum_fusion.2), channel_id=1, source_target_pairs={{0,5},{1,4},{2,7},{3,6},{4,1},{5,0},{6,3},{7,2},{8,13},{9,12},{10,... | collective-permute-start | bytes 73736 | tf_op jit(solution)/shard_map/ppermute | solution.py:171
  17.2 3.3 %collective-permute-start.9 = (f32[24,256]{1,0:T(8,128)S(1)}, f32[24,256]{1,0:T(8,128)S(1)}, u32[]{:S(2)}, u32[]{:S(2)}) collective-permute-start(f32[24,256]{1,0:T(8,128)S(1)} %pad_maximum_fusion.3), channel_id=1, source_target_pairs={{0,9},{1,8},{2,11},{3,10},{4,13},{5,12},{6,15},{7,14},{8,1},{9,0},... | collective-permute-start | bytes 73736 | tf_op jit(solution)/shard_map/ppermute | solution.py:171
  20.6 1.2 %collective-permute-start.11 = (f32[16,256]{1,0:T(8,128)S(1)}, f32[16,256]{1,0:T(8,128)S(1)}, u32[]{:S(2)}, u32[]{:S(2)}) collective-permute-start(f32[16,256]{1,0:T(8,128)S(1)} %get-tuple-element.36), channel_id=1, source_target_pairs={{0,3},{1,2},{2,1},{3,0},{4,7},{5,6},{6,5},{7,4},{8,11},{9,10},{10,... | collective-permute-start | bytes 49160 | tf_op jit(solution)/shard_map/ppermute | solution.py:171
  20.8 1.2 %collective-permute-start.10 = (f32[16,256]{1,0:T(8,128)S(1)}, f32[16,256]{1,0:T(8,128)S(1)}, u32[]{:S(2)}, u32[]{:S(2)}) collective-permute-start(f32[16,256]{1,0:T(8,128)S(1)} %get-tuple-element.37), channel_id=1, source_target_pairs={{0,1},{1,0},{2,19},{3,18},{4,5},{5,4},{6,23},{7,22},{8,9},{9,8},{1... | collective-permute-start | bytes 49160 | tf_op jit(solution)/shard_map/ppermute | solution.py:171
  22.0 8.7 %collective-permute-start.12 = (f32[4,256]{1,0:T(4,128)S(1)}, f32[4,256]{1,0:T(4,128)S(1)}, u32[]{:S(2)}, u32[]{:S(2)}) collective-permute-start(f32[4,256]{1,0:T(4,128)S(1)} %constant_dynamic-slice_fusion), channel_id=1, source_target_pairs={{0,1},{1,0},{2,3},{3,2},{4,5},{5,4},{6,7},{7,6},{8,9},{9,8},{10,11... | collective-permute-start | bytes 12296 | tf_op jit(solution)/shard_map/ppermute | solution.py:171

commit v11 on v10

--- a/solution.py
+++ b/solution.py
@@ -216,7 +216,7 @@
     return columns, rows, size
 
 
-def max_over_users(values, wide_size, narrow_size):
+def max_over_users(values, wide_size, narrow_size, idle):
     columns, rows, size = windows(values, wide_size, narrow_size)
     share, group_size = wide_size // narrow_size, size // 2
     half = wide_size // 2
@@ -241,7 +241,7 @@
     )
     by_rows = swap(
         lax.dynamic_slice_in_dim(values, rows, size, 0),
-        lambda w, n: (w, n ^ 3 if w < half else n ^ 1),
+        lambda w, n: (w, n ^ (3 if w < half else idle)),
         wide_size,
         narrow_size,
     )
@@ -294,7 +294,7 @@
     places_too = (*places, *kept([mate_places], pltpu.SMEM))
     for iteration in range(1, ITERS):
         if four:
-            full, _ = max_over_users(part, wide_size, narrow_size)
+            full, _ = max_over_users(part, wide_size, narrow_size, 1)
         else:
             full = max_over_chips(part, wide_size, narrow_size)
         part = pl.pallas_call(
@@ -310,7 +310,7 @@
             name="next_peaks",
         )(*places_too, *kept([full], pltpu.VMEM), *held, *kept(mates, pltpu.VMEM))
     if four:
-        full, rows_too = max_over_users(part, wide_size, narrow_size)
+        full, rows_too = max_over_users(part, wide_size, narrow_size, 3)
     else:
         full = max_over_chips(part, wide_size, narrow_size)
     own_shape = jax.ShapeDtypeStruct((ROWB, tile), jnp.float32)

time: 31.5 us -> 31.2 us (level)
  starting transfers between devices: 13.6 us -> 13.1 us
    ppermute x13, starting transfers between devices: 13.6 us -> 13.1 us  [swap(): return lax.ppermute(values, BOTH, pairs)]
  transfers between devices with their start and end apart: 13 -> 13, of which waited for: 9 -> 8; matrix products, arithmetic and copies ran while one was open for 0% -> 0% of each run, Pallas kernels for 6% -> 6%
where the time goes in v11:
time: 31.2 us; the launch traced here: 31 us
  starting transfers between devices  13.1 us (42%)
  waiting for transfers between devices  11.2 us (36%)
  Pallas kernels  4.94 us (16%)
  between operations  1.51 us (5%)
    ppermute x13, starting transfers between devices, swap(): return lax.ppermute(values, BOTH, pairs)  13.1 us
    ppermute x13, waiting for transfers between devices, swap(): return lax.ppermute(values, BOTH, pairs)  11.2 us
    pallas_call x1, Pallas kernels, on_device(): pl.pallas_call(first_kernel, out_shape=(pltpu.SMEM(tile_rows.shape, jnp.i...  1.57 us
    pallas_call x1, Pallas kernels, on_device(): pl.pallas_call(functools.partial(last_kernel, ROWB), out_shape=(jax.Shape...  1.31 us
    pallas_call x1, Pallas kernels, on_device(): pl.pallas_call(functools.partial(next_kernel, ROWB), out_shape=pltpu.VMEM...  0.87 us
  transfers between devices with their start and end apart: 13, of which 8 were waited for; matrix products, arithmetic and copies ran while one was open for 0% of the time, Pallas kernels for 6%

profile of v11, /device:TPU:25, one launch (start us, length us, event | category | flops | bytes accessed | tf_op | source)
XLA Modules:
  0.0 31.0 jit_solution(7694369231353970115)
XLA Ops:
  1.3 1.6 %first_peaks.1 = (s32[1,6]{1,0:T(1,128)S(4)}, s32[1,6]{1,0:T(1,128)S(4)}, f32[32,256]{1,0:T(8,128)S(1)}, f32[1,256]{1,0:T(1,128)S(1)}, f32[2,256,256]{2,1,0:T(8,...) custom-call(s32[1,1]{1,0:T(1,128)S(6)} %copy.22.count_ref, s32[1,6]{1,0:T(1,128)} %rows_in.1, ...), custom_call_target="tpu_custom_call" | custom-call | tf_op jit(solution)/shard_map/first_peaks/pallas_call | solution.py:265
  2.9 0.7 %collective-permute-start = (f32[13,256]{1,0:T(8,128)S(1)}, f32[13,256]{1,0:T(8,128)S(1)}, u32[]{:S(2)}, u32[]{:S(2)}) collective-permute-start(f32[13,256]{1,0:T(8,128)S(1)} %pad_maximum_fusion.4), channel_id=1, source_target_pairs={{0,1},{1,0},{2,3},{3,2},{4,5},{5,4},{6,7},{7,6},{8,9},{9,8},{10,11... | collective-permute-start | bytes 39944 | tf_op jit(solution)/shard_map/ppermute | solution.py:171
  3.7 0.8 %collective-permute-done = f32[13,256]{1,0:T(8,128)S(1)} collective-permute-done((f32[13,256]{1,0:T(8,128)S(1)}, f32[13,256]{1,0:T(8,128)S(1)}, u32[]{:S(2)}, u32[]{:S(2)}) %collective-permute-start) | collective-permute-done | bytes 13344 | tf_op jit(solution)/shard_map/ppermute | solution.py:171
  4.6 1.5 %collective-permute-start.1 = (f32[24,256]{1,0:T(8,128)S(1)}, f32[24,256]{1,0:T(8,128)S(1)}, u32[]{:S(2)}, u32[]{:S(2)}) collective-permute-start(f32[24,256]{1,0:T(8,128)S(1)} %pad_maximum_fusion), channel_id=1, source_target_pairs={{0,5},{1,4},{2,7},{3,6},{4,1},{5,0},{6,3},{7,2},{8,13},{9,12},{10,... | collective-permute-start | bytes 73736 | tf_op jit(solution)/shard_map/ppermute | solution.py:171
  6.1 1.8 %collective-permute-done.1 = f32[24,256]{1,0:T(8,128)S(1)} collective-permute-done((f32[24,256]{1,0:T(8,128)S(1)}, f32[24,256]{1,0:T(8,128)S(1)}, u32[]{:S(2)}, u32[]{:S(2)}) %collective-permute-start.1) | collective-permute-done | bytes 24608 | tf_op jit(solution)/shard_map/ppermute | solution.py:171
  7.9 0.5 %collective-permute-start.2 = (f32[24,256]{1,0:T(8,128)S(1)}, f32[24,256]{1,0:T(8,128)S(1)}, u32[]{:S(2)}, u32[]{:S(2)}) collective-permute-start(f32[24,256]{1,0:T(8,128)S(1)} %pad_maximum_fusion.1), channel_id=1, source_target_pairs={{0,9},{1,8},{2,11},{3,10},{4,13},{5,12},{6,15},{7,14},{8,1},{9,0},... | collective-permute-start | bytes 73736 | tf_op jit(solution)/shard_map/ppermute | solution.py:171
  8.4 0.2 collective-permute-start.5
  8.6 0.3 %collective-permute-start.6 = (f32[2,256,256]{2,1,0:T(8,128)S(1)}, f32[2,256,256]{2,1,0:T(8,128)S(1)}, u32[]{:S(2)}, u32[]{:S(2)}) collective-permute-start(f32[2,256,256]{2,1,0:T(8,128)S(1)} %get-tuple-element.30.refs_1_), channel_id=1, source_target_pairs={{0,1},{1,0},{2,3},{3,2},{4,5},{5,4},{6,7},{7,6},{8,9},{9,8},{10,11... | collective-permute-start | bytes 1572872 | tf_op jit(solution)/shard_map/ppermute | solution.py:171
  8.9 0.2 collective-permute-start.7
  9.1 2.2 %collective-permute-done.2 = f32[24,256]{1,0:T(8,128)S(1)} collective-permute-done((f32[24,256]{1,0:T(8,128)S(1)}, f32[24,256]{1,0:T(8,128)S(1)}, u32[]{:S(2)}, u32[]{:S(2)}) %collective-permute-start.2) | collective-permute-done | bytes 24608 | tf_op jit(solution)/shard_map/ppermute | solution.py:171
  11.3 0.4 %collective-permute-start.4 = (f32[16,256]{1,0:T(8,128)S(1)}, f32[16,256]{1,0:T(8,128)S(1)}, u32[]{:S(2)}, u32[]{:S(2)}) collective-permute-start(f32[16,256]{1,0:T(8,128)S(1)} %get-tuple-element.38), channel_id=1, source_target_pairs={{0,3},{1,2},{2,1},{3,0},{4,7},{5,6},{6,5},{7,4},{8,11},{9,10},{10,... | collective-permute-start | bytes 49160 | tf_op jit(solution)/shard_map/ppermute | solution.py:171
  11.7 0.2 collective-permute-start.3
  11.9 0.6 %other_places.1.mate_places = s32[1,256]{1,0:T(1,128)S(4)} custom-call(f32[1,256]{1,0:T(1,128)S(1)} %slice.44.index_ref), custom_call_target="tpu_custom_call" | custom-call | tf_op jit(solution)/shard_map/other_places/pallas_call | solution.py:285
  12.4 0.1 collective-permute-done.4
  12.5 0.3 %collective-permute-done.3 = f32[16,256]{1,0:T(8,128)S(1)} collective-permute-done((f32[16,256]{1,0:T(8,128)S(1)}, f32[16,256]{1,0:T(8,128)S(1)}, u32[]{:S(2)}, u32[]{:S(2)}) %collective-permute-start.3) | collective-permute-done | bytes 16416 | tf_op jit(solution)/shard_map/ppermute | solution.py:171
  12.9 0.0 collective-permute-done.5.refs_3_
  12.9 0.0 collective-permute-done.6.refs_4_
  12.9 0.0 collective-permute-done.7.refs_5_
  12.9 0.9 %next_peaks.1 = f32[32,256]{1,0:T(8,128)S(1)} custom-call(s32[1,6]{1,0:T(1,128)S(4)} %get-tuple-element.19.rows_ref, s32[1,6]{1,0:T(1,128)S(4)} %get-tuple-element.20.cols_ref, s32[1,1]{1,0:T(1,128)S(6)} %copy.22.count_ref, s32[1,256]{1,0:T(1,128)S(4)} %other_places.1.mate_places, f32[32,256]{1,0:T(8,128)S(1)} %maximum_dynamic-update-slice_fusion.2.old_ref, ...), custom_call_target="tpu_custom_call" | custom-call | tf_op jit(solution)/shard_map/next_peaks/pallas_call | solution.py:300
  13.8 1.4 %collective-permute-start.8 = (f32[24,256]{1,0:T(8,128)S(1)}, f32[24,256]{1,0:T(8,128)S(1)}, u32[]{:S(2)}, u32[]{:S(2)}) collective-permute-start(f32[24,256]{1,0:T(8,128)S(1)} %pad_maximum_fusion.2), channel_id=1, source_target_pairs={{0,5},{1,4},{2,7},{3,6},{4,1},{5,0},{6,3},{7,2},{8,13},{9,12},{10,... | collective-permute-start | bytes 73736 | tf_op jit(solution)/shard_map/ppermute | solution.py:171
  15.2 2.0 %collective-permute-done.8 = f32[24,256]{1,0:T(8,128)S(1)} collective-permute-done((f32[24,256]{1,0:T(8,128)S(1)}, f32[24,256]{1,0:T(8,128)S(1)}, u32[]{:S(2)}, u32[]{:S(2)}) %collective-permute-start.8) | collective-permute-done | bytes 24608 | tf_op jit(solution)/shard_map/ppermute | solution.py:171
  17.2 0.4 %collective-permute-start.9 = (f32[24,256]{1,0:T(8,128)S(1)}, f32[24,256]{1,0:T(8,128)S(1)}, u32[]{:S(2)}, u32[]{:S(2)}) collective-permute-start(f32[24,256]{1,0:T(8,128)S(1)} %pad_maximum_fusion.3), channel_id=1, source_target_pairs={{0,9},{1,8},{2,11},{3,10},{4,13},{5,12},{6,15},{7,14},{8,1},{9,0},... | collective-permute-start | bytes 73736 | tf_op jit(solution)/shard_map/ppermute | solution.py:171
  17.6 2.9 %collective-permute-done.9 = f32[24,256]{1,0:T(8,128)S(1)} collective-permute-done((f32[24,256]{1,0:T(8,128)S(1)}, f32[24,256]{1,0:T(8,128)S(1)}, u32[]{:S(2)}, u32[]{:S(2)}) %collective-permute-start.9) | collective-permute-done | bytes 24608 | tf_op jit(solution)/shard_map/ppermute | solution.py:171
  20.6 4.3 %collective-permute-start.11 = (f32[16,256]{1,0:T(8,128)S(1)}, f32[16,256]{1,0:T(8,128)S(1)}, u32[]{:S(2)}, u32[]{:S(2)}) collective-permute-start(f32[16,256]{1,0:T(8,128)S(1)} %get-tuple-element.36), channel_id=1, source_target_pairs={{0,3},{1,2},{2,1},{3,0},{4,7},{5,6},{6,5},{7,4},{8,11},{9,10},{10,... | collective-permute-start | bytes 49160 | tf_op jit(solution)/shard_map/ppermute | solution.py:171
  24.8 0.3 %collective-permute-start.10 = (f32[16,256]{1,0:T(8,128)S(1)}, f32[16,256]{1,0:T(8,128)S(1)}, u32[]{:S(2)}, u32[]{:S(2)}) collective-permute-start(f32[16,256]{1,0:T(8,128)S(1)} %get-tuple-element.37), channel_id=1, source_target_pairs={{0,1},{1,0},{2,19},{3,18},{4,5},{5,4},{6,23},{7,22},{8,9},{9,8},{1... | collective-permute-start | bytes 49160 | tf_op jit(solution)/shard_map/ppermute | solution.py:171
  25.2 1.1 %collective-permute-done.11 = f32[16,256]{1,0:T(8,128)S(1)} collective-permute-done((f32[16,256]{1,0:T(8,128)S(1)}, f32[16,256]{1,0:T(8,128)S(1)}, u32[]{:S(2)}, u32[]{:S(2)}) %collective-permute-start.11) | collective-permute-done | bytes 16416 | tf_op jit(solution)/shard_map/ppermute | solution.py:171
  26.3 0.0 collective-permute-done.10
  26.3 2.8 %collective-permute-start.12 = (f32[4,256]{1,0:T(4,128)S(1)}, f32[4,256]{1,0:T(4,128)S(1)}, u32[]{:S(2)}, u32[]{:S(2)}) collective-permute-start(f32[4,256]{1,0:T(4,128)S(1)} %constant_dynamic-slice_fusion), channel_id=1, source_target_pairs={{0,1},{1,0},{2,3},{3,2},{4,5},{5,4},{6,7},{7,6},{8,9},{9,8},{10,11... | collective-permute-start | bytes 12296 | tf_op jit(solution)/shard_map/ppermute | solution.py:171
  29.1 1.3 %scaled_tiles.1 = (f32[1,6,256,256]{3,2,1,0:T(8,128)}, f32[4,256]{1,0:T(4,128)}) custom-call(s32[1,6]{1,0:T(1,128)S(4)} %get-tuple-element.19.rows_ref, s32[1,6]{1,0:T(1,128)S(4)} %get-tuple-element.20.cols_ref, s32[1,1]{1,0:T(1,128)S(6)} %copy.22.count_ref, f32[32,256]{1,0:T(8,128)S(1)} %maximum_dynamic-update-slice_fusion.old_ref, ...), custom_call_target="tpu_custom_call" | custom-call | flops 786432 | bytes 3145728 | tf_op jit(solution)/shard_map/scaled_tiles/pallas_call | solution.py:317
  30.4 0.0 collective-permute-done.12.given_ref
  30.4 0.6 %given_scaling.1 = f32[4,256]{1,0:T(4,128)} custom-call(f32[4,256]{1,0:T(4,128)S(1)} %collective-permute-done.12.given_ref, f32[4,256]{1,0:T(4,128)} %get-tuple-element.35.own_ref), custom_call_target="tpu_custom_call", output_to_operand_aliasing={{}: (1, {})} | custom-call | tf_op jit(solution)/shard_map/given_scaling/pallas_call | solution.py:335
  (33 shorter events, 0.2 us)
Async XLA Ops:
  2.9 1.6 %collective-permute-start = (f32[13,256]{1,0:T(8,128)S(1)}, f32[13,256]{1,0:T(8,128)S(1)}, u32[]{:S(2)}, u32[]{:S(2)}) collective-permute-start(f32[13,256]{1,0:T(8,128)S(1)} %pad_maximum_fusion.4), channel_id=1, source_target_pairs={{0,1},{1,0},{2,3},{3,2},{4,5},{5,4},{6,7},{7,6},{8,9},{9,8},{10,11... | collective-permute-start | bytes 39944 | tf_op jit(solution)/shard_map/ppermute | solution.py:171
  4.6 3.3 %collective-permute-start.1 = (f32[24,256]{1,0:T(8,128)S(1)}, f32[24,256]{1,0:T(8,128)S(1)}, u32[]{:S(2)}, u32[]{:S(2)}) collective-permute-start(f32[24,256]{1,0:T(8,128)S(1)} %pad_maximum_fusion), channel_id=1, source_target_pairs={{0,5},{1,4},{2,7},{3,6},{4,1},{5,0},{6,3},{7,2},{8,13},{9,12},{10,... | collective-permute-start | bytes 73736 | tf_op jit(solution)/shard_map/ppermute | solution.py:171
  7.9 3.3 %collective-permute-start.2 = (f32[24,256]{1,0:T(8,128)S(1)}, f32[24,256]{1,0:T(8,128)S(1)}, u32[]{:S(2)}, u32[]{:S(2)}) collective-permute-start(f32[24,256]{1,0:T(8,128)S(1)} %pad_maximum_fusion.1), channel_id=1, source_target_pairs={{0,9},{1,8},{2,11},{3,10},{4,13},{5,12},{6,15},{7,14},{8,1},{9,0},... | collective-permute-start | bytes 73736 | tf_op jit(solution)/shard_map/ppermute | solution.py:171
  8.4 4.5 %collective-permute-start.5 = (f32[2,256,256]{2,1,0:T(8,128)S(1)}, f32[2,256,256]{2,1,0:T(8,128)S(1)}, u32[]{:S(2)}, u32[]{:S(2)}) collective-permute-start(f32[2,256,256]{2,1,0:T(8,128)S(1)} %get-tuple-element.29.refs_0_), channel_id=1, source_target_pairs={{0,1},{1,0},{2,3},{3,2},{4,5},{5,4},{6,7},{7,6},{8,9},{9,8},{10,11... | collective-permute-start | bytes 1572872 | tf_op jit(solution)/shard_map/ppermute | solution.py:171
  8.6 4.3 %collective-permute-start.6 = (f32[2,256,256]{2,1,0:T(8,128)S(1)}, f32[2,256,256]{2,1,0:T(8,128)S(1)}, u32[]{:S(2)}, u32[]{:S(2)}) collective-permute-start(f32[2,256,256]{2,1,0:T(8,128)S(1)} %get-tuple-element.30.refs_1_), channel_id=1, source_target_pairs={{0,1},{1,0},{2,3},{3,2},{4,5},{5,4},{6,7},{7,6},{8,9},{9,8},{10,11... | collective-permute-start | bytes 1572872 | tf_op jit(solution)/shard_map/ppermute | solution.py:171
  8.9 4.0 %collective-permute-start.7 = (f32[2,256,256]{2,1,0:T(8,128)S(1)}, f32[2,256,256]{2,1,0:T(8,128)S(1)}, u32[]{:S(2)}, u32[]{:S(2)}) collective-permute-start(f32[2,256,256]{2,1,0:T(8,128)S(1)} %get-tuple-element.31.refs_2_), channel_id=1, source_target_pairs={{0,1},{1,0},{2,3},{3,2},{4,5},{5,4},{6,7},{7,6},{8,9},{9,8},{10,11... | collective-permute-start | bytes 1572872 | tf_op jit(solution)/shard_map/ppermute | solution.py:171
  11.3 1.2 %collective-permute-start.4 = (f32[16,256]{1,0:T(8,128)S(1)}, f32[16,256]{1,0:T(8,128)S(1)}, u32[]{:S(2)}, u32[]{:S(2)}) collective-permute-start(f32[16,256]{1,0:T(8,128)S(1)} %get-tuple-element.38), channel_id=1, source_target_pairs={{0,3},{1,2},{2,1},{3,0},{4,7},{5,6},{6,5},{7,4},{8,11},{9,10},{10,... | collective-permute-start | bytes 49160 | tf_op jit(solution)/shard_map/ppermute | solution.py:171
  11.7 1.2 %collective-permute-start.3 = (f32[16,256]{1,0:T(8,128)S(1)}, f32[16,256]{1,0:T(8,128)S(1)}, u32[]{:S(2)}, u32[]{:S(2)}) collective-permute-start(f32[16,256]{1,0:T(8,128)S(1)} %get-tuple-element.39), channel_id=1, source_target_pairs={{0,1},{1,0},{2,19},{3,18},{4,5},{5,4},{6,23},{7,22},{8,9},{9,8},{1... | collective-permute-start | bytes 49160 | tf_op jit(solution)/shard_map/ppermute | solution.py:171
  13.8 3.3 %collective-permute-start.8 = (f32[24,256]{1,0:T(8,128)S(1)}, f32[24,256]{1,0:T(8,128)S(1)}, u32[]{:S(2)}, u32[]{:S(2)}) collective-permute-start(f32[24,256]{1,0:T(8,128)S(1)} %pad_maximum_fusion.2), channel_id=1, source_target_pairs={{0,5},{1,4},{2,7},{3,6},{4,1},{5,0},{6,3},{7,2},{8,13},{9,12},{10,... | collective-permute-start | bytes 73736 | tf_op jit(solution)/shard_map/ppermute | solution.py:171
  17.2 3.3 %collective-permute-start.9 = (f32[24,256]{1,0:T(8,128)S(1)}, f32[24,256]{1,0:T(8,128)S(1)}, u32[]{:S(2)}, u32[]{:S(2)}) collective-permute-start(f32[24,256]{1,0:T(8,128)S(1)} %pad_maximum_fusion.3), channel_id=1, source_target_pairs={{0,9},{1,8},{2,11},{3,10},{4,13},{5,12},{6,15},{7,14},{8,1},{9,0},... | collective-permute-start | bytes 73736 | tf_op jit(solution)/shard_map/ppermute | solution.py:171
  20.6 5.7 %collective-permute-start.11 = (f32[16,256]{1,0:T(8,128)S(1)}, f32[16,256]{1,0:T(8,128)S(1)}, u32[]{:S(2)}, u32[]{:S(2)}) collective-permute-start(f32[16,256]{1,0:T(8,128)S(1)} %get-tuple-element.36), channel_id=1, source_target_pairs={{0,3},{1,2},{2,1},{3,0},{4,7},{5,6},{6,5},{7,4},{8,11},{9,10},{10,... | collective-permute-start | bytes 49160 | tf_op jit(solution)/shard_map/ppermute | solution.py:171
  24.8 1.4 %collective-permute-start.10 = (f32[16,256]{1,0:T(8,128)S(1)}, f32[16,256]{1,0:T(8,128)S(1)}, u32[]{:S(2)}, u32[]{:S(2)}) collective-permute-start(f32[16,256]{1,0:T(8,128)S(1)} %get-tuple-element.37), channel_id=1, source_target_pairs={{0,1},{1,0},{2,19},{3,18},{4,5},{5,4},{6,23},{7,22},{8,9},{9,8},{1... | collective-permute-start | bytes 49160 | tf_op jit(solution)/shard_map/ppermute | solution.py:171
  26.3 4.1 %collective-permute-start.12 = (f32[4,256]{1,0:T(4,128)S(1)}, f32[4,256]{1,0:T(4,128)S(1)}, u32[]{:S(2)}, u32[]{:S(2)}) collective-permute-start(f32[4,256]{1,0:T(4,128)S(1)} %constant_dynamic-slice_fusion), channel_id=1, source_target_pairs={{0,1},{1,0},{2,3},{3,2},{4,5},{5,4},{6,7},{7,6},{8,9},{9,8},{10,11... | collective-permute-start | bytes 12296 | tf_op jit(solution)/shard_map/ppermute | solution.py:171

commit v12 on v11

--- a/solution.py
+++ b/solution.py
@@ -48,7 +48,8 @@
 ):
     *held_refs, sems = refs
     slots = tiles_ref.shape[1]
-    held = [ref.at[s] for ref in held_refs for s in range(ref.shape[0])]
+    every = [ref.at[s] for ref in held_refs for s in range(ref.shape[0])]
+    held, sizes = every[:slots], every[slots:]
     moves = [(rows_in, rows_ref), (cols_in, cols_ref)]
     moves += [(tiles_ref.at[0, s], held[s]) for s in range(slots)]
     copies = [
@@ -73,6 +74,7 @@
             copy.wait()
         for s in range(first, min(first + 2, slots)):
             size = jnp.abs(held[s][...])
+            sizes[s][...] = size
             found.append((s, jnp.max(size, axis=0, keepdims=True), lane_max(size)))
         for s, column_max, row_max in found:
             live = s < count_ref[0, 0]
@@ -101,7 +103,7 @@
     def add(tiles, count, places):
         found = []
         for tile_ref, (row, col) in zip(tiles, places):
-            size = jnp.abs(tile_ref[...])
+            size = tile_ref[...]
             left = scale_ref[pl.ds(row, 1), :]
             right = scale_ref[pl.ds(col, 1), :]
             row_max = lane_max(size * right) * left
@@ -269,17 +271,18 @@
             pltpu.SMEM(tile_cols.shape, jnp.int32),
             pltpu.VMEM((blocks, tile), jnp.float32),
             pltpu.VMEM((1, tile), jnp.float32),
-            *[pltpu.VMEM((size, tile, tile), jnp.float32) for size in sizes],
+            *[pltpu.VMEM((size, tile, tile), jnp.float32) for size in 2 * sizes],
         ),
         in_specs=[SMEM, HBM, HBM, HBM],
-        out_specs=(SMEM, SMEM, VMEM, VMEM, *[VMEM for size in sizes]),
+        out_specs=(SMEM, SMEM, VMEM, VMEM, *[VMEM for size in 2 * sizes]),
         scratch_shapes=[pltpu.SemaphoreType.DMA((2 + slots,))],
         compiler_params=PARAMS,
         name="first_peaks",
     )(tile_counts, *kept((tile_rows, tile_cols, tiles), pltpu.HBM))
     places = (*kept((rows, cols), pltpu.SMEM), tile_counts)
     part, index = swap_in_chip(part, index, wide_size, narrow_size)
-    part, *sent = lax.optimization_barrier((part, *held))
+    held, magnitudes = held[: len(sizes)], held[len(sizes) :]
+    part, *sent = lax.optimization_barrier((part, *magnitudes))
     mates = [swap(piece, lambda w, n: (w, n ^ 1), wide_size, narrow_size) for piece in sent]
     held = kept(held, pltpu.VMEM)
     mate_places = pl.pallas_call(
@@ -308,7 +311,7 @@
             ],
             compiler_params=PARAMS,
             name="next_peaks",
-        )(*places_too, *kept([full], pltpu.VMEM), *held, *kept(mates, pltpu.VMEM))
+        )(*places_too, *kept([full, *magnitudes, *mates], pltpu.VMEM))
     if four:
         full, rows_too = max_over_users(part, wide_size, narrow_size, 3)
     else:

time: 31.2 us -> 31.1 us (level)
  no operation moved by 1% of the time
where the time goes in v12:
time: 31.1 us; the launch traced here: 30.9 us
  starting transfers between devices  13.1 us (42%)
  waiting for transfers between devices  11.2 us (36%)
  Pallas kernels  4.85 us (16%)
  between operations  1.51 us (5%)
    ppermute x13, starting transfers between devices, swap(): return lax.ppermute(values, BOTH, pairs)  13.1 us
    ppermute x13, waiting for transfers between devices, swap(): return lax.ppermute(values, BOTH, pairs)  11.2 us
    pallas_call x1, Pallas kernels, on_device(): pl.pallas_call(first_kernel, out_shape=(pltpu.SMEM(tile_rows.shape, jnp.i...  1.57 us
    pallas_call x1, Pallas kernels, on_device(): pl.pallas_call(functools.partial(last_kernel, ROWB), out_shape=(jax.Shape...  1.31 us
    pallas_call x1, Pallas kernels, on_device(): pl.pallas_call(functools.partial(next_kernel, ROWB), out_shape=pltpu.VMEM...  0.78 us
  transfers between devices with their start and end apart: 13, of which 8 were waited for; matrix products, arithmetic and copies ran while one was open for 0% of the time, Pallas kernels for 6%

profile of v12, /device:TPU:25, one launch (start us, length us, event | category | flops | bytes accessed | tf_op | source)
XLA Modules:
  0.0 30.9 jit_solution(6180649355163614053)
XLA Ops:
  1.3 1.6 %first_peaks.1 = (s32[1,6]{1,0:T(1,128)S(4)}, s32[1,6]{1,0:T(1,128)S(4)}, f32[32,256]{1,0:T(8,128)S(1)}, f32[1,256]{1,0:T(1,128)S(1)}, f32[2,256,256]{2,1,0:T(8,...) custom-call(s32[1,1]{1,0:T(1,128)S(6)} %copy.22.count_ref, ...), custom_call_target="tpu_custom_call" | custom-call | tf_op jit(solution)/shard_map/first_peaks/pallas_call | solution.py:267
  2.9 0.7 %collective-permute-start = (f32[13,256]{1,0:T(8,128)S(1)}, f32[13,256]{1,0:T(8,128)S(1)}, u32[]{:S(2)}, u32[]{:S(2)}) collective-permute-start(f32[13,256]{1,0:T(8,128)S(1)} %pad_maximum_fusion.4), channel_id=1, source_target_pairs={{0,1},{1,0},{2,3},{3,2},{4,5},{5,4},{6,7},{7,6},{8,9},{9,8},{10,11... | collective-permute-start | bytes 39944 | tf_op jit(solution)/shard_map/ppermute | solution.py:173
  3.7 0.8 %collective-permute-done = f32[13,256]{1,0:T(8,128)S(1)} collective-permute-done((f32[13,256]{1,0:T(8,128)S(1)}, f32[13,256]{1,0:T(8,128)S(1)}, u32[]{:S(2)}, u32[]{:S(2)}) %collective-permute-start) | collective-permute-done | bytes 13344 | tf_op jit(solution)/shard_map/ppermute | solution.py:173
  4.6 1.5 %collective-permute-start.1 = (f32[24,256]{1,0:T(8,128)S(1)}, f32[24,256]{1,0:T(8,128)S(1)}, u32[]{:S(2)}, u32[]{:S(2)}) collective-permute-start(f32[24,256]{1,0:T(8,128)S(1)} %pad_maximum_fusion), channel_id=1, source_target_pairs={{0,5},{1,4},{2,7},{3,6},{4,1},{5,0},{6,3},{7,2},{8,13},{9,12},{10,... | collective-permute-start | bytes 73736 | tf_op jit(solution)/shard_map/ppermute | solution.py:173
  6.1 1.8 %collective-permute-done.1 = f32[24,256]{1,0:T(8,128)S(1)} collective-permute-done((f32[24,256]{1,0:T(8,128)S(1)}, f32[24,256]{1,0:T(8,128)S(1)}, u32[]{:S(2)}, u32[]{:S(2)}) %collective-permute-start.1) | collective-permute-done | bytes 24608 | tf_op jit(solution)/shard_map/ppermute | solution.py:173
  7.9 0.5 %collective-permute-start.2 = (f32[24,256]{1,0:T(8,128)S(1)}, f32[24,256]{1,0:T(8,128)S(1)}, u32[]{:S(2)}, u32[]{:S(2)}) collective-permute-start(f32[24,256]{1,0:T(8,128)S(1)} %pad_maximum_fusion.1), channel_id=1, source_target_pairs={{0,9},{1,8},{2,11},{3,10},{4,13},{5,12},{6,15},{7,14},{8,1},{9,0},... | collective-permute-start | bytes 73736 | tf_op jit(solution)/shard_map/ppermute | solution.py:173
  8.4 0.2 collective-permute-start.5
  8.6 0.3 %collective-permute-start.6 = (f32[2,256,256]{2,1,0:T(8,128)S(1)}, f32[2,256,256]{2,1,0:T(8,128)S(1)}, u32[]{:S(2)}, u32[]{:S(2)}) collective-permute-start(f32[2,256,256]{2,1,0:T(8,128)S(1)} %get-tuple-element.33.refs_1_), channel_id=1, source_target_pairs={{0,1},{1,0},{2,3},{3,2},{4,5},{5,4},{6,7},{7,6},{8,9},{9,8},{10,11... | collective-permute-start | bytes 1572872 | tf_op jit(solution)/shard_map/ppermute | solution.py:173
  8.9 0.2 collective-permute-start.7
  9.1 2.2 %collective-permute-done.2 = f32[24,256]{1,0:T(8,128)S(1)} collective-permute-done((f32[24,256]{1,0:T(8,128)S(1)}, f32[24,256]{1,0:T(8,128)S(1)}, u32[]{:S(2)}, u32[]{:S(2)}) %collective-permute-start.2) | collective-permute-done | bytes 24608 | tf_op jit(solution)/shard_map/ppermute | solution.py:173
  11.3 0.4 %collective-permute-start.4 = (f32[16,256]{1,0:T(8,128)S(1)}, f32[16,256]{1,0:T(8,128)S(1)}, u32[]{:S(2)}, u32[]{:S(2)}) collective-permute-start(f32[16,256]{1,0:T(8,128)S(1)} %get-tuple-element.44), channel_id=1, source_target_pairs={{0,3},{1,2},{2,1},{3,0},{4,7},{5,6},{6,5},{7,4},{8,11},{9,10},{10,... | collective-permute-start | bytes 49160 | tf_op jit(solution)/shard_map/ppermute | solution.py:173
  11.7 0.2 collective-permute-start.3
  11.9 0.6 %other_places.1.mate_places = s32[1,256]{1,0:T(1,128)S(4)} custom-call(f32[1,256]{1,0:T(1,128)S(1)} %slice.44.index_ref), custom_call_target="tpu_custom_call" | custom-call | tf_op jit(solution)/shard_map/other_places/pallas_call | solution.py:288
  12.4 0.1 collective-permute-done.4
  12.5 0.3 %collective-permute-done.3 = f32[16,256]{1,0:T(8,128)S(1)} collective-permute-done((f32[16,256]{1,0:T(8,128)S(1)}, f32[16,256]{1,0:T(8,128)S(1)}, u32[]{:S(2)}, u32[]{:S(2)}) %collective-permute-start.3) | collective-permute-done | bytes 16416 | tf_op jit(solution)/shard_map/ppermute | solution.py:173
  12.9 0.0 collective-permute-done.5.refs_3_
  12.9 0.0 collective-permute-done.6.refs_4_
  12.9 0.0 collective-permute-done.7.refs_5_
  12.9 0.8 %next_peaks.1 = f32[32,256]{1,0:T(8,128)S(1)} custom-call(s32[1,6]{1,0:T(1,128)S(4)} %get-tuple-element.22.rows_ref, s32[1,6]{1,0:T(1,128)S(4)} %get-tuple-element.23.cols_ref, s32[1,1]{1,0:T(1,128)S(6)} %copy.22.count_ref, s32[1,256]{1,0:T(1,128)S(4)} %other_places.1.mate_places, f32[32,256]{1,0:T(8,128)S(1)} %maximum_dynamic-update-slice_fusion.2.old_ref, ...), custom_call_target="tpu_custom_call" | custom-call | tf_op jit(solution)/shard_map/next_peaks/pallas_call | solution.py:303
  13.8 1.3 %collective-permute-start.8 = (f32[24,256]{1,0:T(8,128)S(1)}, f32[24,256]{1,0:T(8,128)S(1)}, u32[]{:S(2)}, u32[]{:S(2)}) collective-permute-start(f32[24,256]{1,0:T(8,128)S(1)} %pad_maximum_fusion.2), channel_id=1, source_target_pairs={{0,5},{1,4},{2,7},{3,6},{4,1},{5,0},{6,3},{7,2},{8,13},{9,12},{10,... | collective-permute-start | bytes 73736 | tf_op jit(solution)/shard_map/ppermute | solution.py:173
  15.1 2.0 %collective-permute-done.8 = f32[24,256]{1,0:T(8,128)S(1)} collective-permute-done((f32[24,256]{1,0:T(8,128)S(1)}, f32[24,256]{1,0:T(8,128)S(1)}, u32[]{:S(2)}, u32[]{:S(2)}) %collective-permute-start.8) | collective-permute-done | bytes 24608 | tf_op jit(solution)/shard_map/ppermute | solution.py:173
  17.1 0.4 %collective-permute-start.9 = (f32[24,256]{1,0:T(8,128)S(1)}, f32[24,256]{1,0:T(8,128)S(1)}, u32[]{:S(2)}, u32[]{:S(2)}) collective-permute-start(f32[24,256]{1,0:T(8,128)S(1)} %pad_maximum_fusion.3), channel_id=1, source_target_pairs={{0,9},{1,8},{2,11},{3,10},{4,13},{5,12},{6,15},{7,14},{8,1},{9,0},... | collective-permute-start | bytes 73736 | tf_op jit(solution)/shard_map/ppermute | solution.py:173
  17.5 2.9 %collective-permute-done.9 = f32[24,256]{1,0:T(8,128)S(1)} collective-permute-done((f32[24,256]{1,0:T(8,128)S(1)}, f32[24,256]{1,0:T(8,128)S(1)}, u32[]{:S(2)}, u32[]{:S(2)}) %collective-permute-start.9) | collective-permute-done | bytes 24608 | tf_op jit(solution)/shard_map/ppermute | solution.py:173
  20.5 4.3 %collective-permute-start.11 = (f32[16,256]{1,0:T(8,128)S(1)}, f32[16,256]{1,0:T(8,128)S(1)}, u32[]{:S(2)}, u32[]{:S(2)}) collective-permute-start(f32[16,256]{1,0:T(8,128)S(1)} %get-tuple-element.42), channel_id=1, source_target_pairs={{0,3},{1,2},{2,1},{3,0},{4,7},{5,6},{6,5},{7,4},{8,11},{9,10},{10,... | collective-permute-start | bytes 49160 | tf_op jit(solution)/shard_map/ppermute | solution.py:173
  24.7 0.3 %collective-permute-start.10 = (f32[16,256]{1,0:T(8,128)S(1)}, f32[16,256]{1,0:T(8,128)S(1)}, u32[]{:S(2)}, u32[]{:S(2)}) collective-permute-start(f32[16,256]{1,0:T(8,128)S(1)} %get-tuple-element.43), channel_id=1, source_target_pairs={{0,1},{1,0},{2,19},{3,18},{4,5},{5,4},{6,23},{7,22},{8,9},{9,8},{1... | collective-permute-start | bytes 49160 | tf_op jit(solution)/shard_map/ppermute | solution.py:173
  25.1 1.1 %collective-permute-done.11 = f32[16,256]{1,0:T(8,128)S(1)} collective-permute-done((f32[16,256]{1,0:T(8,128)S(1)}, f32[16,256]{1,0:T(8,128)S(1)}, u32[]{:S(2)}, u32[]{:S(2)}) %collective-permute-start.11) | collective-permute-done | bytes 16416 | tf_op jit(solution)/shard_map/ppermute | solution.py:173
  26.2 0.0 collective-permute-done.10
  26.2 2.8 %collective-permute-start.12 = (f32[4,256]{1,0:T(4,128)S(1)}, f32[4,256]{1,0:T(4,128)S(1)}, u32[]{:S(2)}, u32[]{:S(2)}) collective-permute-start(f32[4,256]{1,0:T(4,128)S(1)} %constant_dynamic-slice_fusion), channel_id=1, source_target_pairs={{0,1},{1,0},{2,3},{3,2},{4,5},{5,4},{6,7},{7,6},{8,9},{9,8},{10,11... | collective-permute-start | bytes 12296 | tf_op jit(solution)/shard_map/ppermute | solution.py:173
  29.0 1.3 %scaled_tiles.1 = (f32[1,6,256,256]{3,2,1,0:T(8,128)}, f32[4,256]{1,0:T(4,128)}) custom-call(s32[1,6]{1,0:T(1,128)S(4)} %get-tuple-element.22.rows_ref, s32[1,6]{1,0:T(1,128)S(4)} %get-tuple-element.23.cols_ref, s32[1,1]{1,0:T(1,128)S(6)} %copy.22.count_ref, f32[32,256]{1,0:T(8,128)S(1)} %maximum_dynamic-update-slice_fusion.old_ref, ...), custom_call_target="tpu_custom_call" | custom-call | flops 786432 | bytes 3145728 | tf_op jit(solution)/shard_map/scaled_tiles/pallas_call | solution.py:320
  30.3 0.0 collective-permute-done.12.given_ref
  30.3 0.6 %given_scaling.1 = f32[4,256]{1,0:T(4,128)} custom-call(f32[4,256]{1,0:T(4,128)S(1)} %collective-permute-done.12.given_ref, f32[4,256]{1,0:T(4,128)} %get-tuple-element.41.own_ref), custom_call_target="tpu_custom_call", output_to_operand_aliasing={{}: (1, {})} | custom-call | tf_op jit(solution)/shard_map/given_scaling/pallas_call | solution.py:338
  (33 shorter events, 0.2 us)
Async XLA Ops:
  2.9 1.6 %collective-permute-start = (f32[13,256]{1,0:T(8,128)S(1)}, f32[13,256]{1,0:T(8,128)S(1)}, u32[]{:S(2)}, u32[]{:S(2)}) collective-permute-start(f32[13,256]{1,0:T(8,128)S(1)} %pad_maximum_fusion.4), channel_id=1, source_target_pairs={{0,1},{1,0},{2,3},{3,2},{4,5},{5,4},{6,7},{7,6},{8,9},{9,8},{10,11... | collective-permute-start | bytes 39944 | tf_op jit(solution)/shard_map/ppermute | solution.py:173
  4.6 3.3 %collective-permute-start.1 = (f32[24,256]{1,0:T(8,128)S(1)}, f32[24,256]{1,0:T(8,128)S(1)}, u32[]{:S(2)}, u32[]{:S(2)}) collective-permute-start(f32[24,256]{1,0:T(8,128)S(1)} %pad_maximum_fusion), channel_id=1, source_target_pairs={{0,5},{1,4},{2,7},{3,6},{4,1},{5,0},{6,3},{7,2},{8,13},{9,12},{10,... | collective-permute-start | bytes 73736 | tf_op jit(solution)/shard_map/ppermute | solution.py:173
  7.9 3.3 %collective-permute-start.2 = (f32[24,256]{1,0:T(8,128)S(1)}, f32[24,256]{1,0:T(8,128)S(1)}, u32[]{:S(2)}, u32[]{:S(2)}) collective-permute-start(f32[24,256]{1,0:T(8,128)S(1)} %pad_maximum_fusion.1), channel_id=1, source_target_pairs={{0,9},{1,8},{2,11},{3,10},{4,13},{5,12},{6,15},{7,14},{8,1},{9,0},... | collective-permute-start | bytes 73736 | tf_op jit(solution)/shard_map/ppermute | solution.py:173
  8.4 4.5 %collective-permute-start.5 = (f32[2,256,256]{2,1,0:T(8,128)S(1)}, f32[2,256,256]{2,1,0:T(8,128)S(1)}, u32[]{:S(2)}, u32[]{:S(2)}) collective-permute-start(f32[2,256,256]{2,1,0:T(8,128)S(1)} %get-tuple-element.32.refs_0_), channel_id=1, source_target_pairs={{0,1},{1,0},{2,3},{3,2},{4,5},{5,4},{6,7},{7,6},{8,9},{9,8},{10,11... | collective-permute-start | bytes 1572872 | tf_op jit(solution)/shard_map/ppermute | solution.py:173
  8.6 4.3 %collective-permute-start.6 = (f32[2,256,256]{2,1,0:T(8,128)S(1)}, f32[2,256,256]{2,1,0:T(8,128)S(1)}, u32[]{:S(2)}, u32[]{:S(2)}) collective-permute-start(f32[2,256,256]{2,1,0:T(8,128)S(1)} %get-tuple-element.33.refs_1_), channel_id=1, source_target_pairs={{0,1},{1,0},{2,3},{3,2},{4,5},{5,4},{6,7},{7,6},{8,9},{9,8},{10,11... | collective-permute-start | bytes 1572872 | tf_op jit(solution)/shard_map/ppermute | solution.py:173
  8.9 4.0 %collective-permute-start.7 = (f32[2,256,256]{2,1,0:T(8,128)S(1)}, f32[2,256,256]{2,1,0:T(8,128)S(1)}, u32[]{:S(2)}, u32[]{:S(2)}) collective-permute-start(f32[2,256,256]{2,1,0:T(8,128)S(1)} %get-tuple-element.34.refs_2_), channel_id=1, source_target_pairs={{0,1},{1,0},{2,3},{3,2},{4,5},{5,4},{6,7},{7,6},{8,9},{9,8},{10,11... | collective-permute-start | bytes 1572872 | tf_op jit(solution)/shard_map/ppermute | solution.py:173
  11.3 1.2 %collective-permute-start.4 = (f32[16,256]{1,0:T(8,128)S(1)}, f32[16,256]{1,0:T(8,128)S(1)}, u32[]{:S(2)}, u32[]{:S(2)}) collective-permute-start(f32[16,256]{1,0:T(8,128)S(1)} %get-tuple-element.44), channel_id=1, source_target_pairs={{0,3},{1,2},{2,1},{3,0},{4,7},{5,6},{6,5},{7,4},{8,11},{9,10},{10,... | collective-permute-start | bytes 49160 | tf_op jit(solution)/shard_map/ppermute | solution.py:173
  11.7 1.2 %collective-permute-start.3 = (f32[16,256]{1,0:T(8,128)S(1)}, f32[16,256]{1,0:T(8,128)S(1)}, u32[]{:S(2)}, u32[]{:S(2)}) collective-permute-start(f32[16,256]{1,0:T(8,128)S(1)} %get-tuple-element.45), channel_id=1, source_target_pairs={{0,1},{1,0},{2,19},{3,18},{4,5},{5,4},{6,23},{7,22},{8,9},{9,8},{1... | collective-permute-start | bytes 49160 | tf_op jit(solution)/shard_map/ppermute | solution.py:173
  13.8 3.3 %collective-permute-start.8 = (f32[24,256]{1,0:T(8,128)S(1)}, f32[24,256]{1,0:T(8,128)S(1)}, u32[]{:S(2)}, u32[]{:S(2)}) collective-permute-start(f32[24,256]{1,0:T(8,128)S(1)} %pad_maximum_fusion.2), channel_id=1, source_target_pairs={{0,5},{1,4},{2,7},{3,6},{4,1},{5,0},{6,3},{7,2},{8,13},{9,12},{10,... | collective-permute-start | bytes 73736 | tf_op jit(solution)/shard_map/ppermute | solution.py:173
  17.1 3.3 %collective-permute-start.9 = (f32[24,256]{1,0:T(8,128)S(1)}, f32[24,256]{1,0:T(8,128)S(1)}, u32[]{:S(2)}, u32[]{:S(2)}) collective-permute-start(f32[24,256]{1,0:T(8,128)S(1)} %pad_maximum_fusion.3), channel_id=1, source_target_pairs={{0,9},{1,8},{2,11},{3,10},{4,13},{5,12},{6,15},{7,14},{8,1},{9,0},... | collective-permute-start | bytes 73736 | tf_op jit(solution)/shard_map/ppermute | solution.py:173
  20.5 5.7 %collective-permute-start.11 = (f32[16,256]{1,0:T(8,128)S(1)}, f32[16,256]{1,0:T(8,128)S(1)}, u32[]{:S(2)}, u32[]{:S(2)}) collective-permute-start(f32[16,256]{1,0:T(8,128)S(1)} %get-tuple-element.42), channel_id=1, source_target_pairs={{0,3},{1,2},{2,1},{3,0},{4,7},{5,6},{6,5},{7,4},{8,11},{9,10},{10,... | collective-permute-start | bytes 49160 | tf_op jit(solution)/shard_map/ppermute | solution.py:173
  24.7 1.4 %collective-permute-start.10 = (f32[16,256]{1,0:T(8,128)S(1)}, f32[16,256]{1,0:T(8,128)S(1)}, u32[]{:S(2)}, u32[]{:S(2)}) collective-permute-start(f32[16,256]{1,0:T(8,128)S(1)} %get-tuple-element.43), channel_id=1, source_target_pairs={{0,1},{1,0},{2,19},{3,18},{4,5},{5,4},{6,23},{7,22},{8,9},{9,8},{1... | collective-permute-start | bytes 49160 | tf_op jit(solution)/shard_map/ppermute | solution.py:173
  26.2 4.1 %collective-permute-start.12 = (f32[4,256]{1,0:T(4,128)S(1)}, f32[4,256]{1,0:T(4,128)S(1)}, u32[]{:S(2)}, u32[]{:S(2)}) collective-permute-start(f32[4,256]{1,0:T(4,128)S(1)} %constant_dynamic-slice_fusion), channel_id=1, source_target_pairs={{0,1},{1,0},{2,3},{3,2},{4,5},{5,4},{6,7},{7,6},{8,9},{9,8},{10,11... | collective-permute-start | bytes 12296 | tf_op jit(solution)/shard_map/ppermute | solution.py:173

commit v13 on v12

--- a/solution.py
+++ b/solution.py
@@ -89,8 +89,8 @@
     copy.wait()
 
 
-def next_kernel(row_blocks, rows_ref, cols_ref, count_ref, mate_places, old_ref, *refs):
-    *tile_refs, peak_ref, scale_ref, column_ref = refs
+def next_kernel(row_blocks, narrow_size, share, rows_ref, cols_ref, count_ref, mate_places, old_ref, *refs):
+    *tile_refs, peak_ref, sent_ref, scale_ref, column_ref = refs
     tiles = [ref.at[s] for ref in tile_refs for s in range(ref.shape[0])]
     slots, tile = len(tiles) // 2, tiles[0].shape[0]
     half = tile // 2
@@ -125,6 +125,11 @@
     add(tiles[:slots], count_ref[0, 0], own)
     add(tiles[slots:], given[0], list(zip(given[1::2], given[2::2])))
     peak_ref[...] = peak_ref[...] * old_ref[...]
+    group = peak_ref.shape[0] // narrow_size
+    columns = pl.multiple_of((lax.axis_index("narrow") // 2) * 2 * group, group)
+    rows = pl.multiple_of((lax.axis_index("wide") // share) * group, group)
+    sent_ref[: 2 * group] = peak_ref[pl.ds(columns, 2 * group), :]
+    sent_ref[2 * group :] = peak_ref[pl.ds(rows, group), :]
 
 
 def last_kernel(row_blocks, rows_ref, cols_ref, count_ref, old_ref, *refs):
@@ -218,7 +223,7 @@
     return columns, rows, size
 
 
-def max_over_users(values, wide_size, narrow_size, idle):
+def max_over_users(values, wide_size, narrow_size, idle, ready=None):
     columns, rows, size = windows(values, wide_size, narrow_size)
     share, group_size = wide_size // narrow_size, size // 2
     half = wide_size // 2
@@ -232,6 +237,8 @@
                 lax.dynamic_slice_in_dim(values, group_start, group_size, 0),
             ]
         )
+        if bit == 1 and ready is not None:
+            sent = ready
         other = swap(sent, lambda w, n: (w ^ bit, n ^ 1), wide_size, narrow_size)
         values = window_max(values, columns, other[:size])
         values = window_max(values, group_start, other[size:])
@@ -300,11 +307,14 @@
             full, _ = max_over_users(part, wide_size, narrow_size, 1)
         else:
             full = max_over_chips(part, wide_size, narrow_size)
-        part = pl.pallas_call(
-            functools.partial(next_kernel, ROWB),
-            out_shape=pltpu.VMEM((blocks, tile), jnp.float32),
+        part, ready = pl.pallas_call(
+            functools.partial(next_kernel, ROWB, narrow_size, wide_size // narrow_size),
+            out_shape=(
+                pltpu.VMEM((blocks, tile), jnp.float32),
+                pltpu.VMEM((3 * blocks // narrow_size, tile), jnp.float32),
+            ),
             in_specs=[SMEM] * 4 + [VMEM] * (1 + 2 * len(held)),
-            out_specs=VMEM,
+            out_specs=(VMEM, VMEM),
             scratch_shapes=[
                 pltpu.VMEM((blocks, tile), jnp.float32),
                 pltpu.VMEM((ROWB, tile, tile // 2), jnp.float32),
@@ -313,7 +323,7 @@
             name="next_peaks",
         )(*places_too, *kept([full, *magnitudes, *mates], pltpu.VMEM))
     if four:
-        full, rows_too = max_over_users(part, wide_size, narrow_size, 3)
+        full, rows_too = max_over_users(part, wide_size, narrow_size, 3, ready)
     else:
         full = max_over_chips(part, wide_size, narrow_size)
     own_shape = jax.ShapeDtypeStruct((ROWB, tile), jnp.float32)

time: 31.1 us -> 31.1 us (level)
  no operation moved by 1% of the time
where the time goes in v13:
time: 31.1 us; the launch traced here: 30.9 us
  starting transfers between devices  13.1 us (42%)
  waiting for transfers between devices  11.2 us (36%)
  Pallas kernels  4.86 us (16%)
  between operations  1.49 us (5%)
    ppermute x13, starting transfers between devices, swap(): return lax.ppermute(values, BOTH, pairs)  13.1 us
    ppermute x13, waiting for transfers between devices, swap(): return lax.ppermute(values, BOTH, pairs)  11.2 us
    pallas_call x1, Pallas kernels, on_device(): pl.pallas_call(first_kernel, out_shape=(pltpu.SMEM(tile_rows.shape, jnp.i...  1.57 us
    pallas_call x1, Pallas kernels, on_device(): pl.pallas_call(functools.partial(last_kernel, ROWB), out_shape=(jax.Shape...  1.31 us
    pallas_call x1, Pallas kernels, on_device(): pl.pallas_call(functools.partial(next_kernel, ROWB, narrow_size, wide_siz...  0.79 us
  transfers between devices with their start and end apart: 13, of which 8 were waited for; matrix products, arithmetic and copies ran while one was open for 0% of the time, Pallas kernels for 6%

profile of v13, /device:TPU:25, one launch (start us, length us, event | category | flops | bytes accessed | tf_op | source)
XLA Modules:
  0.0 30.9 jit_solution(2658793082530070364)
XLA Ops:
  1.3 1.6 %first_peaks.1 = (s32[1,6]{1,0:T(1,128)S(4)}, s32[1,6]{1,0:T(1,128)S(4)}, f32[32,256]{1,0:T(8,128)S(1)}, f32[1,256]{1,0:T(1,128)S(1)}, f32[2,256,256]{2,1,0:T(8,...) custom-call(s32[1,1]{1,0:T(1,128)S(6)} %copy.22.count_ref, ...), custom_call_target="tpu_custom_call" | custom-call | tf_op jit(solution)/shard_map/first_peaks/pallas_call | solution.py:274
  2.9 0.7 %collective-permute-start = (f32[13,256]{1,0:T(8,128)S(1)}, f32[13,256]{1,0:T(8,128)S(1)}, u32[]{:S(2)}, u32[]{:S(2)}) collective-permute-start(f32[13,256]{1,0:T(8,128)S(1)} %pad_maximum_fusion.3), channel_id=1, source_target_pairs={{0,1},{1,0},{2,3},{3,2},{4,5},{5,4},{6,7},{7,6},{8,9},{9,8},{10,11... | collective-permute-start | bytes 39944 | tf_op jit(solution)/shard_map/ppermute | solution.py:178
  3.7 0.8 %collective-permute-done = f32[13,256]{1,0:T(8,128)S(1)} collective-permute-done((f32[13,256]{1,0:T(8,128)S(1)}, f32[13,256]{1,0:T(8,128)S(1)}, u32[]{:S(2)}, u32[]{:S(2)}) %collective-permute-start) | collective-permute-done | bytes 13344 | tf_op jit(solution)/shard_map/ppermute | solution.py:178
  4.6 1.5 %collective-permute-start.1 = (f32[24,256]{1,0:T(8,128)S(1)}, f32[24,256]{1,0:T(8,128)S(1)}, u32[]{:S(2)}, u32[]{:S(2)}) collective-permute-start(f32[24,256]{1,0:T(8,128)S(1)} %pad_maximum_fusion), channel_id=1, source_target_pairs={{0,5},{1,4},{2,7},{3,6},{4,1},{5,0},{6,3},{7,2},{8,13},{9,12},{10,... | collective-permute-start | bytes 73736 | tf_op jit(solution)/shard_map/ppermute | solution.py:178
  6.1 1.8 %collective-permute-done.1 = f32[24,256]{1,0:T(8,128)S(1)} collective-permute-done((f32[24,256]{1,0:T(8,128)S(1)}, f32[24,256]{1,0:T(8,128)S(1)}, u32[]{:S(2)}, u32[]{:S(2)}) %collective-permute-start.1) | collective-permute-done | bytes 24608 | tf_op jit(solution)/shard_map/ppermute | solution.py:178
  7.9 0.5 %collective-permute-start.2 = (f32[24,256]{1,0:T(8,128)S(1)}, f32[24,256]{1,0:T(8,128)S(1)}, u32[]{:S(2)}, u32[]{:S(2)}) collective-permute-start(f32[24,256]{1,0:T(8,128)S(1)} %pad_maximum_fusion.1), channel_id=1, source_target_pairs={{0,9},{1,8},{2,11},{3,10},{4,13},{5,12},{6,15},{7,14},{8,1},{9,0},... | collective-permute-start | bytes 73736 | tf_op jit(solution)/shard_map/ppermute | solution.py:178
  8.4 0.2 collective-permute-start.5
  8.6 0.3 %collective-permute-start.6 = (f32[2,256,256]{2,1,0:T(8,128)S(1)}, f32[2,256,256]{2,1,0:T(8,128)S(1)}, u32[]{:S(2)}, u32[]{:S(2)}) collective-permute-start(f32[2,256,256]{2,1,0:T(8,128)S(1)} %get-tuple-element.35.refs_1_), channel_id=1, source_target_pairs={{0,1},{1,0},{2,3},{3,2},{4,5},{5,4},{6,7},{7,6},{8,9},{9,8},{10,11... | collective-permute-start | bytes 1572872 | tf_op jit(solution)/shard_map/ppermute | solution.py:178
  8.9 0.2 collective-permute-start.7
  9.1 2.2 %collective-permute-done.2 = f32[24,256]{1,0:T(8,128)S(1)} collective-permute-done((f32[24,256]{1,0:T(8,128)S(1)}, f32[24,256]{1,0:T(8,128)S(1)}, u32[]{:S(2)}, u32[]{:S(2)}) %collective-permute-start.2) | collective-permute-done | bytes 24608 | tf_op jit(solution)/shard_map/ppermute | solution.py:178
  11.3 0.4 %collective-permute-start.4 = (f32[16,256]{1,0:T(8,128)S(1)}, f32[16,256]{1,0:T(8,128)S(1)}, u32[]{:S(2)}, u32[]{:S(2)}) collective-permute-start(f32[16,256]{1,0:T(8,128)S(1)} %get-tuple-element.48), channel_id=1, source_target_pairs={{0,3},{1,2},{2,1},{3,0},{4,7},{5,6},{6,5},{7,4},{8,11},{9,10},{10,... | collective-permute-start | bytes 49160 | tf_op jit(solution)/shard_map/ppermute | solution.py:178
  11.7 0.2 collective-permute-start.3
  11.9 0.6 %other_places.1.mate_places = s32[1,256]{1,0:T(1,128)S(4)} custom-call(f32[1,256]{1,0:T(1,128)S(1)} %slice.44.index_ref), custom_call_target="tpu_custom_call" | custom-call | tf_op jit(solution)/shard_map/other_places/pallas_call | solution.py:295
  12.4 0.1 collective-permute-done.4
  12.5 0.3 %collective-permute-done.3 = f32[16,256]{1,0:T(8,128)S(1)} collective-permute-done((f32[16,256]{1,0:T(8,128)S(1)}, f32[16,256]{1,0:T(8,128)S(1)}, u32[]{:S(2)}, u32[]{:S(2)}) %collective-permute-start.3) | collective-permute-done | bytes 16416 | tf_op jit(solution)/shard_map/ppermute | solution.py:178
  12.9 0.0 collective-permute-done.5.refs_3_
  12.9 0.0 collective-permute-done.6.refs_4_
  12.9 0.0 collective-permute-done.7.refs_5_
  12.9 0.8 %next_peaks.1 = (f32[32,256]{1,0:T(8,128)S(1)}, f32[24,256]{1,0:T(8,128)S(1)}) custom-call(s32[1,6]{1,0:T(1,128)S(4)} %get-tuple-element.24.rows_ref, s32[1,6]{1,0:T(1,128)S(4)} %get-tuple-element.25.cols_ref, s32[1,1]{1,0:T(1,128)S(6)} %copy.22.count_ref, s32[1,256]{1,0:T(1,128)S(4)} %other_places.1.mate_places, ...), custom_call_target="tpu_custom_call" | custom-call | tf_op jit(solution)/shard_map/next_peaks/pallas_call | solution.py:310
  13.7 1.3 %collective-permute-start.8 = (f32[24,256]{1,0:T(8,128)S(1)}, f32[24,256]{1,0:T(8,128)S(1)}, u32[]{:S(2)}, u32[]{:S(2)}) collective-permute-start(f32[24,256]{1,0:T(8,128)S(1)} %get-tuple-element.38), channel_id=1, source_target_pairs={{0,5},{1,4},{2,7},{3,6},{4,1},{5,0},{6,3},{7,2},{8,13},{9,12},{10,... | collective-permute-start | bytes 73736 | tf_op jit(solution)/shard_map/ppermute | solution.py:178
  15.1 2.0 %collective-permute-done.8 = f32[24,256]{1,0:T(8,128)S(1)} collective-permute-done((f32[24,256]{1,0:T(8,128)S(1)}, f32[24,256]{1,0:T(8,128)S(1)}, u32[]{:S(2)}, u32[]{:S(2)}) %collective-permute-start.8) | collective-permute-done | bytes 24608 | tf_op jit(solution)/shard_map/ppermute | solution.py:178
  17.1 0.4 %collective-permute-start.9 = (f32[24,256]{1,0:T(8,128)S(1)}, f32[24,256]{1,0:T(8,128)S(1)}, u32[]{:S(2)}, u32[]{:S(2)}) collective-permute-start(f32[24,256]{1,0:T(8,128)S(1)} %pad_maximum_fusion.2), channel_id=1, source_target_pairs={{0,9},{1,8},{2,11},{3,10},{4,13},{5,12},{6,15},{7,14},{8,1},{9,0},... | collective-permute-start | bytes 73736 | tf_op jit(solution)/shard_map/ppermute | solution.py:178
  17.5 2.9 %collective-permute-done.9 = f32[24,256]{1,0:T(8,128)S(1)} collective-permute-done((f32[24,256]{1,0:T(8,128)S(1)}, f32[24,256]{1,0:T(8,128)S(1)}, u32[]{:S(2)}, u32[]{:S(2)}) %collective-permute-start.9) | collective-permute-done | bytes 24608 | tf_op jit(solution)/shard_map/ppermute | solution.py:178
  20.4 4.3 %collective-permute-start.11 = (f32[16,256]{1,0:T(8,128)S(1)}, f32[16,256]{1,0:T(8,128)S(1)}, u32[]{:S(2)}, u32[]{:S(2)}) collective-permute-start(f32[16,256]{1,0:T(8,128)S(1)} %get-tuple-element.46), channel_id=1, source_target_pairs={{0,3},{1,2},{2,1},{3,0},{4,7},{5,6},{6,5},{7,4},{8,11},{9,10},{10,... | collective-permute-start | bytes 49160 | tf_op jit(solution)/shard_map/ppermute | solution.py:178
  24.7 0.3 %collective-permute-start.10 = (f32[16,256]{1,0:T(8,128)S(1)}, f32[16,256]{1,0:T(8,128)S(1)}, u32[]{:S(2)}, u32[]{:S(2)}) collective-permute-start(f32[16,256]{1,0:T(8,128)S(1)} %get-tuple-element.47), channel_id=1, source_target_pairs={{0,1},{1,0},{2,19},{3,18},{4,5},{5,4},{6,23},{7,22},{8,9},{9,8},{1... | collective-permute-start | bytes 49160 | tf_op jit(solution)/shard_map/ppermute | solution.py:178
  25.1 1.1 %collective-permute-done.11 = f32[16,256]{1,0:T(8,128)S(1)} collective-permute-done((f32[16,256]{1,0:T(8,128)S(1)}, f32[16,256]{1,0:T(8,128)S(1)}, u32[]{:S(2)}, u32[]{:S(2)}) %collective-permute-start.11) | collective-permute-done | bytes 16416 | tf_op jit(solution)/shard_map/ppermute | solution.py:178
  26.1 0.0 collective-permute-done.10
  26.2 2.8 %collective-permute-start.12 = (f32[4,256]{1,0:T(4,128)S(1)}, f32[4,256]{1,0:T(4,128)S(1)}, u32[]{:S(2)}, u32[]{:S(2)}) collective-permute-start(f32[4,256]{1,0:T(4,128)S(1)} %constant_dynamic-slice_fusion.6), channel_id=1, source_target_pairs={{0,1},{1,0},{2,3},{3,2},{4,5},{5,4},{6,7},{7,6},{8,9},{9,8},{10,11... | collective-permute-start | bytes 12296 | tf_op jit(solution)/shard_map/ppermute | solution.py:178
  28.9 1.3 %scaled_tiles.1 = (f32[1,6,256,256]{3,2,1,0:T(8,128)}, f32[4,256]{1,0:T(4,128)}) custom-call(s32[1,6]{1,0:T(1,128)S(4)} %get-tuple-element.24.rows_ref, s32[1,6]{1,0:T(1,128)S(4)} %get-tuple-element.25.cols_ref, s32[1,1]{1,0:T(1,128)S(6)} %copy.22.count_ref, f32[32,256]{1,0:T(8,128)S(1)} %maximum_dynamic-update-slice_fusion.old_ref, ...), custom_call_target="tpu_custom_call" | custom-call | flops 786432 | bytes 3145728 | tf_op jit(solution)/shard_map/scaled_tiles/pallas_call | solution.py:330
  30.3 0.0 collective-permute-done.12.given_ref
  30.3 0.6 %given_scaling.1 = f32[4,256]{1,0:T(4,128)} custom-call(f32[4,256]{1,0:T(4,128)S(1)} %collective-permute-done.12.given_ref, f32[4,256]{1,0:T(4,128)} %get-tuple-element.45.own_ref), custom_call_target="tpu_custom_call", output_to_operand_aliasing={{}: (1, {})} | custom-call | tf_op jit(solution)/shard_map/given_scaling/pallas_call | solution.py:348
  (30 shorter events, 0.2 us)
Async XLA Ops:
  2.9 1.6 %collective-permute-start = (f32[13,256]{1,0:T(8,128)S(1)}, f32[13,256]{1,0:T(8,128)S(1)}, u32[]{:S(2)}, u32[]{:S(2)}) collective-permute-start(f32[13,256]{1,0:T(8,128)S(1)} %pad_maximum_fusion.3), channel_id=1, source_target_pairs={{0,1},{1,0},{2,3},{3,2},{4,5},{5,4},{6,7},{7,6},{8,9},{9,8},{10,11... | collective-permute-start | bytes 39944 | tf_op jit(solution)/shard_map/ppermute | solution.py:178
  4.6 3.3 %collective-permute-start.1 = (f32[24,256]{1,0:T(8,128)S(1)}, f32[24,256]{1,0:T(8,128)S(1)}, u32[]{:S(2)}, u32[]{:S(2)}) collective-permute-start(f32[24,256]{1,0:T(8,128)S(1)} %pad_maximum_fusion), channel_id=1, source_target_pairs={{0,5},{1,4},{2,7},{3,6},{4,1},{5,0},{6,3},{7,2},{8,13},{9,12},{10,... | collective-permute-start | bytes 73736 | tf_op jit(solution)/shard_map/ppermute | solution.py:178
  7.9 3.3 %collective-permute-start.2 = (f32[24,256]{1,0:T(8,128)S(1)}, f32[24,256]{1,0:T(8,128)S(1)}, u32[]{:S(2)}, u32[]{:S(2)}) collective-permute-start(f32[24,256]{1,0:T(8,128)S(1)} %pad_maximum_fusion.1), channel_id=1, source_target_pairs={{0,9},{1,8},{2,11},{3,10},{4,13},{5,12},{6,15},{7,14},{8,1},{9,0},... | collective-permute-start | bytes 73736 | tf_op jit(solution)/shard_map/ppermute | solution.py:178
  8.4 4.5 %collective-permute-start.5 = (f32[2,256,256]{2,1,0:T(8,128)S(1)}, f32[2,256,256]{2,1,0:T(8,128)S(1)}, u32[]{:S(2)}, u32[]{:S(2)}) collective-permute-start(f32[2,256,256]{2,1,0:T(8,128)S(1)} %get-tuple-element.34.refs_0_), channel_id=1, source_target_pairs={{0,1},{1,0},{2,3},{3,2},{4,5},{5,4},{6,7},{7,6},{8,9},{9,8},{10,11... | collective-permute-start | bytes 1572872 | tf_op jit(solution)/shard_map/ppermute | solution.py:178
  8.6 4.3 %collective-permute-start.6 = (f32[2,256,256]{2,1,0:T(8,128)S(1)}, f32[2,256,256]{2,1,0:T(8,128)S(1)}, u32[]{:S(2)}, u32[]{:S(2)}) collective-permute-start(f32[2,256,256]{2,1,0:T(8,128)S(1)} %get-tuple-element.35.refs_1_), channel_id=1, source_target_pairs={{0,1},{1,0},{2,3},{3,2},{4,5},{5,4},{6,7},{7,6},{8,9},{9,8},{10,11... | collective-permute-start | bytes 1572872 | tf_op jit(solution)/shard_map/ppermute | solution.py:178
  8.9 4.0 %collective-permute-start.7 = (f32[2,256,256]{2,1,0:T(8,128)S(1)}, f32[2,256,256]{2,1,0:T(8,128)S(1)}, u32[]{:S(2)}, u32[]{:S(2)}) collective-permute-start(f32[2,256,256]{2,1,0:T(8,128)S(1)} %get-tuple-element.36.refs_2_), channel_id=1, source_target_pairs={{0,1},{1,0},{2,3},{3,2},{4,5},{5,4},{6,7},{7,6},{8,9},{9,8},{10,11... | collective-permute-start | bytes 1572872 | tf_op jit(solution)/shard_map/ppermute | solution.py:178
  11.3 1.2 %collective-permute-start.4 = (f32[16,256]{1,0:T(8,128)S(1)}, f32[16,256]{1,0:T(8,128)S(1)}, u32[]{:S(2)}, u32[]{:S(2)}) collective-permute-start(f32[16,256]{1,0:T(8,128)S(1)} %get-tuple-element.48), channel_id=1, source_target_pairs={{0,3},{1,2},{2,1},{3,0},{4,7},{5,6},{6,5},{7,4},{8,11},{9,10},{10,... | collective-permute-start | bytes 49160 | tf_op jit(solution)/shard_map/ppermute | solution.py:178
  11.7 1.2 %collective-permute-start.3 = (f32[16,256]{1,0:T(8,128)S(1)}, f32[16,256]{1,0:T(8,128)S(1)}, u32[]{:S(2)}, u32[]{:S(2)}) collective-permute-start(f32[16,256]{1,0:T(8,128)S(1)} %get-tuple-element.49), channel_id=1, source_target_pairs={{0,1},{1,0},{2,19},{3,18},{4,5},{5,4},{6,23},{7,22},{8,9},{9,8},{1... | collective-permute-start | bytes 49160 | tf_op jit(solution)/shard_map/ppermute | solution.py:178
  13.7 3.3 %collective-permute-start.8 = (f32[24,256]{1,0:T(8,128)S(1)}, f32[24,256]{1,0:T(8,128)S(1)}, u32[]{:S(2)}, u32[]{:S(2)}) collective-permute-start(f32[24,256]{1,0:T(8,128)S(1)} %get-tuple-element.38), channel_id=1, source_target_pairs={{0,5},{1,4},{2,7},{3,6},{4,1},{5,0},{6,3},{7,2},{8,13},{9,12},{10,... | collective-permute-start | bytes 73736 | tf_op jit(solution)/shard_map/ppermute | solution.py:178
  17.1 3.3 %collective-permute-start.9 = (f32[24,256]{1,0:T(8,128)S(1)}, f32[24,256]{1,0:T(8,128)S(1)}, u32[]{:S(2)}, u32[]{:S(2)}) collective-permute-start(f32[24,256]{1,0:T(8,128)S(1)} %pad_maximum_fusion.2), channel_id=1, source_target_pairs={{0,9},{1,8},{2,11},{3,10},{4,13},{5,12},{6,15},{7,14},{8,1},{9,0},... | collective-permute-start | bytes 73736 | tf_op jit(solution)/shard_map/ppermute | solution.py:178
  20.4 5.7 %collective-permute-start.11 = (f32[16,256]{1,0:T(8,128)S(1)}, f32[16,256]{1,0:T(8,128)S(1)}, u32[]{:S(2)}, u32[]{:S(2)}) collective-permute-start(f32[16,256]{1,0:T(8,128)S(1)} %get-tuple-element.46), channel_id=1, source_target_pairs={{0,3},{1,2},{2,1},{3,0},{4,7},{5,6},{6,5},{7,4},{8,11},{9,10},{10,... | collective-permute-start | bytes 49160 | tf_op jit(solution)/shard_map/ppermute | solution.py:178
  24.7 1.4 %collective-permute-start.10 = (f32[16,256]{1,0:T(8,128)S(1)}, f32[16,256]{1,0:T(8,128)S(1)}, u32[]{:S(2)}, u32[]{:S(2)}) collective-permute-start(f32[16,256]{1,0:T(8,128)S(1)} %get-tuple-element.47), channel_id=1, source_target_pairs={{0,1},{1,0},{2,19},{3,18},{4,5},{5,4},{6,23},{7,22},{8,9},{9,8},{1... | collective-permute-start | bytes 49160 | tf_op jit(solution)/shard_map/ppermute | solution.py:178
  26.2 4.1 %collective-permute-start.12 = (f32[4,256]{1,0:T(4,128)S(1)}, f32[4,256]{1,0:T(4,128)S(1)}, u32[]{:S(2)}, u32[]{:S(2)}) collective-permute-start(f32[4,256]{1,0:T(4,128)S(1)} %constant_dynamic-slice_fusion.6), channel_id=1, source_target_pairs={{0,1},{1,0},{2,3},{3,2},{4,5},{5,4},{6,7},{7,6},{8,9},{9,8},{10,11... | collective-permute-start | bytes 12296 | tf_op jit(solution)/shard_map/ppermute | solution.py:178
